TPU v7x, 32 devices: a whole 2x2x4 slice. The times are simulated.
32 devices in a mesh: section: 2 (over x), tensor: 4 (over z), dp: 4 (over y, core).
Axes of the slice: x: 2, y: 2, z: 4, core: 2. Of those that a mesh axis runs over, the one named last changes fastest.
Arguments:
- hidden_in: bfloat16 [2, 4, 1024, 1024], P(None, 'dp', 'tensor'), may hold values from -6 to 6
- cotangent: bfloat16 [2, 4, 1024, 1024], P(None, 'dp', 'tensor'), may hold values from -6 to 6
- query_w: bfloat16 [2, 1024, 1024], P('section', None, 'tensor'), may hold values from -0.1875 to 0.1875
- key_w: bfloat16 [2, 1024, 1024], P('section', None, 'tensor'), may hold values from -0.1875 to 0.1875
- value_w: bfloat16 [2, 1024, 1024], P('section', None, 'tensor'), may hold values from -0.1875 to 0.1875
- output_w: bfloat16 [2, 1024, 1024], P('section', 'tensor'), may hold values from -0.1875 to 0.1875
- qk_scale: float32 [2, 1024], P('section', 'tensor'), may hold values from 0.25 to 1.75
- attn_rate: float32 [2, 1024], P('section'), may hold values from 0.1 to 0.6
- up_w: bfloat16 [2, 1024, 4096], P('section', None, 'tensor'), may hold values from -0.1875 to 0.1875
- gate_w: bfloat16 [2, 1024, 4096], P('section', None, 'tensor'), may hold values from -0.1875 to 0.1875
- down_w: bfloat16 [2, 4096, 1024], P('section', 'tensor'), may hold values from -0.09375 to 0.09375
- up_scale: float32 [2, 4096], P('section', 'tensor'), may hold values from 0.25 to 1.75
- gate_scale: float32 [2, 4096], P('section', 'tensor'), may hold values from 0.25 to 1.75
- mlp_rate: float32 [2, 1024], P('section'), may hold values from 0.1 to 0.6
Outputs:
- hidden_out: bfloat16 [2, 2, 4, 1024, 1024], P('section', None, 'dp', 'tensor')
- grad_in: float32 [2, 2, 4, 1024, 1024], P('section', None, 'dp', 'tensor')
- grad_query: float32 [2, 1024, 1024], P('section', None, 'tensor')
- grad_key: float32 [2, 1024, 1024], P('section', None, 'tensor')
- grad_value: float32 [2, 1024, 1024], P('section', None, 'tensor')
- grad_output: float32 [2, 1024, 1024], P('section', 'tensor')
- grad_qkscale: float32 [2, 1024], P('section', 'tensor')
- grad_attnrate: float32 [2, 1024], P('section')
- grad_up: float32 [2, 1024, 4096], P('section', None, 'tensor')
- grad_gate: float32 [2, 1024, 4096], P('section', None, 'tensor')
- grad_down: float32 [2, 4096, 1024], P('section', 'tensor')
- grad_upscale: float32 [2, 4096], P('section', 'tensor')
- grad_gatescale: float32 [2, 4096], P('section', 'tensor')
- grad_mlprate: float32 [2, 1024], P('section')
All inputs are finite; a program needn't handle non-finite values.
Results may differ from a plain program's by a relative error of at most 0.034.
Values may be sent and summed in bfloat16 or wider, within the bound.
No kernel may reach another device: no remote copies, remote signals or barrier semaphores. Data moves between devices by JAX's collectives and lax.ppermute only.
A program may use at most 320 MiB of HBM per device.

v0:
```python
import jax
import jax.numpy as jnp
from jax import lax
from jax.sharding import PartitionSpec as P

HD = 64


def from_behind(value, axis, steps):
    count = lax.axis_size(axis)
    initial, last = (max(0, -steps), min(count, count - steps))
    return lax.ppermute(value, axis, [(source, source + steps) for source in range(initial, last)])


def sphere(values):
    return values * lax.rsqrt(jnp.mean(values * values, axis=-1, keepdims=True) + 1e-06)


def head_sphere(query, scaling):
    head_parts = query.reshape(query.shape[0], -1, HD)
    return sphere(head_parts).reshape(query.shape) * scaling


def blend_rows(hidden, branch, rate_vec):
    return sphere(hidden + rate_vec * (sphere(branch) - hidden))


def gating(up_raw, gate_raw, up_scale, gate_scale):
    return jax.nn.silu(gate_raw * gate_scale) * (up_raw * up_scale)


def gather_rows(row_shard):
    return lax.all_gather(row_shard, "tensor", axis=0, tiled=True)


def gather_middle(row_shard):
    return lax.all_gather(row_shard, "tensor", axis=0, tiled=True)


def attend(query_low, key_low, value_low):
    length = query_low.shape[0]
    head_count = query_low.shape[1] // HD
    block_rows = min(512, length)
    count_blocks = length // block_rows
    query_blocks = query_low.reshape(count_blocks, block_rows, head_count, HD)
    key_heads = key_low.reshape(length, head_count, HD)
    value_heads = value_low.reshape(length, head_count, HD)
    positions = jnp.arange(length)

    def attend_per_block(inputs):
        query_blk, block_index = inputs
        scores = jnp.einsum(
            "qhd,khd->hqk", query_blk, key_heads, preferred_element_type=jnp.float32
        ) * HD ** (-0.5)
        row_pos = block_index * block_rows + jnp.arange(block_rows)
        causal = positions[None, :] <= row_pos[:, None]
        scores = jnp.where(causal[None], scores, -1e30)
        row_max = jnp.max(scores, axis=-1, keepdims=True)
        raised = jnp.exp(scores - row_max)
        row_total = jnp.sum(raised, axis=-1, keepdims=True)
        weights_low = (raised / row_total).astype(jnp.bfloat16)
        result = jnp.einsum(
            "hqk,khd->qhd", weights_low, value_heads, preferred_element_type=jnp.float32
        )
        return (result, (row_max + jnp.log(row_total))[..., 0])

    results, logsum = lax.map(attend_per_block, (query_blocks, jnp.arange(count_blocks)))
    return (results.reshape(length, head_count * HD), logsum)


def attention_backward(query_low, key_low, value_low, logsum, grad_low):
    length = query_low.shape[0]
    head_count = query_low.shape[1] // HD
    block_rows = min(512, length)
    count_blocks = length // block_rows
    query_blocks = query_low.reshape(count_blocks, block_rows, head_count, HD)
    grad_blocks = grad_low.reshape(count_blocks, block_rows, head_count, HD)
    key_heads = key_low.reshape(length, head_count, HD)
    value_heads = value_low.reshape(length, head_count, HD)
    positions = jnp.arange(length)
    scale_factor = HD ** (-0.5)

    def attention_per_block(carry, inputs):
        key_acc, value_acc = carry
        query_blk, grad_blk, lse_blk, block_index = inputs
        scores = (
            jnp.einsum("qhd,khd->hqk", query_blk, key_heads, preferred_element_type=jnp.float32)
            * scale_factor
        )
        row_pos = block_index * block_rows + jnp.arange(block_rows)
        causal = positions[None, :] <= row_pos[:, None]
        scores = jnp.where(causal[None], scores, -1e30)
        probs = jnp.exp(scores - lse_blk[..., None])
        probs_low = probs.astype(jnp.bfloat16)
        grad_probs = jnp.einsum(
            "qhd,khd->hqk", grad_blk, value_heads, preferred_element_type=jnp.float32
        )
        grad_scores = probs * (grad_probs - jnp.sum(probs * grad_probs, axis=-1, keepdims=True))
        scores_low = grad_scores.astype(jnp.bfloat16)
        query_grad = (
            jnp.einsum("hqk,khd->qhd", scores_low, key_heads, preferred_element_type=jnp.float32)
            * scale_factor
        )
        key_acc = (
            key_acc
            + jnp.einsum("hqk,qhd->khd", scores_low, query_blk, preferred_element_type=jnp.float32)
            * scale_factor
        )
        value_acc = value_acc + jnp.einsum(
            "hqk,qhd->khd", probs_low, grad_blk, preferred_element_type=jnp.float32
        )
        return ((key_acc, value_acc), query_grad)

    zero_acc = jnp.zeros((length, head_count, HD), jnp.float32)
    (key_grad, value_grad), query_grads = lax.scan(
        attention_per_block,
        (zero_acc, zero_acc),
        (query_blocks, grad_blocks, logsum, jnp.arange(count_blocks)),
    )
    return (
        query_grads.reshape(length, -1),
        key_grad.reshape(length, -1),
        value_grad.reshape(length, -1),
    )


def layer_forward(row_shard, params):
    (
        query_w,
        key_w,
        value_w,
        output_w,
        qk_scale,
        attn_rate,
        up_w,
        gate_w,
        down_w,
        up_scale,
        gate_scale,
        mlp_rate,
    ) = params
    full_in = gather_rows(row_shard)
    query_raw = jnp.dot(full_in, query_w, preferred_element_type=jnp.float32)
    key_raw = jnp.dot(full_in, key_w, preferred_element_type=jnp.float32)
    value_raw = jnp.dot(full_in, value_w, preferred_element_type=jnp.float32)
    query_low = head_sphere(query_raw, qk_scale).astype(jnp.bfloat16)
    key_low = head_sphere(key_raw, qk_scale).astype(jnp.bfloat16)
    value_low = value_raw.astype(jnp.bfloat16)
    attended, logsum = attend(query_low, key_low, value_low)
    attended_low = attended.astype(jnp.bfloat16)
    attn_sum = lax.psum_scatter(
        jnp.dot(attended_low, output_w, preferred_element_type=jnp.float32).astype(jnp.bfloat16),
        "tensor",
        scatter_dimension=0,
        tiled=True,
    ).astype(jnp.float32)
    hidden = row_shard.astype(jnp.float32)
    middle = blend_rows(hidden, attn_sum, attn_rate)
    middle_low = middle.astype(jnp.bfloat16)
    full_mid = gather_middle(middle_low)
    up_raw = jnp.dot(full_mid, up_w, preferred_element_type=jnp.float32)
    gate_raw = jnp.dot(full_mid, gate_w, preferred_element_type=jnp.float32)
    inner_low = gating(up_raw, gate_raw, up_scale, gate_scale).astype(jnp.bfloat16)
    mlp_sum = lax.psum_scatter(
        jnp.dot(inner_low, down_w, preferred_element_type=jnp.float32).astype(jnp.bfloat16),
        "tensor",
        scatter_dimension=0,
        tiled=True,
    ).astype(jnp.float32)
    result = blend_rows(middle, mlp_sum, mlp_rate)
    kept = {
        "row_shard": row_shard,
        "attn_sum": attn_sum,
        "middle": middle,
        "mlp_sum": mlp_sum,
        "query_raw": query_raw,
        "key_raw": key_raw,
        "query_low": query_low,
        "key_low": key_low,
        "value_low": value_low,
        "logsum": logsum,
        "attended_low": attended_low,
        "up_raw": up_raw,
        "gate_raw": gate_raw,
        "inner_low": inner_low,
    }
    return (result, kept)


def layer_backward(grad_out, kept, params):
    (
        query_w,
        key_w,
        value_w,
        output_w,
        qk_scale,
        attn_rate,
        up_w,
        gate_w,
        down_w,
        up_scale,
        gate_scale,
        mlp_rate,
    ) = params
    hidden = kept["row_shard"].astype(jnp.float32)
    full_in = gather_rows(kept["row_shard"])
    full_mid = gather_middle(kept["middle"].astype(jnp.bfloat16))
    blend_value, blend_pull = jax.vjp(blend_rows, kept["middle"], kept["mlp_sum"], mlp_rate)
    grad_middle, grad_mlp, grad_mlprate = blend_pull(grad_out)
    full_grad_mlp = lax.all_gather(grad_mlp.astype(jnp.bfloat16), "tensor", axis=0, tiled=True)
    grad_inner = jnp.einsum("ld,fd->lf", full_grad_mlp, down_w, preferred_element_type=jnp.float32)
    grad_down = jnp.einsum(
        "lf,ld->fd", kept["inner_low"], full_grad_mlp, preferred_element_type=jnp.float32
    )
    gate_value, gate_pull = jax.vjp(gating, kept["up_raw"], kept["gate_raw"], up_scale, gate_scale)
    grad_up_raw, grad_gate_raw, grad_upscale, grad_gatescale = gate_pull(grad_inner)
    up_back = grad_up_raw.astype(jnp.bfloat16)
    gate_back = grad_gate_raw.astype(jnp.bfloat16)
    grad_up = jnp.einsum("ld,lf->df", full_mid, up_back, preferred_element_type=jnp.float32)
    grad_gate = jnp.einsum("ld,lf->df", full_mid, gate_back, preferred_element_type=jnp.float32)
    grad_middle = grad_middle + lax.psum_scatter(
        (
            jnp.einsum("lf,df->ld", up_back, up_w, preferred_element_type=jnp.float32)
            + jnp.einsum("lf,df->ld", gate_back, gate_w, preferred_element_type=jnp.float32)
        ).astype(jnp.bfloat16),
        "tensor",
        scatter_dimension=0,
        tiled=True,
    ).astype(jnp.float32)
    attn_value, attn_pull = jax.vjp(blend_rows, hidden, kept["attn_sum"], attn_rate)
    grad_hidden, grad_attn, grad_attnrate = attn_pull(grad_middle)
    full_grad_attn = lax.all_gather(grad_attn.astype(jnp.bfloat16), "tensor", axis=0, tiled=True)
    grad_attended = jnp.einsum(
        "ld,hd->lh", full_grad_attn, output_w, preferred_element_type=jnp.float32
    ).astype(jnp.bfloat16)
    grad_output = jnp.einsum(
        "lh,ld->hd", kept["attended_low"], full_grad_attn, preferred_element_type=jnp.float32
    )
    reduced_query_gradient, reduced_key_gradient, reduced_value_gradient = attention_backward(
        kept["query_low"], kept["key_low"], kept["value_low"], kept["logsum"], grad_attended
    )
    query_value, query_pull = jax.vjp(head_sphere, kept["query_raw"], qk_scale)
    grad_query_raw, scale_first = query_pull(reduced_query_gradient)
    key_value, key_vector_product = jax.vjp(head_sphere, kept["key_raw"], qk_scale)
    unscaled_key_gradient, second_section_scale = key_vector_product(reduced_key_gradient)
    grad_qkscale = scale_first + second_section_scale
    query_back = grad_query_raw.astype(jnp.bfloat16)
    key_back = unscaled_key_gradient.astype(jnp.bfloat16)
    value_back = reduced_value_gradient.astype(jnp.bfloat16)
    grad_query = jnp.einsum("ld,lh->dh", full_in, query_back, preferred_element_type=jnp.float32)
    grad_key = jnp.einsum("ld,lh->dh", full_in, key_back, preferred_element_type=jnp.float32)
    grad_value = jnp.einsum("ld,lh->dh", full_in, value_back, preferred_element_type=jnp.float32)
    grad_hidden = grad_hidden + lax.psum_scatter(
        (
            jnp.einsum("lh,dh->ld", query_back, query_w, preferred_element_type=jnp.float32)
            + jnp.einsum("lh,dh->ld", key_back, key_w, preferred_element_type=jnp.float32)
            + jnp.einsum("lh,dh->ld", value_back, value_w, preferred_element_type=jnp.float32)
        ).astype(jnp.bfloat16),
        "tensor",
        scatter_dimension=0,
        tiled=True,
    ).astype(jnp.float32)
    grad_list = (
        grad_query,
        grad_key,
        grad_value,
        grad_output,
        grad_qkscale,
        grad_attnrate,
        grad_up,
        grad_gate,
        grad_down,
        grad_upscale,
        grad_gatescale,
        grad_mlprate,
    )
    return (grad_hidden, grad_list)


def replica_sum(grad_list):
    sharded = (
        lax.psum(grad_list[0].astype(jnp.bfloat16), "dp").astype(jnp.float32),
        lax.psum(grad_list[1].astype(jnp.bfloat16), "dp").astype(jnp.float32),
        lax.psum(grad_list[2].astype(jnp.bfloat16), "dp").astype(jnp.float32),
        lax.psum(grad_list[3].astype(jnp.bfloat16), "dp").astype(jnp.float32),
        lax.psum(grad_list[4].astype(jnp.bfloat16), "dp").astype(jnp.float32),
        lax.psum(grad_list[6].astype(jnp.bfloat16), "dp").astype(jnp.float32),
        lax.psum(grad_list[7].astype(jnp.bfloat16), "dp").astype(jnp.float32),
        lax.psum(grad_list[8].astype(jnp.bfloat16), "dp").astype(jnp.float32),
        lax.psum(grad_list[9].astype(jnp.bfloat16), "dp").astype(jnp.float32),
        lax.psum(grad_list[10].astype(jnp.bfloat16), "dp").astype(jnp.float32),
    )
    rates = lax.psum((grad_list[5], grad_list[11]), ("tensor", "dp"))
    return (
        sharded[0],
        sharded[1],
        sharded[2],
        sharded[3],
        sharded[4],
        rates[0],
        sharded[5],
        sharded[6],
        sharded[7],
        sharded[8],
        sharded[9],
        rates[1],
    )


def body(
    hidden_in,
    cotangent,
    query_w,
    key_w,
    value_w,
    output_w,
    qk_scale,
    attn_rate,
    up_w,
    gate_w,
    down_w,
    up_scale,
    gate_scale,
    mlp_rate,
):
    on_first = lax.axis_index("section") == 0
    params = tuple(
        (
            member[0]
            for member in (
                query_w,
                key_w,
                value_w,
                output_w,
                qk_scale,
                attn_rate,
                up_w,
                gate_w,
                down_w,
                up_scale,
                gate_scale,
                mlp_rate,
            )
        )
    )
    micro_count = hidden_in.shape[0]
    inputs = hidden_in[:, 0]
    cot_rows = cotangent[:, 0].astype(jnp.float32)
    received = jnp.zeros_like(inputs[0])
    out_list = []
    kept_list = []
    for step_index in range(micro_count + 1):
        layer_input = jnp.where(on_first, inputs[min(step_index, micro_count - 1)], received)
        result, kept = layer_forward(layer_input, params)
        sent_rows = result.astype(jnp.bfloat16)
        out_list.append(sent_rows)
        kept_list.append(kept)
        if step_index < micro_count:
            received = from_behind(sent_rows, "section", 1)
    hidden_rows = jnp.stack(
        [
            jnp.where(on_first, out_list[index_m], out_list[index_m + 1])
            for index_m in range(micro_count)
        ]
    )
    grad_recv = jnp.zeros_like(inputs[0])
    grad_sums = None
    back_list = []
    for step_index in range(micro_count + 1):
        grad_out = jnp.where(
            on_first, grad_recv.astype(jnp.float32), cot_rows[min(step_index, micro_count - 1)]
        )
        picked = jax.tree.map(
            lambda former, latter: jnp.where(on_first, former, latter),
            kept_list[max(step_index - 1, 0)],
            kept_list[min(step_index + 1, micro_count)],
        )
        grad_hidden, layer_grads = layer_backward(grad_out, picked, params)
        valid = jnp.where(on_first, step_index >= 1, step_index < micro_count)
        masked = tuple((jnp.where(valid, member, 0.0) for member in layer_grads))
        if grad_sums is None:
            grad_sums = masked
        else:
            grad_sums = tuple((former + latter for former, latter in zip(grad_sums, masked)))
        back_rows = grad_hidden.astype(jnp.bfloat16)
        back_list.append((grad_hidden, back_rows))
        if step_index < micro_count:
            grad_recv = from_behind(back_rows, "section", -1)
    grad_rows = jnp.stack(
        [
            jnp.where(
                on_first, back_list[index_m + 1][0], back_list[index_m][1].astype(jnp.float32)
            )
            for index_m in range(micro_count)
        ]
    )
    summed = replica_sum(grad_sums)
    return (hidden_rows[None, :, None], grad_rows[None, :, None]) + tuple(
        (member[None] for member in summed)
    )


def solution(mesh):
    in_specs = (
        P(None, "dp", "tensor", None),
        P(None, "dp", "tensor", None),
        P("section", None, "tensor"),
        P("section", None, "tensor"),
        P("section", None, "tensor"),
        P("section", "tensor", None),
        P("section", "tensor"),
        P("section", None),
        P("section", None, "tensor"),
        P("section", None, "tensor"),
        P("section", "tensor", None),
        P("section", "tensor"),
        P("section", "tensor"),
        P("section", None),
    )
    out_specs = (
        P("section", None, "dp", "tensor", None),
        P("section", None, "dp", "tensor", None),
        P("section", None, "tensor"),
        P("section", None, "tensor"),
        P("section", None, "tensor"),
        P("section", "tensor", None),
        P("section", "tensor"),
        P("section", None),
        P("section", None, "tensor"),
        P("section", None, "tensor"),
        P("section", "tensor", None),
        P("section", "tensor"),
        P("section", "tensor"),
        P("section", None),
    )
    return jax.shard_map(body, mesh=mesh, in_specs=in_specs, out_specs=out_specs, check_vma=False)
```

profile of v0, /device:TPU:0, one launch (start us, length us, event | category | flops | bytes accessed | tf_op | source)
XLA Modules:
  0.0 1998.0 jit_solution(17263594475661797079)
XLA Ops:
  9.4 49.5 %all-gather.54.cloned.1.call-done = bf16[1,1,1024,1024]{3,2,1,0:T(8,128)(2,1)} async-done(((bf16[1,1,256,1024]{3,2,1,0:T(8,128)(2,1)}), bf16[1,1,1024,1024]{3,2,1,0:T(8,128)(2,1)}) %all-gather.54.cloned.1.call-update) | async-done | bytes 2097168 | tf_op jit(solution)/shard_map/all_gather | solution.py:33
  98.3 42.7 %reduce-scatter.13.cloned.1.call-done = bf16[256,1024]{1,0:T(8,128)(2,1)} async-done(((bf16[1024,1024]{1,0:T(8,128)(2,1)}), bf16[256,1024]{1,0:T(8,128)(2,1)}) %reduce-scatter.13.cloned.1.call-update) | async-done | bytes 524304 | tf_op jit(solution)/shard_map/reduce_scatter | solution.py:151
  146.6 45.1 %all-gather.20.cloned.1.call-done = bf16[1024,1024]{1,0:T(8,128)(2,1)} async-done(((bf16[256,1024]{1,0:T(8,128)(2,1)}), bf16[1024,1024]{1,0:T(8,128)(2,1)}) %all-gather.20.cloned.1.call-update) | async-done | bytes 2097168 | tf_op jit(solution)/shard_map/all_gather | solution.py:37
  206.3 42.7 %reduce-scatter.15.cloned.1.call-done = bf16[256,1024]{1,0:T(8,128)(2,1)} async-done(((bf16[1024,1024]{1,0:T(8,128)(2,1)}), bf16[256,1024]{1,0:T(8,128)(2,1)}) %reduce-scatter.15.cloned.1.call-update) | async-done | bytes 524304 | tf_op jit(solution)/shard_map/reduce_scatter | solution.py:164
  270.4 46.4 %all-gather.22.cloned.1.call-done = bf16[1024,1024]{1,0:T(8,128)(2,1)} async-done(((bf16[256,1024]{1,0:T(8,128)(2,1)}), bf16[1024,1024]{1,0:T(8,128)(2,1)}) %all-gather.22.cloned.1.call-update) | async-done | bytes 2097168 | tf_op jit(solution)/shard_map/all_gather | solution.py:33
  358.2 42.7 %reduce-scatter.17.cloned.1.call-done = bf16[256,1024]{1,0:T(8,128)(2,1)} async-done(((bf16[1024,1024]{1,0:T(8,128)(2,1)}), bf16[256,1024]{1,0:T(8,128)(2,1)}) %reduce-scatter.17.cloned.1.call-update) | async-done | bytes 524304 | tf_op jit(solution)/shard_map/reduce_scatter | solution.py:151
  407.5 44.9 %all-gather.24.cloned.1.call-done = bf16[1024,1024]{1,0:T(8,128)(2,1)} async-done(((bf16[256,1024]{1,0:T(8,128)(2,1)}), bf16[1024,1024]{1,0:T(8,128)(2,1)}) %all-gather.24.cloned.1.call-update) | async-done | bytes 2097168 | tf_op jit(solution)/shard_map/all_gather | solution.py:37
  469.8 39.8 %reduce-scatter.19.cloned.1.call-done = bf16[256,1024]{1,0:T(8,128)(2,1)} async-done(((bf16[1024,1024]{1,0:T(8,128)(2,1)}), bf16[256,1024]{1,0:T(8,128)(2,1)}) %reduce-scatter.19.cloned.1.call-update) | async-done | bytes 524304 | tf_op jit(solution)/shard_map/reduce_scatter | solution.py:164
  517.1 45.2 %all-gather.30.cloned.1.call-done = bf16[1024,1024]{1,0:T(8,128)(2,1)} async-done(((bf16[256,1024]{1,0:T(8,128)(2,1)}), bf16[1024,1024]{1,0:T(8,128)(2,1)}) %all-gather.30.cloned.1.call-update) | async-done | bytes 2097168 | tf_op jit(solution)/shard_map/all_gather | solution.py:210
  581.2 42.6 %reduce-scatter.25.cloned.1.call-done = bf16[256,1024]{1,0:T(8,128)(2,1)} async-done(((bf16[1024,1024]{1,0:T(8,128)(2,1)}), bf16[256,1024]{1,0:T(8,128)(2,1)}) %reduce-scatter.25.cloned.1.call-update) | async-done | bytes 524304 | tf_op jit(solution)/shard_map/reduce_scatter | solution.py:221
  645.5 46.4 %all-gather.26.cloned.1.call-done = bf16[1024,1024]{1,0:T(8,128)(2,1)} async-done(((bf16[256,1024]{1,0:T(8,128)(2,1)}), bf16[1024,1024]{1,0:T(8,128)(2,1)}) %all-gather.26.cloned.1.call-update) | async-done | bytes 2097168 | tf_op jit(solution)/shard_map/all_gather | solution.py:33
  734.1 42.7 %reduce-scatter.21.cloned.1.call-done = bf16[256,1024]{1,0:T(8,128)(2,1)} async-done(((bf16[1024,1024]{1,0:T(8,128)(2,1)}), bf16[256,1024]{1,0:T(8,128)(2,1)}) %reduce-scatter.21.cloned.1.call-update) | async-done | bytes 524304 | tf_op jit(solution)/shard_map/reduce_scatter | solution.py:151
  790.9 40.1 %all-gather.32.cloned.1.call-done = bf16[1024,1024]{1,0:T(8,128)(2,1)} async-done(((bf16[256,1024]{1,0:T(8,128)(2,1)}), bf16[1024,1024]{1,0:T(8,128)(2,1)}) %all-gather.32.cloned.1.call-update) | async-done | bytes 2097168 | tf_op jit(solution)/shard_map/all_gather | solution.py:232
  838.3 66.0 %while.87 = (s32[]{:T(128)}, f32[1024,4,64]{0,2,1:T(8,128)}, f32[1024,4,64]{0,2,1:T(8,128)}, f32[2,512,4,64]{1,0,3,2:T(2,128)}, bf16[2,512,4,64]{1,3,2,0:T(8,128...) while((s32[]{:T(128)}, f32[1024,4,64]{0,2,1:T(8,128)}, ...), condition=%wide.region_47.48_spmd.clone, body=%wide.region_45.47_spmd.clone.sunk | while | flops 1375599104 | bytes 164688240 | solution.py:115
  964.6 42.2 %reduce-scatter.23.cloned.1.call-done = bf16[256,1024]{1,0:T(8,128)(2,1)} async-done(((bf16[1024,1024]{1,0:T(8,128)(2,1)}), bf16[256,1024]{1,0:T(8,128)(2,1)}) %reduce-scatter.23.cloned.1.call-update) | async-done | bytes 524304 | tf_op jit(solution)/shard_map/reduce_scatter | solution.py:164
  1014.1 45.3 %all-gather.34.cloned.1.call-done = bf16[1024,1024]{1,0:T(8,128)(2,1)} async-done(((bf16[256,1024]{1,0:T(8,128)(2,1)}), bf16[1024,1024]{1,0:T(8,128)(2,1)}) %all-gather.34.cloned.1.call-update) | async-done | bytes 2097168 | tf_op jit(solution)/shard_map/all_gather | solution.py:210
  1078.3 42.6 %reduce-scatter.29.cloned.1.call-done = bf16[256,1024]{1,0:T(8,128)(2,1)} async-done(((bf16[1024,1024]{1,0:T(8,128)(2,1)}), bf16[256,1024]{1,0:T(8,128)(2,1)}) %reduce-scatter.29.cloned.1.call-update) | async-done | bytes 524304 | tf_op jit(solution)/shard_map/reduce_scatter | solution.py:221
  1137.6 39.1 %all-gather.36.cloned.1.call-done = bf16[1024,1024]{1,0:T(8,128)(2,1)} async-done(((bf16[256,1024]{1,0:T(8,128)(2,1)}), bf16[1024,1024]{1,0:T(8,128)(2,1)}) %all-gather.36.cloned.1.call-update) | async-done | bytes 2097168 | tf_op jit(solution)/shard_map/all_gather | solution.py:232
  1186.5 65.8 %while.88 = (s32[]{:T(128)}, f32[1024,4,64]{0,2,1:T(8,128)}, f32[1024,4,64]{0,2,1:T(8,128)}, f32[2,512,4,64]{1,0,3,2:T(2,128)}, bf16[2,512,4,64]{1,3,2,0:T(8,128...) while((s32[]{:T(128)}, f32[1024,4,64]{0,2,1:T(8,128)}, ...), condition=%wide.region_64.65_spmd.clone, body=%wide.region_62.64_spmd.clone.sunk | while | flops 1375599104 | bytes 164688240 | solution.py:115
  1265.3 42.7 %reduce-scatter.31.cloned.1.call-done = bf16[256,1024]{1,0:T(8,128)(2,1)} async-done(((bf16[1024,1024]{1,0:T(8,128)(2,1)}), bf16[256,1024]{1,0:T(8,128)(2,1)}) %reduce-scatter.31.cloned.1.call-update) | async-done | bytes 524304 | tf_op jit(solution)/shard_map/reduce_scatter | solution.py:253
  1330.4 44.7 %all-gather.38.cloned.1.call-done = bf16[1024,1024]{1,0:T(8,128)(2,1)} async-done(((bf16[256,1024]{1,0:T(8,128)(2,1)}), bf16[1024,1024]{1,0:T(8,128)(2,1)}) %all-gather.38.cloned.1.call-update) | async-done | bytes 2097168 | tf_op jit(solution)/shard_map/all_gather | solution.py:210
  1405.1 40.0 %reduce-scatter.33.cloned.1.call-done = bf16[256,1024]{1,0:T(8,128)(2,1)} async-done(((bf16[1024,1024]{1,0:T(8,128)(2,1)}), bf16[256,1024]{1,0:T(8,128)(2,1)}) %reduce-scatter.33.cloned.1.call-update) | async-done | bytes 524304 | tf_op jit(solution)/shard_map/reduce_scatter | solution.py:221
  1687.2 66.4 %while.89 = (s32[]{:T(128)}, f32[1024,4,64]{0,2,1:T(8,128)}, f32[1024,4,64]{0,2,1:T(8,128)}, f32[2,512,4,64]{1,0,3,2:T(2,128)}, bf16[2,512,4,64]{1,3,2,0:T(8,128...) while((s32[]{:T(128)}, f32[1024,4,64]{0,2,1:T(8,128)}, ...), condition=%wide.region_81.82_spmd.clone, body=%wide.region_79.81_spmd.clone.sunk | while | flops 1375599104 | bytes 164688240 | solution.py:115
  1837.5 101.9 %all-reduce.5.cloned.1.call-done = (bf16[1,1024,256]{1,2,0:T(8,128)(2,1)}, bf16[1,1024,256]{1,2,0:T(8,128)(2,1)}, bf16[1,1024,256]{1,2,0:T(8,128)(2,1)}, bf16[1,...) async-done(((bf16[1,1024,256]{1,2,0:T(8,128)(2,1)}, bf16[1,1024,256]{1,2,0:T(8,128)(2,1)}, ...) | async-done | bytes 8388624 | tf_op jit(solution)/shard_map/psum | solution.py:282
  (972 shorter events, 1064.9 us)
Async XLA Ops:
  9.3 131.7 %reduce-scatter.13.cloned.1.call-start = ((), (), s32[]{:S(2)}) async-start(), calls=%async_computation.12 | async-start | bytes 2621440 | tf_op jit(solution)/shard_map/reduce_scatter | solution.py:151
  146.3 102.7 %reduce-scatter.15.cloned.1.call-start = ((), (), s32[]{:S(2)}) async-start(), calls=%async_computation.14 | async-start | bytes 2621440 | tf_op jit(solution)/shard_map/reduce_scatter | solution.py:164
  206.2 110.5 %all-gather.22.cloned.1.call-start = ((), (), s32[]{:S(2)}) async-start(), calls=%async_computation.15 | async-start | bytes 2621440 | tf_op jit(solution)/shard_map/all_gather | solution.py:33
  270.1 130.8 %reduce-scatter.17.cloned.1.call-start = ((), (), s32[]{:S(2)}) async-start(), calls=%async_computation.16 | async-start | bytes 2621440 | tf_op jit(solution)/shard_map/reduce_scatter | solution.py:151
  406.9 102.7 %reduce-scatter.19.cloned.1.call-start = ((), (), s32[]{:S(2)}) async-start(), calls=%async_computation.18 | async-start | bytes 2621440 | tf_op jit(solution)/shard_map/reduce_scatter | solution.py:164
  516.8 107.0 %reduce-scatter.25.cloned.1.call-start = ((), (), s32[]{:S(2)}) async-start(), calls=%async_computation.24 | async-start | bytes 2621440 | tf_op jit(solution)/shard_map/reduce_scatter | solution.py:221
  581.1 110.8 %all-gather.26.cloned.1.call-start = ((), (), s32[]{:S(2)}) async-start(), calls=%async_computation.19 | async-start | bytes 2621440 | tf_op jit(solution)/shard_map/all_gather | solution.py:33
  645.2 131.6 %reduce-scatter.21.cloned.1.call-start = ((), (), s32[]{:S(2)}) async-start(), calls=%async_computation.20 | async-start | bytes 2621440 | tf_op jit(solution)/shard_map/reduce_scatter | solution.py:151
  785.6 131.1 %all-gather.28.cloned.1.call-start = ((), (), s32[]{:S(2)}) async-start(), calls=%async_computation.21 | async-start | bytes 2621440 | tf_op jit(solution)/shard_map/all_gather | solution.py:37
  790.4 170.3 %reduce-scatter.27.cloned.1.call-start = ((), (), s32[]{:S(2)}) async-start(), calls=%async_computation.26 | async-start | bytes 2621440 | tf_op jit(solution)/shard_map/reduce_scatter | solution.py:253
  931.3 128.2 %all-gather.34.cloned.1.call-start = ((), (), s32[]{:S(2)}) async-start(), calls=%async_computation.27 | async-start | bytes 2621440 | tf_op jit(solution)/shard_map/all_gather | solution.py:210
  1014.0 106.9 %reduce-scatter.29.cloned.1.call-start = ((), (), s32[]{:S(2)}) async-start(), calls=%async_computation.28 | async-start | bytes 2621440 | tf_op jit(solution)/shard_map/reduce_scatter | solution.py:221
  1078.2 98.5 %all-gather.36.cloned.1.call-start = ((), (), s32[]{:S(2)}) async-start(), calls=%async_computation.29 | async-start | bytes 2621440 | tf_op jit(solution)/shard_map/all_gather | solution.py:232
  1131.3 176.7 %reduce-scatter.31.cloned.1.call-start = ((), (), s32[]{:S(2)}) async-start(), calls=%async_computation.30 | async-start | bytes 2621440 | tf_op jit(solution)/shard_map/reduce_scatter | solution.py:253
  1265.2 109.9 %all-gather.38.cloned.1.call-start = ((), (), s32[]{:S(2)}) async-start(), calls=%async_computation.31 | async-start | bytes 2621440 | tf_op jit(solution)/shard_map/all_gather | solution.py:210
  1330.4 114.8 %reduce-scatter.33.cloned.1.call-start = ((), (), s32[]{:S(2)}) async-start(), calls=%async_computation.32 | async-start | bytes 2621440 | tf_op jit(solution)/shard_map/reduce_scatter | solution.py:221
  1403.2 135.1 %all-gather.50.cloned.1.call-start = ((), (), s32[]{:S(2)}) async-start(), calls=%async_computation.39 | async-start | bytes 2621440 | tf_op jit(solution)/shard_map/all_gather | solution.py:37
  1403.8 180.9 %all-gather.44.cloned.1.call-start = ((), (), s32[]{:S(2)}) async-start(), calls=%async_computation.36 | async-start | bytes 2621440 | tf_op jit(solution)/shard_map/all_gather | solution.py:33
  1404.5 226.3 %all-gather.52.cloned.1.call-start = ((), (), s32[]{:S(2)}) async-start(), calls=%async_computation.40 | async-start | bytes 2621440 | tf_op jit(solution)/shard_map/all_gather | solution.py:37
  1405.1 272.5 %all-gather.40.cloned.1.call-start = ((), (), s32[]{:S(2)}) async-start(), calls=%async_computation.33 | async-start | bytes 2621440 | tf_op jit(solution)/shard_map/all_gather | solution.py:232
  1453.4 310.3 %all-gather.46.cloned.1.call-start = ((), (), s32[]{:S(2)}) async-start(), calls=%async_computation.37 | async-start | bytes 2621440 | tf_op jit(solution)/shard_map/all_gather | solution.py:33
  1454.2 318.3 %all-gather.42.cloned.1.call-start = ((), (), s32[]{:S(2)}) async-start(), calls=%async_computation.35 | async-start | bytes 2621440 | tf_op jit(solution)/shard_map/all_gather | solution.py:33
  1504.0 435.4 %all-reduce.5.cloned.1.call-start = ((), (), s32[]{:S(2)}) async-start(), calls=%async_computation.42 | async-start | bytes 16777216 | tf_op jit(solution)/shard_map/psum | solution.py:282
  1782.6 203.9 %reduce-scatter.35.cloned.1.call-start = ((), (), s32[]{:S(2)}) async-start(), calls=%async_computation.34 | async-start | bytes 2621440 | tf_op jit(solution)/shard_map/reduce_scatter | solution.py:253
  (274 other events, 3876.4 us)
Sparse Core Ops, SparseCore 0:
  10.2 48.6 all-gather.53
  98.4 42.5 reduce-scatter.12
  146.4 45.2 all-gather.19
  206.3 42.5 reduce-scatter.14
  270.2 46.4 all-gather.21
  407.1 45.2 all-gather.23
  517.0 45.2 all-gather.29
  645.4 46.4 all-gather.25
  785.7 45.2 all-gather.31
  832.4 44.6 all-gather.27
  916.7 43.9 reduce-scatter.26
  963.5 43.1 reduce-scatter.22
  1014.2 45.2 all-gather.33
  1131.4 45.2 all-gather.35
  1330.5 44.5 all-gather.37
  1446.8 45.2 all-gather.47
  1493.6 44.6 all-gather.49
  1539.9 44.6 all-gather.43
  1586.1 44.5 all-gather.51
  1632.8 44.6 all-gather.39
  1679.2 44.6 all-gather.45
  1725.5 44.6 all-gather.41
  1782.7 156.7 all-reduce.4
  1942.4 44.0 reduce-scatter.34
  (7 shorter events, 297.6 us)
where the time goes:
time: 2010 us; the launch traced here: 2000 us
  waiting for transfers between devices  1220 us (61%)
  matrix products  351 us (17%)
  local copies, waits for them, and re-layouts  178 us (9%)
  other arithmetic  174 us (9%)
  blocking collectives  40.2 us (2%)
    all_gather x6, waiting for transfers between devices, gather_middle(): return lax.all_gather(row_shard, 'tensor', axis=0, tiled=True)  180 us
    all_gather x6, waiting for transfers between devices, gather_rows(): return lax.all_gather(row_shard, 'tensor', axis=0, tiled=True)  172 us
    all_gather x3, waiting for transfers between devices, layer_backward(): lax.all_gather(grad_mlp.astype(jnp.bfloat16), 'tensor', axis=0, tiled=True)  135 us
    reduce_scatter x3, waiting for transfers between devices, layer_forward(): lax.psum_scatter(jnp.dot(attended_low, output_w, preferred_element_type=j...  128 us
    reduce_scatter x3, waiting for transfers between devices, layer_backward(): lax.psum_scatter((jnp.einsum('lf,df->ld', up_back, up_w, preferred_elemen...  125 us
    reduce_scatter x3, waiting for transfers between devices, layer_forward(): lax.psum_scatter(jnp.dot(inner_low, down_w, preferred_element_type=jnp.fl...  125 us
    all_gather x3, waiting for transfers between devices, layer_backward(): lax.all_gather(grad_attn.astype(jnp.bfloat16), 'tensor', axis=0, tiled=True)  106 us
    reduce_scatter x3, waiting for transfers between devices, layer_backward(): lax.psum_scatter((jnp.einsum('lh,dh->ld', query_back, query_w, preferred_...  102 us
  transfers between devices with their start and end apart: 35, of which 31 were waited for; matrix products, arithmetic and copies ran while one was open for 16% of the time, Pallas kernels for 0%

commit v1 on v0

v1 whole, which is shorter than its diff:
```python
import functools

import jax
import jax.numpy as jnp
from jax import lax
from jax.experimental import pallas as pl
from jax.experimental.pallas import tpu as pltpu
from jax.sharding import PartitionSpec as P

HD = 64
EPS = 1e-06
AXES = ("section", "tensor", "dp")
F32 = jnp.float32
LOW = jnp.bfloat16
VMEM_LIMIT = 50 * 1024 * 1024


def cost(flops, bytes_accessed, transcendentals):
    return pl.CostEstimate(flops=0, bytes_accessed=0, transcendentals=0)


class Place:
    def __init__(self, mesh):
        self.sections = mesh.shape["section"]
        self.tensors = mesh.shape["tensor"]
        self.replicas = mesh.shape["dp"]
        self.lanes = self.tensors // 2
        self.pairs = self.replicas // 2
        self.lane_bits = [1 << bit for bit in range(self.lanes.bit_length() - 1)]
        self.pair_bits = [1 << bit for bit in range(self.pairs.bit_length() - 1)]

    def here(self):
        tensor = lax.axis_index("tensor")
        replica = lax.axis_index("dp")
        self.section = lax.axis_index("section")
        self.half = tensor // self.lanes
        self.lane = tensor % self.lanes
        self.pair = replica // 2
        self.core = replica % 2
        self.own = self.half == self.core
        self.first = self.section == 0

    def move(self, value, target):
        def index(section, half, lane, pair, core):
            tensor = half * self.lanes + lane
            return (section * self.tensors + tensor) * self.replicas + pair * 2 + core

        links = []
        for section in range(self.sections):
            for half in range(2):
                for lane in range(self.lanes):
                    for pair in range(self.pairs):
                        for core in range(2):
                            source = (section, half, lane, pair, core)
                            sink = target(*source)
                            if sink is not None:
                                links.append((index(*source), index(*sink)))
        return lax.ppermute(value, AXES, links)

    def across_cores(self, value):
        return self.move(value, lambda s, h, l, p, c: (s, h, l, p, 1 - c))

    def across_lanes(self, value, bit):
        return self.move(value, lambda s, h, l, p, c: (s, h, l ^ bit, p, c))


def to_section(s, h, l, p, c):
    return (1 - s, h, l, p, c)


def to_core(s, h, l, p, c):
    return (s, h, l, p, 1 - c)


def to_half(s, h, l, p, c):
    return (s, 1 - h, l, p, c)


def transposed(s, h, l, p, c):
    return (s, c, l, p, h) if h != c else None


def to_pair(bit):
    return lambda s, h, l, p, c: (s, h, l, p ^ bit, c)


def to_lane(bit):
    return lambda s, h, l, p, c: (s, h, l ^ bit, p, c)


def only(target, test):
    return lambda s, h, l, p, c: target(s, h, l, p, c) if test(s, h, c) else None


class Background:
    def __init__(self, place):
        self.place = place
        self.waiting = []
        self.active = []

    def add(self, task):
        self.waiting.append(task)

    def busy(self):
        return bool(self.waiting or self.active)

    def step(self, anchor, starts=1):
        if not self.busy():
            return anchor
        due = [entry for entry in self.active if entry[2] <= 1]
        kept = [(task, flying, left - 1) for task, flying, left in self.active if left > 1]
        anchor, landed = lax.optimization_barrier((anchor, [flying for _, flying, _ in due]))
        tasks = [(task, arrived) for (task, _, _), arrived in zip(due, landed)]
        for _ in range(starts):
            if self.waiting:
                tasks.append((self.waiting.pop(0), None))
        asked = []
        for task, arrived in tasks:
            try:
                wanted = task.send(arrived)
            except StopIteration:
                continue
            wanted, steps = wanted if isinstance(wanted, tuple) else (wanted, 1)
            asked.append((task, wanted, steps))
        arrays = [[array for array, _ in wanted] for _, wanted, _ in asked]
        anchor, arrays = lax.optimization_barrier((anchor, arrays))
        self.active = kept + [
            (
                task,
                [self.place.move(array, target) for array, (_, target) in zip(ready, wanted)],
                steps,
            )
            for (task, wanted, steps), ready in zip(asked, arrays)
        ]
        return anchor

    def drain(self):
        while self.busy():
            self.step((), 8)


def spec(count):
    return [pl.BlockSpec(memory_space=pltpu.VMEM)] * count


def mean_of(values):
    return jnp.mean(values, axis=-1, keepdims=True)


def load_terms(refs, swaps, lanes):
    total = refs[0][...].astype(F32)
    for ref, bit in zip(refs[1:], swaps[1:]):
        part = ref.shape[0] // lanes
        order = [ref[(at ^ bit) * part : ((at ^ bit) + 1) * part, :] for at in range(lanes)]
        value = order[0] if lanes == 1 else jnp.concatenate(order, axis=0)
        total = total + value.astype(F32)
    return total


def blend_forward(lanes, hidden, branch, rate, out_dtypes):
    rows, width = hidden.shape
    branch, swaps = zip(*branch)

    def kernel(*refs):
        hidden_ref, rate_ref = refs[:2]
        branch_refs = refs[2 : 2 + len(branch)]
        out_refs = refs[2 + len(branch) :]
        h = hidden_ref[...].astype(F32)
        b = load_terms(branch_refs, swaps, lanes)
        mixed = b * lax.rsqrt(mean_of(b * b) + EPS)
        u = h + rate_ref[...] * (mixed - h)
        y = u * lax.rsqrt(mean_of(u * u) + EPS)
        for ref in out_refs:
            ref[...] = y.astype(ref.dtype)

    return pl.pallas_call(
        kernel,
        out_shape=[jax.ShapeDtypeStruct((rows, width), kind) for kind in out_dtypes],
        in_specs=spec(2 + len(branch)),
        out_specs=spec(len(out_dtypes)),
        compiler_params=pltpu.CompilerParams(vmem_limit_bytes=VMEM_LIMIT),
        cost_estimate=cost(
            flops=12 * rows * width, bytes_accessed=10 * rows * width, transcendentals=0
        ),
        name="blend_forward",
    )(hidden, rate, *branch)


def blend_backward(lanes, hidden, branch, rate, grads):
    rows, width = hidden.shape
    branch, branch_swaps = zip(*branch)
    grads, grad_swaps = zip(*grads)
    branches = len(branch)

    def kernel(*refs):
        hidden_ref, rate_ref = refs[:2]
        hidden_out, branch_out, rate_out = refs[-3:]
        h = hidden_ref[...].astype(F32)
        b = load_terms(refs[2 : 2 + branches], branch_swaps, lanes)
        g = load_terms(refs[2 + branches : -3], grad_swaps, lanes)
        a = rate_ref[...]
        root_b = lax.rsqrt(mean_of(b * b) + EPS)
        delta = b * root_b - h
        u = h + a * delta
        root_u = lax.rsqrt(mean_of(u * u) + EPS)
        grad_u = root_u * g - u * (root_u * root_u * root_u * mean_of(u * g))
        grad_mixed = grad_u * a
        hidden_out[...] = grad_u - grad_mixed
        rate_out[...] = jnp.sum(grad_u * delta, axis=0, keepdims=True)
        grad_b = root_b * grad_mixed - b * (
            root_b * root_b * root_b * mean_of(b * grad_mixed)
        )
        branch_out[...] = grad_b.astype(branch_out.dtype)

    return pl.pallas_call(
        kernel,
        out_shape=[
            jax.ShapeDtypeStruct((rows, width), F32),
            jax.ShapeDtypeStruct((rows, width), LOW),
            jax.ShapeDtypeStruct((1, width), F32),
        ],
        in_specs=spec(2 + branches + len(grads)),
        out_specs=spec(3),
        compiler_params=pltpu.CompilerParams(vmem_limit_bytes=VMEM_LIMIT),
        cost_estimate=cost(
            flops=30 * rows * width, bytes_accessed=20 * rows * width, transcendentals=0
        ),
        name="blend_backward",
    )(hidden, rate, *branch, *grads)


def head_masks(width):
    lanes = lax.broadcasted_iota(jnp.int32, (1, width), 1)
    return [
        (lanes >= head * HD) & (lanes < (head + 1) * HD) for head in range(width // HD)
    ]


def head_mean(values, masks):
    if len(masks) == 1:
        return jnp.sum(values, axis=-1, keepdims=True) * (1.0 / HD)
    result = None
    for mask in masks:
        total = jnp.sum(jnp.where(mask, values, 0.0), axis=-1, keepdims=True) * (1.0 / HD)
        result = total if result is None else jnp.where(mask, total, result)
    return result


def nt_dot(left, right):
    return lax.dot_general(left, right, (((1,), (1,)), ((), ())), preferred_element_type=F32)


def tn_dot(left, right):
    return lax.dot_general(left, right, (((0,), (0,)), ((), ())), preferred_element_type=F32)


def nn_dot(left, right):
    return lax.dot_general(left, right, (((1,), (0,)), ((), ())), preferred_element_type=F32)


def fused_dot(xs, used, tiled, outs, epilogue, tile, name, keep=None, at=0, count=1, total=None):
    rows = sum(piece.shape[0] for piece in xs[0])
    outer = used[0][3][0] if len(used[0]) > 3 else used[0][1].shape[0 if used[0][2] else 1]
    tile = min(tile, outer)
    steps = outer // tile
    operands, in_specs = [], []

    def whole(array):
        operands.append(array)
        in_specs.append(pl.BlockSpec(array.shape, lambda i: (0, 0)))

    for pieces in xs:
        for piece in pieces:
            whole(piece)
    for _, weight, flipped, *place in used:
        operands.append(weight)
        begin = place[0][1] if place else 0
        if flipped:
            in_specs.append(pl.BlockSpec((tile, weight.shape[1]), lambda i: (i, 0)))
        else:
            in_specs.append(
                pl.BlockSpec((weight.shape[0], tile), lambda i, begin=begin: (0, begin + i))
            )
    for array, stacked in tiled:
        operands.append(array)
        if stacked:
            in_specs.append(pl.BlockSpec((rows, tile), lambda i: (at, i)))
        else:
            in_specs.append(pl.BlockSpec((array.shape[0], tile), lambda i: (0, i)))
    total_weights = total[0] if total else []
    for weight, flipped in total_weights:
        operands.append(weight)
        if flipped:
            in_specs.append(pl.BlockSpec((weight.shape[0], tile), lambda i: (0, i)))
        else:
            in_specs.append(pl.BlockSpec((tile, weight.shape[1]), lambda i: (i, 0)))
    out_shape, out_specs, aliases, behind = [], [], {}, []

    def stacked_out(kind, columns, block, index, stack):
        if stack:
            aliases[len(operands) + len(behind)] = len(out_shape)
            behind.append(stack[-1])
        out_shape.append(jax.ShapeDtypeStruct((rows * count, columns), kind))
        out_specs.append(pl.BlockSpec(block, index))

    for out_rows, kind, stack in outs:
        if stack is None:
            out_shape.append(jax.ShapeDtypeStruct((out_rows, outer), kind))
            out_specs.append(pl.BlockSpec((out_rows, tile), lambda i: (0, i)))
        else:
            stacked_out(kind, outer, (rows, tile), lambda i: (at, i), stack)
    inner = xs[0][0].shape[1]
    if keep is not None:
        stacked_out(LOW, inner, (rows, inner), lambda i: (at, 0), keep)
    pieces_out = 0
    scratch = []
    if total:
        weight, flipped = total_weights[0]
        columns = weight.shape[0 if flipped else 1]
        pieces_out = 2
        for _ in range(2):
            out_shape.append(jax.ShapeDtypeStruct((rows // 2, columns), LOW))
            out_specs.append(pl.BlockSpec((rows // 2, columns), lambda i: (0, 0)))
        scratch.append(pltpu.VMEM((rows, columns), F32))
    counts = [len(pieces) for pieces in xs]

    def kernel(*refs):
        refs = list(refs)

        def take(number):
            taken, refs[:number] = refs[:number], []
            return taken

        x_refs = [take(number) for number in counts]
        weight_refs = take(len(used))
        tiled_refs = take(len(tiled))
        total_refs = take(len(total_weights))
        take(len(behind))
        out_refs = take(len(outs))
        keep_ref = take(1)[0] if keep is not None else None
        piece_refs = take(pieces_out)
        step = pl.program_id(0)
        if keep_ref is not None:

            @pl.when(step == 0)
            def _():
                start = 0
                for ref in x_refs[0]:
                    keep_ref[start : start + ref.shape[0], :] = ref[...]
                    start += ref.shape[0]

        values = [keep_ref if at_x == 0 and keep_ref is not None else members[0]
                  for at_x, members in enumerate(x_refs)]
        dots = [
            (nt_dot if flipped else nn_dot)(values[which][...], ref[...])
            for (which, _, flipped, *_), ref in zip(used, weight_refs)
        ]
        results, terms = epilogue(dots, [ref[...] for ref in tiled_refs])
        for ref, result in zip(out_refs, results):
            ref[...] = result.astype(ref.dtype)
        if total:
            sum_ref = refs[0]
            term = None
            for (_, flipped), ref, value in zip(total_weights, total_refs, terms):
                product = (nt_dot if flipped else nn_dot)(value, ref[...])
                term = product if term is None else term + product

            @pl.when(step == 0)
            def _():
                sum_ref[...] = term

            @pl.when(step > 0)
            def _():
                sum_ref[...] += term

            @pl.when(step == steps - 1)
            def _():
                start = 0
                for ref in piece_refs:
                    ref[...] = sum_ref[start : start + ref.shape[0], :].astype(LOW)
                    start += ref.shape[0]

    flops = sum(2 * rows * weight.shape[0] * weight.shape[1] for _, weight, *_ in used)
    flops += sum(2 * rows * weight.shape[0] * weight.shape[1] for weight, _ in total_weights)
    moved = sum(array.size * array.dtype.itemsize for array in operands)
    results = pl.pallas_call(
        kernel,
        grid=(steps,),
        out_shape=out_shape,
        in_specs=in_specs + [pl.BlockSpec(memory_space=pl.ANY)] * len(behind),
        out_specs=out_specs,
        scratch_shapes=scratch,
        input_output_aliases=aliases,
        compiler_params=pltpu.CompilerParams(
            vmem_limit_bytes=VMEM_LIMIT, dimension_semantics=("arbitrary",)
        ),
        cost_estimate=cost(flops=flops, bytes_accessed=2 * moved, transcendentals=0),
        name=name,
    )(*operands, *behind)
    results = list(results)
    for (_, _, stack), result in zip(outs, results):
        if stack is not None:
            stack.append(result)
    if keep is not None:
        keep.append(results[len(outs)])
    return results[: len(outs)], results[len(results) - pieces_out :]


def project(pieces, packed, width, at, count, keep):
    rows = sum(piece.shape[0] for piece in pieces)
    used = 3 * width if width % 128 == 0 else 4 * width
    results, _ = fused_dot(
        [pieces],
        [(0, packed, False, (used, 0))],
        [],
        [(rows, F32, None)],
        lambda dots, _: (dots, None),
        width if width % 128 == 0 else used,
        "project",
        keep=keep,
        at=at,
        count=count,
    )
    return results[0]


def mlp_forward(pieces, weights, scales, at, count, stacks):
    up_w, gate_w, down_w = weights
    rows = sum(piece.shape[0] for piece in pieces)

    def epilogue(dots, tiles):
        up_raw, gate_raw = dots
        up_scale, gate_scale = tiles
        gated = gate_raw * gate_scale
        inner = (gated / (1.0 + jnp.exp(-gated)) * (up_raw * up_scale)).astype(LOW)
        return [up_raw, gate_raw, inner], [inner]

    mid, up_raw, gate_raw, inner = stacks
    _, out = fused_dot(
        [pieces],
        [(0, up_w, False), (0, gate_w, False)],
        [(scales[0], False), (scales[1], False)],
        [(rows, LOW, up_raw), (rows, LOW, gate_raw), (rows, LOW, inner)],
        epilogue,
        256,
        "mlp_forward",
        keep=mid,
        at=at,
        count=count,
        total=([(down_w, False)], None),
    )
    return out


def mlp_backward(pieces, weights, scales, raws, at, count, stacks):
    up_w, gate_w, down_w = weights
    rows = sum(piece.shape[0] for piece in pieces)

    def epilogue(dots, tiles):
        up_raw, gate_raw, up_scale, gate_scale = tiles
        up_raw, gate_raw = up_raw.astype(F32), gate_raw.astype(F32)
        grad = dots[0]
        gated = gate_raw * gate_scale
        sigmoid = 1.0 / (1.0 + jnp.exp(-gated))
        silu = gated * sigmoid
        slope = sigmoid * (1.0 + gated * (1.0 - sigmoid))
        from_up = grad * silu
        from_gate = grad * (up_raw * up_scale) * slope
        up_back = (from_up * up_scale).astype(LOW)
        gate_back = (from_gate * gate_scale).astype(LOW)
        up_sum = jnp.sum(from_up * up_raw, axis=0, keepdims=True)
        gate_sum = jnp.sum(from_gate * gate_raw, axis=0, keepdims=True)
        return [up_back, gate_back, up_sum, gate_sum], [up_back, gate_back]

    full, up_back, gate_back = stacks
    results, out = fused_dot(
        [pieces],
        [(0, down_w, True)],
        [(raws[0], True), (raws[1], True), (scales[0], False), (scales[1], False)],
        [(rows, LOW, up_back), (rows, LOW, gate_back), (1, F32, None), (1, F32, None)],
        epilogue,
        256,
        "mlp_backward",
        keep=full,
        at=at,
        count=count,
        total=([(up_w, True), (gate_w, True)], None),
    )
    return results[2], results[3], out


def output_backward(pieces, output_w, at, count, keep):
    rows = sum(piece.shape[0] for piece in pieces)
    results, _ = fused_dot(
        [pieces],
        [(0, output_w, True)],
        [],
        [(rows, LOW, None)],
        lambda dots, _: (dots, None),
        256,
        "output_backward",
        keep=keep,
        at=at,
        count=count,
    )
    return results[0]


def block_starts(places_ref, blocks, part):
    return [
        (block, pl.multiple_of(places_ref[block] * part, part)) for block in range(blocks)
    ]


def load_heads(starts, part, width, gain, masks, raw_ref, query, key, value):
    for block, start in starts:
        rows = pl.ds(block * part, part)
        place = pl.ds(start, part)
        raw = raw_ref[rows, 0:width]
        root = lax.rsqrt(head_mean(raw * raw, masks) + EPS)
        query[place, :] = (raw * root * gain).astype(LOW) * LOW(HD ** (-0.5))
        raw = raw_ref[rows, width : 2 * width]
        root = lax.rsqrt(head_mean(raw * raw, masks) + EPS)
        key[place, :] = (raw * root * gain).astype(LOW)
        value[place, :] = raw_ref[rows, 2 * width : 3 * width].astype(LOW)


def whole_spec(array):
    return pl.BlockSpec(array.shape, lambda i: (0, 0))


def stacked_specs(stack, operands):
    if not stack:
        return [], [], {}
    return [stack[-1]], [pl.BlockSpec(memory_space=pl.ANY)], {operands: 0}


def attention_forward(places, scale, raw, output_w, at, count, stack):
    width = scale.shape[1]
    blocks = places.shape[0]
    length = raw.shape[0]
    part = length // blocks
    span = min(256, length)
    model = output_w.shape[1]
    behind, behind_specs, aliases = stacked_specs(stack, 4)

    def kernel(*refs):
        places_ref, scale_ref, output_ref, raw_ref = refs[:4]
        attended_ref, mine_ref, theirs_ref, query, key, value, result = refs[4 + len(behind) :]
        masks = head_masks(width)
        starts = block_starts(places_ref, blocks, part)
        load_heads(starts, part, width, scale_ref[...], masks, raw_ref, query, key, value)
        row_at = lax.broadcasted_iota(jnp.int32, (span, span), 0)
        col_at = lax.broadcasted_iota(jnp.int32, (span, span), 1)
        causal = col_at <= row_at
        for begin in range(0, length, span):
            rows = query[begin : begin + span, :]
            total = None
            for mask in masks:
                picked = jnp.where(mask, rows, LOW(0))
                last = nt_dot(picked, key[begin : begin + span, :])
                last = jnp.where(causal, jnp.exp(last), 0.0)
                weight = jnp.sum(last, axis=-1, keepdims=True)
                head = nn_dot(last.astype(LOW), value[begin : begin + span, :])
                if begin > 0:
                    first = jnp.exp(nt_dot(picked, key[0:begin, :]))
                    weight = weight + jnp.sum(first, axis=-1, keepdims=True)
                    head = head + nn_dot(first.astype(LOW), value[0:begin, :])
                head = head * (1.0 / weight)
                total = head if total is None else jnp.where(mask, head, total)
            result[begin : begin + span, :] = total.astype(LOW)
        for block, start in starts:
            attended_ref[block * part : (block + 1) * part, :] = result[pl.ds(start, part), :]
        half = length // 2
        mine_ref[...] = nn_dot(attended_ref[:half, :], output_ref[...]).astype(LOW)
        theirs_ref[...] = nn_dot(attended_ref[half:, :], output_ref[...]).astype(LOW)

    attended, mine, theirs = pl.pallas_call(
        kernel,
        grid=(1,),
        out_shape=[
            jax.ShapeDtypeStruct((length * count, width), LOW),
            jax.ShapeDtypeStruct((length // 2, model), LOW),
            jax.ShapeDtypeStruct((length // 2, model), LOW),
        ],
        in_specs=[pl.BlockSpec(memory_space=pltpu.SMEM)]
        + [whole_spec(array) for array in (scale, output_w, raw)]
        + behind_specs,
        out_specs=[pl.BlockSpec((length, width), lambda i: (at, 0))]
        + [pl.BlockSpec((length // 2, model), lambda i: (0, 0))] * 2,
        scratch_shapes=[pltpu.VMEM((length, width), LOW)] * 4,
        input_output_aliases=aliases,
        compiler_params=pltpu.CompilerParams(vmem_limit_bytes=VMEM_LIMIT),
        cost_estimate=cost(
            flops=8 * length * length * width,
            bytes_accessed=24 * length * width,
            transcendentals=length * length * (width // HD),
        ),
        name="attention_forward",
    )(places, scale, output_w, raw, *behind)
    stack.append(attended)
    return mine, theirs


def attention_backward(places, scale, raw, grads, packed, at, count, stack):
    width = scale.shape[1]
    blocks = places.shape[0]
    length = raw.shape[0]
    part = length // blocks
    span = min(256, length)
    model = packed.shape[0]
    behind, behind_specs, aliases = stacked_specs(stack, 5)

    def kernel(*refs):
        places_ref, scale_ref, packed_ref, raw_ref, grad_ref = refs[:5]
        back_ref, scale_out, mine_ref, theirs_ref = refs[5 + len(behind) : 9 + len(behind)]
        query, key, value, grad, query_sum, key_sum, value_sum = refs[9 + len(behind) :]
        masks = head_masks(width)
        gain = scale_ref[...]
        starts = block_starts(places_ref, blocks, part)
        load_heads(starts, part, width, gain, masks, raw_ref, query, key, value)
        for block, start in starts:
            grad[pl.ds(start, part), :] = grad_ref[block * part : (block + 1) * part, :]
        key_sum[...] = jnp.zeros_like(key_sum)
        value_sum[...] = jnp.zeros_like(value_sum)
        key_at = lax.broadcasted_iota(jnp.int32, (span, span), 0)
        query_at = lax.broadcasted_iota(jnp.int32, (span, span), 1)
        causal = key_at <= query_at
        for origin in range(0, length, span):
            rows = query[origin : origin + span, :]
            grad_rows = grad[origin : origin + span, :]
            total = None
            for mask in masks:
                picked = jnp.where(mask, rows, LOW(0))
                grad_picked = jnp.where(mask, grad_rows, LOW(0))
                pieces = [slice(0, origin)] if origin > 0 else []
                pieces.append(slice(origin, origin + span))
                raised = [jnp.exp(nt_dot(key[piece, :], picked)) for piece in pieces]
                raised[-1] = jnp.where(causal, raised[-1], 0.0)
                weight = sum(jnp.sum(member, axis=0, keepdims=True) for member in raised)
                inverse = 1.0 / weight
                probs = [member * inverse for member in raised]
                grad_probs = [nt_dot(value[piece, :], grad_picked) for piece in pieces]
                row_sum = sum(
                    jnp.sum(left * right, axis=0, keepdims=True)
                    for left, right in zip(probs, grad_probs)
                )
                head = None
                for piece, prob, grad_prob in zip(pieces, probs, grad_probs):
                    grad_score = (prob * (grad_prob - row_sum)).astype(LOW)
                    value_sum[piece, :] += nn_dot(prob.astype(LOW), grad_picked)
                    key_sum[piece, :] += nn_dot(grad_score, picked)
                    term = tn_dot(grad_score, key[piece, :])
                    head = term if head is None else head + term
                total = head if total is None else jnp.where(mask, head, total)
            query_sum[origin : origin + span, :] = total * (HD ** (-0.5))
        scale_sum = jnp.zeros((1, width), F32)
        for block, start in starts:
            rows = slice(block * part, (block + 1) * part)
            place = pl.ds(start, part)
            for slot, source in ((0, query_sum), (1, key_sum)):
                lanes = slice(slot * width, (slot + 1) * width)
                raw_rows = raw_ref[rows, lanes]
                root = lax.rsqrt(head_mean(raw_rows * raw_rows, masks) + EPS)
                grad_low = source[place, :]
                scale_sum = scale_sum + jnp.sum(
                    grad_low * (raw_rows * root), axis=0, keepdims=True
                )
                grad_unit = grad_low * gain
                cross = head_mean(raw_rows * grad_unit, masks)
                result = root * grad_unit - raw_rows * (root * root * root * cross)
                back_ref[rows, lanes] = result.astype(LOW)
            back_ref[rows, 2 * width : 3 * width] = value_sum[place, :].astype(LOW)
        scale_out[...] = scale_sum
        half = length // 2
        weights = packed_ref[:, : 3 * width]
        mine_ref[...] = nt_dot(back_ref[:half, :], weights).astype(LOW)
        theirs_ref[...] = nt_dot(back_ref[half:, :], weights).astype(LOW)

    back, scale_sum, mine, theirs = pl.pallas_call(
        kernel,
        grid=(1,),
        out_shape=[
            jax.ShapeDtypeStruct((length * count, 3 * width), LOW),
            jax.ShapeDtypeStruct((1, width), F32),
            jax.ShapeDtypeStruct((length // 2, model), LOW),
            jax.ShapeDtypeStruct((length // 2, model), LOW),
        ],
        in_specs=[pl.BlockSpec(memory_space=pltpu.SMEM)]
        + [whole_spec(array) for array in (scale, packed, raw, grads)]
        + behind_specs,
        out_specs=[
            pl.BlockSpec((length, 3 * width), lambda i: (at, 0)),
            pl.BlockSpec((1, width), lambda i: (0, 0)),
        ]
        + [pl.BlockSpec((length // 2, model), lambda i: (0, 0))] * 2,
        scratch_shapes=[pltpu.VMEM((length, width), LOW)] * 4
        + [pltpu.VMEM((length, width), F32)] * 3,
        input_output_aliases=aliases,
        compiler_params=pltpu.CompilerParams(vmem_limit_bytes=VMEM_LIMIT),
        cost_estimate=cost(
            flops=20 * length * length * width,
            bytes_accessed=32 * length * width,
            transcendentals=length * length * (width // HD),
        ),
        name="attention_backward",
    )(places, scale, packed, raw, grads, *behind)
    stack.append(back)
    return scale_sum, mine, theirs


def gather(place, value):
    half = value.shape[0] // 2
    return [value, place.across_cores(value[:half]), place.across_cores(value[half:])]


def gather_lanes(place, value):
    rows = [value]
    for bit in place.lane_bits:
        rows = rows + [place.across_lanes(member, bit) for member in rows]
    return jnp.concatenate(rows, axis=0)


def exchange(place, total):
    terms = [(total, 0)]
    for bit in place.lane_bits:
        total = terms[0][0]
        for value, swapped in terms[1:]:
            total = plus(total, unswapped(place, value, swapped))
        terms = [(total, 0), (place.across_lanes(total, bit), bit)]
    return terms


def unswapped(place, value, bit):
    part = value.shape[0] // place.lanes
    order = [value[(at ^ bit) * part : ((at ^ bit) + 1) * part] for at in range(place.lanes)]
    return jnp.concatenate(order, axis=0)


def spread_task(place, name, shard, steps, ready):
    rows = shard.shape[0] // place.pairs
    cut = lax.dynamic_slice_in_dim(shard, place.pair * rows, rows, 0)
    parts = yield [(cut, only(to_half, lambda s, h, c: c == h))], steps
    for bit in place.pair_bits:
        got = yield [(part, only(to_pair(bit), lambda s, h, c: c != h)) for part in parts]
        parts = parts + got
    ready[name] = assemble(place, shard, parts)


def assemble(place, shard, parts):
    pairs = place.pairs
    flags = jnp.stack([place.own.astype(jnp.int32), place.pair])

    def kernel(flags_ref, own_ref, *refs):
        part_refs, out_ref, sems = refs[:pairs], refs[pairs], refs[-1]

        @pl.when(flags_ref[0] == 1)
        def _():
            copy = pltpu.make_async_copy(own_ref, out_ref, sems.at[0])
            copy.start()
            copy.wait()

        @pl.when(flags_ref[0] == 0)
        def _():
            copies = []
            for step in range(pairs):
                rows = part_refs[step].shape[0]
                begin = pl.multiple_of((flags_ref[1] ^ step) * rows, rows)
                sink = out_ref.at[pl.ds(begin, rows), :]
                copies.append(pltpu.make_async_copy(part_refs[step], sink, sems.at[step]))
            for copy in copies:
                copy.start()
            for copy in copies:
                copy.wait()

    return pl.pallas_call(
        kernel,
        out_shape=jax.ShapeDtypeStruct(shard.shape, shard.dtype),
        in_specs=[pl.BlockSpec(memory_space=pltpu.SMEM)]
        + [pl.BlockSpec(memory_space=pl.ANY)] * (1 + pairs),
        out_specs=pl.BlockSpec(memory_space=pltpu.VMEM),
        scratch_shapes=[pltpu.SemaphoreType.DMA((pairs,))],
        compiler_params=pltpu.CompilerParams(vmem_limit_bytes=VMEM_LIMIT),
        cost_estimate=cost(
            flops=0, bytes_accessed=4 * shard.size, transcendentals=0
        ),
        name="assemble",
    )(flags, shard, *parts)


def halved(value, bit, rows):
    half = rows // 2
    kept = lax.dynamic_slice_in_dim(value, bit * half, half, 0)
    sent = lax.dynamic_slice_in_dim(value, (1 - bit) * half, half, 0)
    return kept, sent


def plus(left, right):
    return (left.astype(F32) + right.astype(F32)).astype(LOW)


def collect_task(place, grad, store):
    held = grad
    for bit in place.pair_bits[::-1]:
        kept, sent = halved(held, (place.pair // bit) % 2, held.shape[0])
        (met,) = yield [(sent, to_pair(bit))]
        held = plus(kept, met)
    (met,) = yield [(held, only(to_half, lambda s, h, c: c != h))]
    held = plus(held, met)
    parts = [held]
    for bit in place.pair_bits:
        got = yield [(value, only(to_pair(bit), lambda s, h, c: c == h)) for value in parts]
        parts = parts + got
    got = yield [(value, only(to_core, lambda s, h, c: c == h)) for value in parts]
    store.append((parts, got))


def finish(place, sides, shape, columns):
    pairs = place.pairs
    rows, width = shape
    piece = rows // pairs
    flags = jnp.stack([place.own.astype(jnp.int32), place.pair])
    operands = [member for side in sides for member in side]

    def kernel(flags_ref, *refs):
        part_refs = refs[: len(operands)]
        out_refs = refs[len(operands) : -2]
        landing, sems = refs[-2:]
        step = pl.program_id(0)

        @pl.when(step == 0)
        def _():
            for side in range(2):

                @pl.when(flags_ref[0] == 1 - side)
                def _():
                    for relative in range(pairs):
                        block = flags_ref[1] ^ relative
                        pltpu.make_async_copy(
                            part_refs[side * pairs + relative],
                            landing.at[block],
                            sems.at[block],
                        ).start()

        pltpu.make_async_copy(part_refs[0], landing.at[step], sems.at[step]).wait()
        value = landing[step].astype(F32)
        begin = 0
        for count, ref in zip(columns, out_refs):
            ref[...] = value[:, begin : begin + count]
            begin += count

    return pl.pallas_call(
        kernel,
        grid=(pairs,),
        out_shape=[jax.ShapeDtypeStruct((rows, count), F32) for count in columns],
        in_specs=[pl.BlockSpec(memory_space=pltpu.SMEM)]
        + [pl.BlockSpec(memory_space=pl.ANY)] * len(operands),
        out_specs=[pl.BlockSpec((piece, count), lambda i: (i, 0)) for count in columns],
        scratch_shapes=[
            pltpu.VMEM((pairs, piece, width), LOW),
            pltpu.SemaphoreType.DMA((pairs,)),
        ],
        compiler_params=pltpu.CompilerParams(
            vmem_limit_bytes=VMEM_LIMIT, dimension_semantics=("arbitrary",)
        ),
        cost_estimate=cost(
            flops=0, bytes_accessed=6 * rows * width, transcendentals=0
        ),
        name="finish",
    )(flags, *operands)


def move_task(place, value, target, store, steps=1):
    (met,) = yield [(value, target)], steps
    store.append(jnp.where(place.own, value, met))


def small_task(place, small, rates, store):
    count = small.shape[1]
    slots = jnp.concatenate(
        [jnp.where(place.core == slot, small, 0.0) for slot in range(2)] + [rates], axis=1
    )
    targets = [to_core, to_half] + [to_pair(bit) for bit in place.pair_bits]
    for target in targets:
        (met,) = yield [(slots, target)]
        slots = slots + met
    store.append(jnp.where(place.half == 0, slots[:, :count], slots[:, count : 2 * count]))
    store.append(slots[:, 2 * count :])


class Weights:
    def __init__(self, bg, width, ready):
        self.bg, self.width, self.ready = bg, width, ready

    def wait(self, names, anchor):
        while any(name not in self.ready for name in names):
            anchor = self.bg.step(anchor)
        if "out" not in self.ready:
            self.ready["out"] = self.ready["attn"][:, 3 * self.width :].T
        return anchor

    def __getitem__(self, name):
        return self.ready[name]


class Chain:
    def __init__(self, place, bg):
        self.place, self.bg = place, bg
        self.last = None
        self.ready = None

    def exchange(self, mine, theirs, starts=None):
        if self.last:
            flying = [value for value, _ in self.last]
            theirs, flying = lax.optimization_barrier((theirs, flying))
            self.last[:] = [(value, bit) for value, (_, bit) in zip(flying, self.last)]
        if starts is not None:
            theirs = self.bg.step(theirs, starts)
        self.ready = plus(mine, self.place.across_cores(theirs))
        self.last = []
        return self.last

    def after(self, values):
        if self.ready is not None:
            values, total = lax.optimization_barrier((values, self.ready))
            self.ready = None
            self.last[:] = exchange(self.place, total)
        return values

    def terms_after(self, terms):
        if terms is self.last and self.ready is not None:
            self.after([])
        values = self.after([value for value, _ in terms])
        return [(value, bit) for value, (_, bit) in zip(values, terms)]


def layer_forward(place, places, bg, chain, rows, weights, scales, late=None):
    qk_scale, attn_rate, up_scale, gate_scale, mlp_rate = scales
    width = qk_scale.shape[1]
    count = late[1] if late else len(rows)
    streams = range(count)
    lanes = place.lanes
    full_in, attended, raws, attn_terms = [], [], [], []
    for at in streams:
        if at == len(rows):
            rows.append(gather_lanes(place, chain.after(late[0][at])))
        pieces = chain.after(gather(place, rows[at]))
        pieces = weights.wait(("attn",), pieces)
        raws.append(project(pieces, weights["attn"], width, at, count, full_in))
        mine, theirs = attention_forward(
            places, qk_scale, raws[at], weights["out"], at, count, attended
        )
        attn_terms.append(chain.exchange(mine, theirs, 1))
    middles, mlp_terms, results = [], [], []
    stacks = [[], [], [], []]
    for at in streams:
        terms = chain.terms_after(attn_terms[at])
        middles.append(blend_forward(lanes, rows[at], terms, attn_rate, [F32, LOW]))
        pieces = gather(place, middles[at][1])
        pieces = weights.wait(("up", "gate", "down"), pieces)
        mine, theirs = mlp_forward(
            pieces,
            (weights["up"], weights["gate"], weights["down"]),
            (up_scale, gate_scale),
            at,
            count,
            stacks,
        )
        mlp_terms.append(chain.exchange(mine, theirs))
    for at in streams:
        results.append(
            blend_forward(
                lanes, middles[at][0], chain.terms_after(mlp_terms[at]), mlp_rate, [LOW]
            )[0]
        )
    kept = (rows, full_in[-1], raws, attended[-1], attn_terms, middles, stacks, mlp_terms)
    return results, kept


def layer_backward(place, places, chain, grads, kept, weights, scales, collect, starts):
    rows, full_in, raws, attended, attn_terms, middles, stacks, mlp_terms = kept
    full_mid, up_raw, gate_raw, inner = (stack[-1] for stack in stacks)
    qk_scale, attn_rate, up_scale, gate_scale, mlp_rate = scales
    count = len(rows)
    streams = range(count)
    lanes = place.lanes

    mlp_back, sums, mid_terms = [], [], []
    back_stacks = [[], [], []]
    for at in streams:
        terms = chain.terms_after(grads[at])
        mlp_back.append(
            blend_backward(lanes, middles[at][0], mlp_terms[at], mlp_rate, terms)
        )
        pieces = gather(place, mlp_back[at][1])
        up_sum, gate_sum, (mine, theirs) = mlp_backward(
            pieces,
            (weights["up"], weights["gate"], weights["down"]),
            (up_scale, gate_scale),
            (up_raw, gate_raw),
            at,
            count,
            back_stacks,
        )
        sums.append((up_sum, gate_sum))
        mid_terms.append(chain.exchange(mine, theirs, starts[at]))
    full_mlp, up_back, gate_back = chain.after([stack[-1] for stack in back_stacks])
    collect("down", tn_dot(inner, full_mlp).astype(LOW))
    collect("up", tn_dot(full_mid, up_back).astype(LOW))
    collect("gate", tn_dot(full_mid, gate_back).astype(LOW))
    attn_back, full_attn, back, in_terms, qk_sums = [], [], [], [], []
    for at in streams:
        terms = chain.terms_after([(mlp_back[at][0], 0)] + mid_terms[at])
        attn_back.append(blend_backward(lanes, rows[at], attn_terms[at], attn_rate, terms))
        pieces = gather(place, attn_back[at][1])
        grad_attended = output_backward(pieces, weights["out"], at, count, full_attn)
        qk_sum, mine, theirs = attention_backward(
            places, qk_scale, raws[at], grad_attended, weights["attn"], at, count, back
        )
        qk_sums.append(qk_sum)
        in_terms.append(chain.exchange(mine, theirs, starts[count + at]))
    last = chain.after(back[-1])
    collect(
        "attn",
        jnp.concatenate(
            [tn_dot(full_in, last), tn_dot(full_attn[-1], attended)], axis=1
        ).astype(LOW),
    )
    small = jnp.concatenate(
        [sum(qk_sums), sum(member[0] for member in sums), sum(member[1] for member in sums)],
        axis=1,
    )
    rates = jnp.concatenate(
        [sum(member[2] for member in attn_back), sum(member[2] for member in mlp_back)], axis=1
    )
    grad_rows = [[(attn_back[at][0], 0)] + in_terms[at] for at in streams]
    return grad_rows, small, rates


def body(place, *args):
    (
        hidden_in,
        cotangent,
        query_w,
        key_w,
        value_w,
        output_w,
        qk_scale,
        attn_rate,
        up_w,
        gate_w,
        down_w,
        up_scale,
        gate_scale,
        mlp_rate,
    ) = args
    place.here()
    first = place.first
    width, units = query_w.shape[2], up_w.shape[2]
    part = hidden_in.shape[2]
    streams = range(hidden_in.shape[0])
    bg = Background(place)
    chain = Chain(place, bg)

    shards = {
        "attn": jnp.concatenate([query_w[0], key_w[0], value_w[0], output_w[0].T], axis=1),
        "up": up_w[0],
        "gate": gate_w[0],
        "down": down_w[0],
    }
    ready = {}

    small_in = jnp.concatenate([qk_scale, up_scale, gate_scale], axis=1)
    start_rows, small_rows = [], []
    start = [jnp.where(first, hidden_in[at, 0], cotangent[at, 0]) for at in streams]
    bg.add(move_task(place, start[0], transposed, start_rows))
    bg.add(move_task(place, small_in, only(to_half, lambda s, h, c: c == h), small_rows))
    bg.add(spread_task(place, "attn", shards["attn"], 1, ready))
    for member in start[1:]:
        bg.add(move_task(place, member, transposed, start_rows, 2))
    for name in ("up", "gate", "down"):
        bg.add(spread_task(place, name, shards[name], 2, ready))
    bg.step((), 3)
    bg.step((), len(start))
    start = [gather_lanes(place, start_rows[0])]
    edges = [0, width, width + units, width + 2 * units]
    qk, up, gate = (small_rows[0][:, a:b] for a, b in zip(edges[:3], edges[1:]))
    scales = (qk, attn_rate, up, gate, mlp_rate)
    weights = Weights(bg, width, ready)

    blocks = [
        (place.core ^ other) * place.lanes + (place.lane ^ step)
        for other in range(2)
        for step in range(place.lanes)
    ]
    places = jnp.stack(blocks).astype(jnp.int32)

    def own_rows(members):
        return jnp.stack([member[:part] for member in members])

    def hop(value, source):
        return place.move(value, only(to_section, lambda s, h, c: s == source))

    def summed(terms):
        total = terms[0][0].astype(F32)
        for value, bit in terms[1:]:
            total = total + (unswapped(place, value, bit) if bit else value).astype(F32)
        return total.astype(LOW)

    first_out, kept_first = layer_forward(
        place, places, bg, chain, start, weights, scales, (start_rows, len(streams))
    )
    second_in = [hop(member, 0) for member in first_out]
    second_out, kept_second = layer_forward(place, places, bg, chain, second_in, weights, scales)
    hidden_out, grad_in, sums = [], [], []
    late = {}
    grad_mid, second_small, second_rates = layer_backward(
        place,
        places,
        chain,
        [[(member, 0)] for member in start],
        kept_second,
        weights,
        scales,
        late.__setitem__,
        [None] * (2 * len(streams)),
    )
    grad_second = [summed(terms) for terms in grad_mid]
    grad_back = [hop(member, 1) for member in grad_second]
    stores = {name: [] for name in shards}

    def collect(name, grad):
        mine = jnp.where(first, grad, late[name])
        bg.add(collect_task(place, mine, stores[name]))

    grad_start, first_small, first_rates = layer_backward(
        place,
        places,
        chain,
        [[(member, 0)] for member in grad_back],
        kept_first,
        weights,
        scales,
        collect,
        [None] * len(streams) + [2] + [1] * (len(streams) - 1),
    )
    grad_first = [summed(terms) for terms in grad_start]
    bg.add(
        small_task(
            place,
            jnp.where(first, first_small, second_small),
            jnp.where(first, first_rates, second_rates),
            sums,
        )
    )
    in_rows = jnp.where(first, own_rows(grad_first), own_rows(grad_second))
    bg.add(move_task(place, in_rows, transposed, grad_in))
    out_rows = jnp.where(first, own_rows(first_out), own_rows(second_out))
    bg.add(move_task(place, out_rows, transposed, hidden_out))
    bg.step((), 3)
    bg.drain()

    def done(name, columns):
        return finish(place, stores[name][0], shards[name].shape, columns)

    (down,) = done("down", [shards["down"].shape[1]])
    (up,) = done("up", [units])
    (gate,) = done("gate", [units])
    query, key, value, out = done("attn", [width] * 4)
    mine, total = sums
    model = total.shape[1] // 2
    return (
        hidden_out[0][None, :, None],
        grad_in[0].astype(F32)[None, :, None],
        query[None],
        key[None],
        value[None],
        out.T[None],
        mine[:, :width],
        total[:, :model],
        up[None],
        gate[None],
        down[None],
        mine[:, width : width + units],
        mine[:, width + units :],
        total[:, model:],
    )


def solution(mesh):
    rows = P(None, "dp", "tensor", None)
    columns = P("section", None, "tensor")
    units = P("section", "tensor", None)
    split = P("section", "tensor")
    whole = P("section", None)
    placed = P("section", None, "dp", "tensor", None)
    weights = (columns, columns, columns, units, split, whole, columns, columns, units)
    scales = (split, split, whole)
    return jax.shard_map(
        functools.partial(body, Place(mesh)),
        mesh=mesh,
        in_specs=(rows, rows) + weights + scales,
        out_specs=(placed, placed) + weights + scales,
        check_vma=False,
    )
```

time: 2010 us -> 1000 us (0.50)
  waiting for transfers between devices: 1220 us -> 343 us
  Pallas kernels: 0 us -> 360 us
  matrix products: 351 us -> 47 us
  starting transfers between devices: 13 us -> 165 us
  other arithmetic: 174 us -> 27.8 us
  local copies, waits for them, and re-layouts: 178 us -> 47.1 us
  blocking collectives: 40.2 us -> 0 us
    all_gather x18 -> x0, waiting for transfers between devices: 594 us -> none  [the longest x6 180 us: gather_middle(): return lax.all_gather(row_shard, 'tensor', axis=0, tiled=True)]
    reduce_scatter x12 -> x0, waiting for transfers between devices: 480 us -> none  [the longest x3 128 us: layer_forward(): lax.psum_scatter(jnp.dot(attended_low, output_w, preferred_element_type=j...]
    pallas_call x0 -> x48, Pallas kernels: none -> 360 us  [the longest x16 163 us: fused_dot(): pl.pallas_call(kernel, grid=(steps,), out_shape=out_shape, in_specs=in_sp...]
    ppermute x4 -> x106, waiting for transfers between devices: 36 us -> 343 us  [move(): return lax.ppermute(value, AXES, links)]
    dot_general x105 -> x10, matrix products: 351 us -> 47 us  [tn_dot(): lax.dot_general(left, right, (((0,), (0,)), ((), ())), preferred_element_...]
    ppermute x4 -> x106, starting transfers between devices: 9.56 us -> 165 us  [move(): return lax.ppermute(value, AXES, links)]
    psum x1 -> x0, waiting for transfers between devices: 102 us -> none  [replica_sum(): lax.psum(grad_list[0].astype(jnp.bfloat16), 'dp').astype(jnp.float32)]
    reduce_sum x40 -> x0, other arithmetic: 79.6 us -> none  [the longest x21 36.2 us: sphere(): jnp.mean(values * values, axis=-1, keepdims=True) + 1e-06]
  transfers between devices with their start and end apart: 35 -> 106, of which waited for: 31 -> 54; matrix products, arithmetic and copies ran while one was open for 16% -> 8% of each run, Pallas kernels for 0% -> 34%
where the time goes in v1:
time: 1000 us; the launch traced here: 992 us
  Pallas kernels  360 us (36%)
  waiting for transfers between devices  343 us (34%)
  starting transfers between devices  165 us (16%)
  local copies, waits for them, and re-layouts  47.1 us (5%)
  matrix products  47 us (5%)
  other arithmetic  27.8 us (3%)
    ppermute x106, waiting for transfers between devices, move(): return lax.ppermute(value, AXES, links)  343 us
    ppermute x106, starting transfers between devices, move(): return lax.ppermute(value, AXES, links)  165 us
    pallas_call x16, Pallas kernels, fused_dot(): pl.pallas_call(kernel, grid=(steps,), out_shape=out_shape, in_specs=in_sp...  163 us
    pallas_call x4, Pallas kernels, attention_backward(): pl.pallas_call(kernel, grid=(1,), out_shape=[jax.ShapeDtypeStruct((length...  69.6 us
    dot_general x10, matrix products, tn_dot(): lax.dot_general(left, right, (((0,), (0,)), ((), ())), preferred_element_...  47 us
    pallas_call x8, Pallas kernels, blend_backward(): pl.pallas_call(kernel, out_shape=[jax.ShapeDtypeStruct((rows, width), F32...  45 us
    pallas_call x4, Pallas kernels, attention_forward(): pl.pallas_call(kernel, grid=(1,), out_shape=[jax.ShapeDtypeStruct((length...  29.1 us
    unnamed x230, local copies, waits for them, and re-layouts  28.4 us
  transfers between devices with their start and end apart: 106, of which 54 were waited for; matrix products, arithmetic and copies ran while one was open for 8% of the time, Pallas kernels for 34%

profile of v1, /device:TPU:0, one launch (start us, length us, event | category | flops | bytes accessed | tf_op | source)
XLA Modules:
  0.0 992.5 jit_solution(10077845189215971336)
XLA Ops:
  18.2 14.7 %collective-permute-done.1 = f32[1,2304]{1,0:T(1,128)S(1)} collective-permute-done((f32[1,2304]{1,0:T(1,128)S(1)}, f32[1,2304]{1,0:T(1,128)S(1)}, u32[]{:S(2)}, u32[]{:S(2)}) %collective-permute-start.1) | collective-permute-done | bytes 9248 | tf_op jit(solution)/shard_map/ppermute | solution.py:58
  33.0 18.5 %collective-permute-start.3 = (bf16[256,1024]{1,0:T(8,128)(2,1)S(1)}, bf16[256,1024]{1,0:T(8,128)(2,1)S(1)}, u32[]{:S(2)}, u32[]{:S(2)}) collective-permute-start(bf16[256,1024]{1,0:T(8,128)(2,1)S(1)} %broadcast_select_fusion.1), channel_id=1, source_target_pairs={{0,4},{1,5},{2,6},{3,7},{4,0},{5,1},{6,2},{7,3},{8,12},{9,13},{10,... | collective-permute-start | bytes 1572872 | tf_op jit(solution)/shard_map/ppermute | solution.py:58
  109.6 17.5 %collective-permute-done.10 = bf16[256,1024]{1,0:T(8,128)(2,1)S(1)} collective-permute-done((bf16[256,1024]{1,0:T(8,128)(2,1)S(1)}, bf16[256,1024]{1,0:T(8,128)(2,1)S(1)}, u32[]{:S(2)}, u32[]{:S(2)}) %collective-permute-start.10) | collective-permute-done | bytes 524320 | tf_op jit(solution)/shard_map/ppermute | solution.py:58
  190.6 13.7 %mlp_forward.4 = (bf16[2048,1024]{1,0:T(8,128)(2,1)}, bf16[2048,1024]{1,0:T(8,128)(2,1)}, bf16[2048,1024]{1,0:T(8,128)(2,1)}, bf16[2048,1024]{1,0:T(8,128)(2,1)}...) custom-call(bf16[512,1024]{1,0:T(8,128)(2,1)} %copy-done.10, ...), custom_call_target="tpu_custom_call" | custom-call | tf_op jit(solution)/shard_map/mlp_forward/pallas_call | solution.py:386
  247.1 22.3 %collective-permute-done.29.refs_0_ = bf16[512,1024]{1,0:T(8,128)(2,1)S(1)} collective-permute-done((bf16[512,1024]{1,0:T(8,128)(2,1)S(1)}, bf16[512,1024]{1,0:T(8,128)(2,1)S(1)}, u32[]{:S(2)}, u32[]{:S(2)}) %collective-permute-start.29) | collective-permute-done | bytes 1048608 | tf_op jit(solution)/shard_map/ppermute | solution.py:58
  337.9 13.7 %mlp_forward.6 = (bf16[2048,1024]{1,0:T(8,128)(2,1)}, bf16[2048,1024]{1,0:T(8,128)(2,1)}, bf16[2048,1024]{1,0:T(8,128)(2,1)}, bf16[2048,1024]{1,0:T(8,128)(2,1)}...) custom-call(bf16[512,1024]{1,0:T(8,128)(2,1)} %copy-done.15, ...), custom_call_target="tpu_custom_call" | custom-call | tf_op jit(solution)/shard_map/mlp_forward/pallas_call | solution.py:386
  366.3 14.2 %mlp_forward.7 = (bf16[2048,1024]{1,0:T(8,128)(2,1)}, bf16[2048,1024]{1,0:T(8,128)(2,1)}, bf16[2048,1024]{1,0:T(8,128)(2,1)}, bf16[2048,1024]{1,0:T(8,128)(2,1)}...) custom-call(bf16[512,1024]{1,0:T(8,128)(2,1)} %copy-done.14, ...), custom_call_target="tpu_custom_call", output_to_operand_aliasing={{0}: (8, {}), {1}: (9, {}), {2}: (10, {}), {3}: (11, {})} | custom-call | tf_op jit(solution)/shard_map/mlp_forward/pallas_call | solution.py:386
  397.0 19.8 %mlp_backward.4 = (bf16[2048,1024]{1,0:T(8,128)(2,1)}, bf16[2048,1024]{1,0:T(8,128)(2,1)}, f32[1,1024]{1,0:T(1,128)S(1)}, f32[1,1024]{1,0:T(1,128)S(1)}, bf16[20...) custom-call(bf16[512,1024]{1,0:T(8,128)(2,1)} %copy-done.23, ...), custom_call_target="tpu_custom_call" | custom-call | tf_op jit(solution)/shard_map/mlp_backward/pallas_call | solution.py:386
  429.9 19.8 %mlp_backward.5 = (bf16[2048,1024]{1,0:T(8,128)(2,1)}, bf16[2048,1024]{1,0:T(8,128)(2,1)}, f32[1,1024]{1,0:T(1,128)S(1)}, f32[1,1024]{1,0:T(1,128)S(1)}, bf16[20...) custom-call(bf16[512,1024]{1,0:T(8,128)(2,1)} %copy-done.12, ...), custom_call_target="tpu_custom_call", output_to_operand_aliasing={{0}: (10, {}), {1}: (11, {}), {4}: (12, {})} | custom-call | tf_op jit(solution)/shard_map/mlp_backward/pallas_call | solution.py:386
  463.9 17.3 %attention_backward.4 = (bf16[2048,768]{1,0:T(8,128)(2,1)}, f32[1,256]{1,0:T(1,128)S(1)}, bf16[512,1024]{1,0:T(8,128)(2,1)S(1)}, bf16[512,1024]{1,0:T(8,128)(2,1)S(1)}) custom-call(s32[4]{0:T(128)S(1)} %pad_add_fusion.refs_0_, f32[1,256]{1,0:T(1,128)S(1)} %slice.239.refs_1_, bf16[1024,1024]{1,0:T(8,128)(2,1)} %assemble.4.refs_3_.refs_2_, ...), custom_call_target="tpu_custom_call" | custom-call | tf_op jit(solution)/shard_map/attention_backward/pallas_call | solution.py:680
  496.8 17.5 %attention_backward.5 = (bf16[2048,768]{1,0:T(8,128)(2,1)}, f32[1,256]{1,0:T(1,128)S(1)}, bf16[512,1024]{1,0:T(8,128)(2,1)S(1)}, bf16[512,1024]{1,0:T(8,128)(2,1)S(1)}) custom-call(s32[4]{0:T(128)S(1)} %pad_add_fusion.refs_0_, f32[1,256]{1,0:T(1,128)S(1)} %slice.239.refs_1_, ...), custom_call_target="tpu_custom_call", output_to_operand_aliasing={{0}: (5, {})} | custom-call | tf_op jit(solution)/shard_map/attention_backward/pallas_call | solution.py:680
  519.7 24.1 %collective-permute-done.64.refs_4_ = bf16[512,1024]{1,0:T(8,128)(2,1)S(1)} collective-permute-done((bf16[512,1024]{1,0:T(8,128)(2,1)S(1)}, bf16[512,1024]{1,0:T(8,128)(2,1)S(1)}, u32[]{:S(2)}, u32[]{:S(2)}) %collective-permute-start.64) | collective-permute-done | bytes 1048608 | tf_op jit(solution)/shard_map/ppermute | solution.py:58
  554.8 19.8 %mlp_backward.6 = (bf16[2048,1024]{1,0:T(8,128)(2,1)}, bf16[2048,1024]{1,0:T(8,128)(2,1)}, f32[1,1024]{1,0:T(1,128)S(1)}, f32[1,1024]{1,0:T(1,128)S(1)}, bf16[20...) custom-call(bf16[512,1024]{1,0:T(8,128)(2,1)} %copy-done.22, ...), custom_call_target="tpu_custom_call" | custom-call | tf_op jit(solution)/shard_map/mlp_backward/pallas_call | solution.py:386
  587.0 18.7 %collective-permute-done.63.refs_4_ = bf16[512,1024]{1,0:T(8,128)(2,1)S(1)} collective-permute-done((bf16[512,1024]{1,0:T(8,128)(2,1)S(1)}, bf16[512,1024]{1,0:T(8,128)(2,1)S(1)}, u32[]{:S(2)}, u32[]{:S(2)}) %collective-permute-start.63) | collective-permute-done | bytes 1048608 | tf_op jit(solution)/shard_map/ppermute | solution.py:58
  616.9 20.1 %mlp_backward.7 = (bf16[2048,1024]{1,0:T(8,128)(2,1)}, bf16[2048,1024]{1,0:T(8,128)(2,1)}, f32[1,1024]{1,0:T(1,128)S(1)}, f32[1,1024]{1,0:T(1,128)S(1)}, bf16[20...) custom-call(bf16[512,1024]{1,0:T(8,128)(2,1)} %copy-done.11, ...), custom_call_target="tpu_custom_call", output_to_operand_aliasing={{0}: (10, {}), {1}: (11, {}), {4}: (12, {})} | custom-call | tf_op jit(solution)/shard_map/mlp_backward/pallas_call | solution.py:386
  652.0 17.4 %attention_backward.6 = (bf16[2048,768]{1,0:T(8,128)(2,1)}, f32[1,256]{1,0:T(1,128)S(1)}, bf16[512,1024]{1,0:T(8,128)(2,1)S(1)}, bf16[512,1024]{1,0:T(8,128)(2,1)S(1)}) custom-call(s32[4]{0:T(128)S(1)} %pad_add_fusion.refs_0_, f32[1,256]{1,0:T(1,128)S(1)} %slice.239.refs_1_, bf16[1024,1024]{1,0:T(8,128)(2,1)} %assemble.4.refs_3_.refs_2_, ...), custom_call_target="tpu_custom_call" | custom-call | tf_op jit(solution)/shard_map/attention_backward/pallas_call | solution.py:680
  726.9 17.4 %attention_backward.7 = (bf16[2048,768]{1,0:T(8,128)(2,1)}, f32[1,256]{1,0:T(1,128)S(1)}, bf16[512,1024]{1,0:T(8,128)(2,1)S(1)}, bf16[512,1024]{1,0:T(8,128)(2,1)S(1)}) custom-call(s32[4]{0:T(128)S(1)} %pad_add_fusion.refs_0_, f32[1,256]{1,0:T(1,128)S(1)} %slice.239.refs_1_, ...), custom_call_target="tpu_custom_call", output_to_operand_aliasing={{0}: (5, {})} | custom-call | tf_op jit(solution)/shard_map/attention_backward/pallas_call | solution.py:680
  748.5 21.1 %collective-permute-done.80 = bf16[512,1024]{1,0:T(8,128)(2,1)} collective-permute-done((bf16[512,1024]{1,0:T(8,128)(2,1)S(1)}, bf16[512,1024]{1,0:T(8,128)(2,1)}, u32[]{:S(2)}, u32[]{:S(2)}) %collective-permute-start.80) | collective-permute-done | bytes 1048608 | tf_op jit(solution)/shard_map/ppermute | solution.py:58
  784.6 24.0 %collective-permute-done.81 = bf16[512,1024]{1,0:T(8,128)(2,1)S(1)} collective-permute-done((bf16[512,1024]{1,0:T(8,128)(2,1)S(1)}, bf16[512,1024]{1,0:T(8,128)(2,1)S(1)}, u32[]{:S(2)}, u32[]{:S(2)}) %collective-permute-start.81) | collective-permute-done | bytes 1048608 | tf_op jit(solution)/shard_map/ppermute | solution.py:58
  808.6 19.1 %collective-permute-done.82 = bf16[512,1024]{1,0:T(8,128)(2,1)S(1)} collective-permute-done((bf16[512,1024]{1,0:T(8,128)(2,1)S(1)}, bf16[512,1024]{1,0:T(8,128)(2,1)S(1)}, u32[]{:S(2)}, u32[]{:S(2)}) %collective-permute-start.82) | collective-permute-done | bytes 1048608 | tf_op jit(solution)/shard_map/ppermute | solution.py:58
  842.0 15.1 %collective-permute-done.86.refs_1_ = bf16[512,1024]{1,0:T(8,128)(2,1)S(1)} collective-permute-done((bf16[512,1024]{1,0:T(8,128)(2,1)S(1)}, bf16[512,1024]{1,0:T(8,128)(2,1)S(1)}, u32[]{:S(2)}, u32[]{:S(2)}) %collective-permute-start.86) | collective-permute-done | bytes 1048608 | tf_op jit(solution)/shard_map/ppermute | solution.py:58
  857.1 15.5 %collective-permute-done.87.refs_1_ = bf16[512,1024]{1,0:T(8,128)(2,1)S(1)} collective-permute-done((bf16[512,1024]{1,0:T(8,128)(2,1)S(1)}, bf16[512,1024]{1,0:T(8,128)(2,1)S(1)}, u32[]{:S(2)}, u32[]{:S(2)}) %collective-permute-start.87) | collective-permute-done | bytes 1048608 | tf_op jit(solution)/shard_map/ppermute | solution.py:58
  917.0 25.4 %collective-permute-done.97 = bf16[512,1024]{1,0:T(8,128)(2,1)S(1)} collective-permute-done((bf16[512,1024]{1,0:T(8,128)(2,1)S(1)}, bf16[512,1024]{1,0:T(8,128)(2,1)S(1)}, u32[]{:S(2)}, u32[]{:S(2)}) %collective-permute-start.97) | collective-permute-done | bytes 1048608 | tf_op jit(solution)/shard_map/ppermute | solution.py:58
  943.8 13.9 %collective-permute-start.100 = (bf16[512,1024]{1,0:T(8,128)(2,1)S(1)}, bf16[512,1024]{1,0:T(8,128)(2,1)}, u32[]{:S(2)}, u32[]{:S(2)}) collective-permute-start(bf16[512,1024]{1,0:T(8,128)(2,1)S(1)} %add_convert_fusion.2.refs_0_), channel_id=1, source_target_pairs={{0,1},{2,3},{4,5},{6,7},{9,8},{11,10},{13,12},{15,14},{16,17},{18,... | collective-permute-start | bytes 3145736 | tf_op jit(solution)/shard_map/ppermute | solution.py:58
  (573 shorter events, 548.9 us)
Async XLA Ops:
  33.0 35.4 %collective-permute-start.3 = (bf16[256,1024]{1,0:T(8,128)(2,1)S(1)}, bf16[256,1024]{1,0:T(8,128)(2,1)S(1)}, u32[]{:S(2)}, u32[]{:S(2)}) collective-permute-start(bf16[256,1024]{1,0:T(8,128)(2,1)S(1)} %broadcast_select_fusion.1), channel_id=1, source_target_pairs={{0,4},{1,5},{2,6},{3,7},{4,0},{5,1},{6,2},{7,3},{8,12},{9,13},{10,... | collective-permute-start | bytes 1572872 | tf_op jit(solution)/shard_map/ppermute | solution.py:58
  56.8 32.6 %collective-permute-start.8 = (bf16[512,1024]{1,0:T(8,128)(2,1)}, bf16[512,1024]{1,0:T(8,128)(2,1)}, u32[]{:S(2)}, u32[]{:S(2)}) collective-permute-start(bf16[512,1024]{1,0:T(8,128)(2,1)} %dynamic-slice_bitcast_fusion.2), channel_id=1, source_target_pairs={{0,8},{2,10},{4,12},{6,14},{9,1},{11,3},{13,5},{15,7},{16,24},{18,... | collective-permute-start | bytes 3145736 | tf_op jit(solution)/shard_map/ppermute | solution.py:58
  103.2 45.9 %collective-permute-start.13 = (bf16[512,1024]{1,0:T(8,128)(2,1)S(1)}, bf16[512,1024]{1,0:T(8,128)(2,1)S(1)}, u32[]{:S(2)}, u32[]{:S(2)}) collective-permute-start(bf16[512,1024]{1,0:T(8,128)(2,1)S(1)} %add_convert_fusion.25.refs_2_), channel_id=1, source_target_pairs={{0,4},{1,5},{2,6},{3,7},{4,0},{5,1},{6,2},{7,3},{8,12},{9,13},{10,... | collective-permute-start | bytes 3145736 | tf_op jit(solution)/shard_map/ppermute | solution.py:58
  103.3 45.9 %collective-permute-start.14 = (bf16[512,1024]{1,0:T(8,128)(2,1)S(1)}, bf16[512,1024]{1,0:T(8,128)(2,1)S(1)}, u32[]{:S(2)}, u32[]{:S(2)}) collective-permute-start(bf16[512,1024]{1,0:T(8,128)(2,1)S(1)} %copy-done.96), channel_id=1, source_target_pairs={{0,8},{2,10},{4,12},{6,14},{9,1},{11,3},{13,5},{15,7},{16,24},{18,... | collective-permute-start | bytes 3145736 | tf_op jit(solution)/shard_map/ppermute | solution.py:58
  108.6 40.5 %collective-permute-start.15 = (bf16[512,1024]{1,0:T(8,128)(2,1)}, bf16[512,1024]{1,0:T(8,128)(2,1)S(1)}, u32[]{:S(2)}, u32[]{:S(2)}) collective-permute-start(bf16[512,1024]{1,0:T(8,128)(2,1)} %collective-permute-done.8.refs_0_), channel_id=1, source_target_pairs={{1,3},{3,1},{5,7},{7,5},{8,10},{10,8},{12,14},{14,12},{17,19},{19,... | collective-permute-start | bytes 3145736 | tf_op jit(solution)/shard_map/ppermute | solution.py:58
  167.2 37.1 %collective-permute-start.22 = (bf16[512,1024]{1,0:T(8,128)(2,1)S(1)}, bf16[512,1024]{1,0:T(8,128)(2,1)S(1)}, u32[]{:S(2)}, u32[]{:S(2)}) collective-permute-start(bf16[512,1024]{1,0:T(8,128)(2,1)S(1)} %add_convert_fusion.24.refs_2_), channel_id=1, source_target_pairs={{0,4},{1,5},{2,6},{3,7},{4,0},{5,1},{6,2},{7,3},{8,12},{9,13},{10,... | collective-permute-start | bytes 3145736 | tf_op jit(solution)/shard_map/ppermute | solution.py:58
  387.8 29.0 %collective-permute-start.46 = (bf16[512,1024]{1,0:T(8,128)(2,1)S(1)}, bf16[512,1024]{1,0:T(8,128)(2,1)}, u32[]{:S(2)}, u32[]{:S(2)}) collective-permute-start(bf16[512,1024]{1,0:T(8,128)(2,1)S(1)} %add_convert_fusion.18.refs_2_), channel_id=1, source_target_pairs={{0,4},{1,5},{2,6},{3,7},{4,0},{5,1},{6,2},{7,3},{8,12},{9,13},{10,... | collective-permute-start | bytes 3145736 | tf_op jit(solution)/shard_map/ppermute | solution.py:58
  419.9 29.8 %collective-permute-start.52 = (bf16[512,1024]{1,0:T(8,128)(2,1)S(1)}, bf16[512,1024]{1,0:T(8,128)(2,1)}, u32[]{:S(2)}, u32[]{:S(2)}) collective-permute-start(bf16[512,1024]{1,0:T(8,128)(2,1)S(1)} %add_convert_fusion.17.refs_5_), channel_id=1, source_target_pairs={{0,4},{1,5},{2,6},{3,7},{4,0},{5,1},{6,2},{7,3},{8,12},{9,13},{10,... | collective-permute-start | bytes 3145736 | tf_op jit(solution)/shard_map/ppermute | solution.py:58
  452.9 28.3 %collective-permute-start.56 = (bf16[512,1024]{1,0:T(8,128)(2,1)S(1)}, bf16[512,1024]{1,0:T(8,128)(2,1)S(1)}, u32[]{:S(2)}, u32[]{:S(2)}) collective-permute-start(bf16[512,1024]{1,0:T(8,128)(2,1)S(1)} %add_convert_fusion.16.refs_5_), channel_id=1, source_target_pairs={{0,4},{1,5},{2,6},{3,7},{4,0},{5,1},{6,2},{7,3},{8,12},{9,13},{10,... | collective-permute-start | bytes 3145736 | tf_op jit(solution)/shard_map/ppermute | solution.py:58
  484.3 30.0 %collective-permute-start.60 = (bf16[512,1024]{1,0:T(8,128)(2,1)S(1)}, bf16[512,1024]{1,0:T(8,128)(2,1)S(1)}, u32[]{:S(2)}, u32[]{:S(2)}) collective-permute-start(bf16[512,1024]{1,0:T(8,128)(2,1)S(1)} %add_convert_fusion.15), channel_id=1, source_target_pairs={{0,4},{1,5},{2,6},{3,7},{4,0},{5,1},{6,2},{7,3},{8,12},{9,13},{10,... | collective-permute-start | bytes 3145736 | tf_op jit(solution)/shard_map/ppermute | solution.py:58
  519.4 55.2 %collective-permute-start.62 = (bf16[512,1024]{1,0:T(8,128)(2,1)}, bf16[512,1024]{1,0:T(8,128)(2,1)}, u32[]{:S(2)}, u32[]{:S(2)}) collective-permute-start(bf16[512,1024]{1,0:T(8,128)(2,1)} %add_convert_fusion.14), channel_id=1, source_target_pairs={{0,4},{1,5},{2,6},{3,7},{4,0},{5,1},{6,2},{7,3},{8,12},{9,13},{10,... | collective-permute-start | bytes 3145736 | tf_op jit(solution)/shard_map/ppermute | solution.py:58
  605.8 31.2 %collective-permute-start.70 = (bf16[512,1024]{1,0:T(8,128)(2,1)S(1)}, bf16[512,1024]{1,0:T(8,128)(2,1)S(1)}, u32[]{:S(2)}, u32[]{:S(2)}) collective-permute-start(bf16[512,1024]{1,0:T(8,128)(2,1)S(1)} %add_convert_fusion.11.refs_5_), channel_id=1, source_target_pairs={{0,4},{1,5},{2,6},{3,7},{4,0},{5,1},{6,2},{7,3},{8,12},{9,13},{10,... | collective-permute-start | bytes 3145736 | tf_op jit(solution)/shard_map/ppermute | solution.py:58
  722.4 47.1 %collective-permute-start.80 = (bf16[512,1024]{1,0:T(8,128)(2,1)S(1)}, bf16[512,1024]{1,0:T(8,128)(2,1)}, u32[]{:S(2)}, u32[]{:S(2)}) collective-permute-start(bf16[512,1024]{1,0:T(8,128)(2,1)S(1)} %copy-done.99), channel_id=1, source_target_pairs={{0,2},{1,3},{2,0},{3,1},{4,6},{5,7},{6,4},{7,5},{8,10},{9,11},{10,... | collective-permute-start | bytes 3145736 | tf_op jit(solution)/shard_map/ppermute | solution.py:58
  774.6 34.0 %collective-permute-start.81 = (bf16[512,1024]{1,0:T(8,128)(2,1)S(1)}, bf16[512,1024]{1,0:T(8,128)(2,1)S(1)}, u32[]{:S(2)}, u32[]{:S(2)}) collective-permute-start(bf16[512,1024]{1,0:T(8,128)(2,1)S(1)} %add_convert_fusion.8), channel_id=1, source_target_pairs={{1,9},{3,11},{5,13},{7,15},{8,0},{10,2},{12,4},{14,6},{17,25},{19,... | collective-permute-start | bytes 3145736 | tf_op jit(solution)/shard_map/ppermute | solution.py:58
  775.9 51.8 %collective-permute-start.82 = (bf16[512,1024]{1,0:T(8,128)(2,1)S(1)}, bf16[512,1024]{1,0:T(8,128)(2,1)S(1)}, u32[]{:S(2)}, u32[]{:S(2)}) collective-permute-start(bf16[512,1024]{1,0:T(8,128)(2,1)S(1)} %add_convert_fusion.7), channel_id=1, source_target_pairs={{1,9},{3,11},{5,13},{7,15},{8,0},{10,2},{12,4},{14,6},{17,25},{19,... | collective-permute-start | bytes 3145736 | tf_op jit(solution)/shard_map/ppermute | solution.py:58
  777.2 50.5 %collective-permute-start.83 = (bf16[512,1024]{1,0:T(8,128)(2,1)S(1)}, bf16[512,1024]{1,0:T(8,128)(2,1)S(1)}, u32[]{:S(2)}, u32[]{:S(2)}) collective-permute-start(bf16[512,1024]{1,0:T(8,128)(2,1)S(1)} %copy-done.97), channel_id=1, source_target_pairs={{0,2},{1,3},{2,0},{3,1},{4,6},{5,7},{6,4},{7,5},{8,10},{9,11},{10,... | collective-permute-start | bytes 3145736 | tf_op jit(solution)/shard_map/ppermute | solution.py:58
  778.6 52.4 %collective-permute-start.85 = (bf16[512,1024]{1,0:T(8,128)(2,1)S(1)}, bf16[512,1024]{1,0:T(8,128)(2,1)S(1)}, u32[]{:S(2)}, u32[]{:S(2)}) collective-permute-start(bf16[512,1024]{1,0:T(8,128)(2,1)S(1)} %add_convert_fusion.3), channel_id=1, source_target_pairs={{0,4},{1,5},{2,6},{3,7},{4,0},{5,1},{6,2},{7,3},{8,12},{9,13},{10,... | collective-permute-start | bytes 3145736 | tf_op jit(solution)/shard_map/ppermute | solution.py:58
  835.9 36.6 %collective-permute-start.87 = (bf16[512,1024]{1,0:T(8,128)(2,1)S(1)}, bf16[512,1024]{1,0:T(8,128)(2,1)S(1)}, u32[]{:S(2)}, u32[]{:S(2)}) collective-permute-start(bf16[512,1024]{1,0:T(8,128)(2,1)S(1)} %get-tuple-element.623.refs_0_), channel_id=1, source_target_pairs={{0,2},{2,0},{4,6},{6,4},{9,11},{11,9},{13,15},{15,13},{16,18},{18,... | collective-permute-start | bytes 3145736 | tf_op jit(solution)/shard_map/ppermute | solution.py:58
  839.3 39.8 %collective-permute-start.88 = (bf16[512,1024]{1,0:T(8,128)(2,1)S(1)}, bf16[512,1024]{1,0:T(8,128)(2,1)S(1)}, u32[]{:S(2)}, u32[]{:S(2)}) collective-permute-start(bf16[512,1024]{1,0:T(8,128)(2,1)S(1)} %get-tuple-element.612), channel_id=1, source_target_pairs={{1,9},{3,11},{5,13},{7,15},{8,0},{10,2},{12,4},{14,6},{17,25},{19,... | collective-permute-start | bytes 3145736 | tf_op jit(solution)/shard_map/ppermute | solution.py:58
  840.6 43.2 %collective-permute-start.89 = (bf16[512,1024]{1,0:T(8,128)(2,1)S(1)}, bf16[512,1024]{1,0:T(8,128)(2,1)S(1)}, u32[]{:S(2)}, u32[]{:S(2)}) collective-permute-start(bf16[512,1024]{1,0:T(8,128)(2,1)S(1)} %constant_dynamic-slice_fusion), channel_id=1, source_target_pairs={{0,2},{1,3},{2,0},{3,1},{4,6},{5,7},{6,4},{7,5},{8,10},{9,11},{10,... | collective-permute-start | bytes 3145736 | tf_op jit(solution)/shard_map/ppermute | solution.py:58
  841.2 42.6 %collective-permute-start.91 = (bf16[2,256,1024]{2,1,0:T(8,128)(2,1)S(1)}, bf16[2,256,1024]{2,1,0:T(8,128)(2,1)S(1)}, u32[]{:S(2)}, u32[]{:S(2)}) collective-permute-start(bf16[2,256,1024]{2,1,0:T(8,128)(2,1)S(1)} %get-tuple-element.615), channel_id=1, source_target_pairs={{1,8},{3,10},{5,12},{7,14},{8,1},{10,3},{12,5},{14,7},{17,24},{19,... | collective-permute-start | bytes 3145736 | tf_op jit(solution)/shard_map/ppermute | solution.py:58
  903.7 38.7 %collective-permute-start.97 = (bf16[512,1024]{1,0:T(8,128)(2,1)S(1)}, bf16[512,1024]{1,0:T(8,128)(2,1)S(1)}, u32[]{:S(2)}, u32[]{:S(2)}) collective-permute-start(bf16[512,1024]{1,0:T(8,128)(2,1)S(1)} %add_convert_fusion.1), channel_id=1, source_target_pairs={{1,9},{3,11},{5,13},{7,15},{8,0},{10,2},{12,4},{14,6},{17,25},{19,... | collective-permute-start | bytes 3145736 | tf_op jit(solution)/shard_map/ppermute | solution.py:58
  905.0 37.4 %collective-permute-start.99 = (bf16[2,256,1024]{2,1,0:T(8,128)(2,1)S(1)}, bf16[2,256,1024]{2,1,0:T(8,128)(2,1)S(1)}, u32[]{:S(2)}, u32[]{:S(2)}) collective-permute-start(bf16[2,256,1024]{2,1,0:T(8,128)(2,1)S(1)} %get-tuple-element.628), channel_id=1, source_target_pairs={{1,8},{3,10},{5,12},{7,14},{8,1},{10,3},{12,5},{14,7},{17,24},{19,... | collective-permute-start | bytes 3145736 | tf_op jit(solution)/shard_map/ppermute | solution.py:58
  943.8 33.4 %collective-permute-start.100 = (bf16[512,1024]{1,0:T(8,128)(2,1)S(1)}, bf16[512,1024]{1,0:T(8,128)(2,1)}, u32[]{:S(2)}, u32[]{:S(2)}) collective-permute-start(bf16[512,1024]{1,0:T(8,128)(2,1)S(1)} %add_convert_fusion.2.refs_0_), channel_id=1, source_target_pairs={{0,1},{2,3},{4,5},{6,7},{9,8},{11,10},{13,12},{15,14},{16,17},{18,... | collective-permute-start | bytes 3145736 | tf_op jit(solution)/shard_map/ppermute | solution.py:58
  (194 other events, 2414.7 us)

commit v2 on v1

--- a/solution.py
+++ b/solution.py
@@ -12,7 +12,8 @@
 AXES = ("section", "tensor", "dp")
 F32 = jnp.float32
 LOW = jnp.bfloat16
-VMEM_LIMIT = 50 * 1024 * 1024
+VMEM_LIMIT = 24 * 1024 * 1024
+BAND = 256
 
 
 def cost(flops, bytes_accessed, transcendentals):
@@ -147,26 +148,38 @@
     return jnp.mean(values, axis=-1, keepdims=True)
 
 
-def load_terms(refs, swaps, lanes):
+def row_specs(lanes, rows, width):
+    part = rows // lanes
+    size = min(128, part)
+    per = part // size
+
+    def spec_of(bit):
+        if bit == 0:
+            return pl.BlockSpec((size, width), lambda i: (i, 0))
+        return pl.BlockSpec(
+            (size, width), lambda i: (((i // per) ^ bit) * per + lax.rem(i, per), 0)
+        )
+
+    return rows // size, size, spec_of
+
+
+def load_terms(refs):
     total = refs[0][...].astype(F32)
-    for ref, bit in zip(refs[1:], swaps[1:]):
-        part = ref.shape[0] // lanes
-        order = [ref[(at ^ bit) * part : ((at ^ bit) + 1) * part, :] for at in range(lanes)]
-        value = order[0] if lanes == 1 else jnp.concatenate(order, axis=0)
-        total = total + value.astype(F32)
+    for ref in refs[1:]:
+        total = total + ref[...].astype(F32)
     return total
 
 
 def blend_forward(lanes, hidden, branch, rate, out_dtypes):
     rows, width = hidden.shape
     branch, swaps = zip(*branch)
+    steps, size, spec_of = row_specs(lanes, rows, width)
 
     def kernel(*refs):
         hidden_ref, rate_ref = refs[:2]
-        branch_refs = refs[2 : 2 + len(branch)]
         out_refs = refs[2 + len(branch) :]
         h = hidden_ref[...].astype(F32)
-        b = load_terms(branch_refs, swaps, lanes)
+        b = load_terms(refs[2 : 2 + len(branch)])
         mixed = b * lax.rsqrt(mean_of(b * b) + EPS)
         u = h + rate_ref[...] * (mixed - h)
         y = u * lax.rsqrt(mean_of(u * u) + EPS)
@@ -175,9 +188,11 @@
 
     return pl.pallas_call(
         kernel,
+        grid=(steps,),
         out_shape=[jax.ShapeDtypeStruct((rows, width), kind) for kind in out_dtypes],
-        in_specs=spec(2 + len(branch)),
-        out_specs=spec(len(out_dtypes)),
+        in_specs=[spec_of(0), pl.BlockSpec((1, width), lambda i: (0, 0))]
+        + [spec_of(bit) for bit in swaps],
+        out_specs=[spec_of(0)] * len(out_dtypes),
         compiler_params=pltpu.CompilerParams(vmem_limit_bytes=VMEM_LIMIT),
         cost_estimate=cost(
             flops=12 * rows * width, bytes_accessed=10 * rows * width, transcendentals=0
@@ -191,13 +206,14 @@
     branch, branch_swaps = zip(*branch)
     grads, grad_swaps = zip(*grads)
     branches = len(branch)
+    steps, size, spec_of = row_specs(lanes, rows, width)
 
     def kernel(*refs):
         hidden_ref, rate_ref = refs[:2]
         hidden_out, branch_out, rate_out = refs[-3:]
         h = hidden_ref[...].astype(F32)
-        b = load_terms(refs[2 : 2 + branches], branch_swaps, lanes)
-        g = load_terms(refs[2 + branches : -3], grad_swaps, lanes)
+        b = load_terms(refs[2 : 2 + branches])
+        g = load_terms(refs[2 + branches : -3])
         a = rate_ref[...]
         root_b = lax.rsqrt(mean_of(b * b) + EPS)
         delta = b * root_b - h
@@ -206,22 +222,35 @@
         grad_u = root_u * g - u * (root_u * root_u * root_u * mean_of(u * g))
         grad_mixed = grad_u * a
         hidden_out[...] = grad_u - grad_mixed
-        rate_out[...] = jnp.sum(grad_u * delta, axis=0, keepdims=True)
+        rate_sum = jnp.sum(grad_u * delta, axis=0, keepdims=True)
+
+        @pl.when(pl.program_id(0) == 0)
+        def _():
+            rate_out[...] = rate_sum
+
+        @pl.when(pl.program_id(0) > 0)
+        def _():
+            rate_out[...] += rate_sum
+
         grad_b = root_b * grad_mixed - b * (
             root_b * root_b * root_b * mean_of(b * grad_mixed)
         )
         branch_out[...] = grad_b.astype(branch_out.dtype)
 
+    one_row = pl.BlockSpec((1, width), lambda i: (0, 0))
     return pl.pallas_call(
         kernel,
+        grid=(steps,),
         out_shape=[
             jax.ShapeDtypeStruct((rows, width), F32),
             jax.ShapeDtypeStruct((rows, width), LOW),
             jax.ShapeDtypeStruct((1, width), F32),
         ],
-        in_specs=spec(2 + branches + len(grads)),
-        out_specs=spec(3),
-        compiler_params=pltpu.CompilerParams(vmem_limit_bytes=VMEM_LIMIT),
+        in_specs=[spec_of(0), one_row] + [spec_of(bit) for bit in branch_swaps + grad_swaps],
+        out_specs=[spec_of(0), spec_of(0), one_row],
+        compiler_params=pltpu.CompilerParams(
+            vmem_limit_bytes=VMEM_LIMIT, dimension_semantics=("arbitrary",)
+        ),
         cost_estimate=cost(
             flops=30 * rows * width, bytes_accessed=20 * rows * width, transcendentals=0
         ),
@@ -351,27 +380,34 @@
 
         values = [keep_ref if at_x == 0 and keep_ref is not None else members[0]
                   for at_x, members in enumerate(x_refs)]
-        dots = [
-            (nt_dot if flipped else nn_dot)(values[which][...], ref[...])
-            for (which, _, flipped, *_), ref in zip(used, weight_refs)
-        ]
-        results, terms = epilogue(dots, [ref[...] for ref in tiled_refs])
-        for ref, result in zip(out_refs, results):
-            ref[...] = result.astype(ref.dtype)
+        sums = [None] * len(outs)
+        band = min(BAND, rows)
+        for begin in range(0, rows, band):
+            here = slice(begin, begin + band)
+            dots = [
+                (nt_dot if flipped else nn_dot)(values[which][here, :], ref[...])
+                for (which, _, flipped, *_), ref in zip(used, weight_refs)
+            ]
+            results, terms = epilogue(
+                dots, [ref[here, :] if ref.shape[0] == rows else ref[...] for ref in tiled_refs]
+            )
+            for at_out, (ref, result) in enumerate(zip(out_refs, results)):
+                if ref.shape[0] == rows:
+                    ref[here, :] = result.astype(ref.dtype)
+                else:
+                    former = sums[at_out]
+                    sums[at_out] = result if former is None else former + result
+            if total:
+                sum_ref = refs[0]
+                term = None
+                for (_, flipped), ref, value in zip(total_weights, total_refs, terms):
+                    product = (nt_dot if flipped else nn_dot)(value, ref[...])
+                    term = product if term is None else term + product
+                sum_ref[here, :] = jnp.where(step == 0, 0.0, sum_ref[here, :]) + term
+        for ref, result in zip(out_refs, sums):
+            if result is not None:
+                ref[...] = result.astype(ref.dtype)
         if total:
-            sum_ref = refs[0]
-            term = None
-            for (_, flipped), ref, value in zip(total_weights, total_refs, terms):
-                product = (nt_dot if flipped else nn_dot)(value, ref[...])
-                term = product if term is None else term + product
-
-            @pl.when(step == 0)
-            def _():
-                sum_ref[...] = term
-
-            @pl.when(step > 0)
-            def _():
-                sum_ref[...] += term
 
             @pl.when(step == steps - 1)
             def _():
@@ -424,6 +460,10 @@
     return results[0]
 
 
+def sigmoid_of(values):
+    return 0.5 + 0.5 * jnp.tanh(0.5 * values)
+
+
 def mlp_forward(pieces, weights, scales, at, count, stacks):
     up_w, gate_w, down_w = weights
     rows = sum(piece.shape[0] for piece in pieces)
@@ -432,7 +472,7 @@
         up_raw, gate_raw = dots
         up_scale, gate_scale = tiles
         gated = gate_raw * gate_scale
-        inner = (gated / (1.0 + jnp.exp(-gated)) * (up_raw * up_scale)).astype(LOW)
+        inner = (gated * sigmoid_of(gated) * (up_raw * up_scale)).astype(LOW)
         return [up_raw, gate_raw, inner], [inner]
 
     mid, up_raw, gate_raw, inner = stacks
@@ -461,7 +501,7 @@
         up_raw, gate_raw = up_raw.astype(F32), gate_raw.astype(F32)
         grad = dots[0]
         gated = gate_raw * gate_scale
-        sigmoid = 1.0 / (1.0 + jnp.exp(-gated))
+        sigmoid = sigmoid_of(gated)
         silu = gated * sigmoid
         slope = sigmoid * (1.0 + gated * (1.0 - sigmoid))
         from_up = grad * silu
@@ -799,13 +839,13 @@
     return (left.astype(F32) + right.astype(F32)).astype(LOW)
 
 
-def collect_task(place, grad, store):
+def collect_task(place, grad, store, steps):
     held = grad
     for bit in place.pair_bits[::-1]:
         kept, sent = halved(held, (place.pair // bit) % 2, held.shape[0])
-        (met,) = yield [(sent, to_pair(bit))]
+        (met,) = yield [(sent, to_pair(bit))], steps[0]
         held = plus(kept, met)
-    (met,) = yield [(held, only(to_half, lambda s, h, c: c != h))]
+    (met,) = yield [(held, only(to_half, lambda s, h, c: c != h))], steps[1]
     held = plus(held, met)
     parts = [held]
     for bit in place.pair_bits:
@@ -908,14 +948,17 @@
         self.place, self.bg = place, bg
         self.last = None
         self.ready = None
+        self.beside = []
 
     def exchange(self, mine, theirs, starts=None):
-        if self.last:
-            flying = [value for value, _ in self.last]
-            theirs, flying = lax.optimization_barrier((theirs, flying))
-            self.last[:] = [(value, bit) for value, (_, bit) in zip(flying, self.last)]
         if starts is not None:
             theirs = self.bg.step(theirs, starts)
+        last = self.last or []
+        flying = [value for value, _ in last]
+        theirs, flying, beside = lax.optimization_barrier((theirs, flying, self.beside))
+        last[:] = [(value, bit) for value, (_, bit) in zip(flying, last)]
+        self.beside[:] = beside
+        self.beside = []
         self.ready = plus(mine, self.place.across_cores(theirs))
         self.last = []
         return self.last
@@ -937,21 +980,23 @@
 def layer_forward(place, places, bg, chain, rows, weights, scales, late=None):
     qk_scale, attn_rate, up_scale, gate_scale, mlp_rate = scales
     width = qk_scale.shape[1]
-    count = late[1] if late else len(rows)
-    streams = range(count)
     lanes = place.lanes
     full_in, attended, raws, attn_terms = [], [], [], []
+    pieces = weights.wait(("attn",), chain.after(gather(place, rows[0])))
+    if late:
+        rows = rows + late()
+        chain.beside = rows[1:]
+    count = len(rows)
+    streams = range(count)
     for at in streams:
-        if at == len(rows):
-            rows.append(gather_lanes(place, chain.after(late[0][at])))
-        pieces = chain.after(gather(place, rows[at]))
-        pieces = weights.wait(("attn",), pieces)
+        if at > 0:
+            pieces = chain.after(gather(place, rows[at]))
         raws.append(project(pieces, weights["attn"], width, at, count, full_in))
         mine, theirs = attention_forward(
             places, qk_scale, raws[at], weights["out"], at, count, attended
         )
         attn_terms.append(chain.exchange(mine, theirs, 1))
-    middles, mlp_terms, results = [], [], []
+    middles, mlp_terms = [], []
     stacks = [[], [], [], []]
     for at in streams:
         terms = chain.terms_after(attn_terms[at])
@@ -967,17 +1012,18 @@
             stacks,
         )
         mlp_terms.append(chain.exchange(mine, theirs))
-    for at in streams:
-        results.append(
-            blend_forward(
-                lanes, middles[at][0], chain.terms_after(mlp_terms[at]), mlp_rate, [LOW]
-            )[0]
-        )
+
+    def result(at, after=()):
+        terms = chain.terms_after(mlp_terms[at])
+        middle = middles[at][0]
+        middle, after = lax.optimization_barrier((middle, after))
+        return blend_forward(lanes, middle, terms, mlp_rate, [LOW])[0]
+
     kept = (rows, full_in[-1], raws, attended[-1], attn_terms, middles, stacks, mlp_terms)
-    return results, kept
-
-
-def layer_backward(place, places, chain, grads, kept, weights, scales, collect, starts):
+    return result, kept
+
+
+def layer_backward(place, places, bg, chain, grads, kept, weights, scales, collect, starts):
     rows, full_in, raws, attended, attn_terms, middles, stacks, mlp_terms = kept
     full_mid, up_raw, gate_raw, inner = (stack[-1] for stack in stacks)
     qk_scale, attn_rate, up_scale, gate_scale, mlp_rate = scales
@@ -1003,29 +1049,26 @@
             back_stacks,
         )
         sums.append((up_sum, gate_sum))
-        mid_terms.append(chain.exchange(mine, theirs, starts[at]))
+        mid_terms.append(chain.exchange(mine, theirs, starts["mlp"][at]))
     full_mlp, up_back, gate_back = chain.after([stack[-1] for stack in back_stacks])
-    collect("down", tn_dot(inner, full_mlp).astype(LOW))
-    collect("up", tn_dot(full_mid, up_back).astype(LOW))
-    collect("gate", tn_dot(full_mid, gate_back).astype(LOW))
+    collect("down", [(inner, full_mlp)])
+    collect("up", [(full_mid, up_back)])
+    collect("gate", [(full_mid, gate_back)])
     attn_back, full_attn, back, in_terms, qk_sums = [], [], [], [], []
     for at in streams:
         terms = chain.terms_after([(mlp_back[at][0], 0)] + mid_terms[at])
         attn_back.append(blend_backward(lanes, rows[at], attn_terms[at], attn_rate, terms))
         pieces = gather(place, attn_back[at][1])
+        if starts["attention"][at] is not None:
+            pieces = bg.step(pieces, starts["attention"][at])
         grad_attended = output_backward(pieces, weights["out"], at, count, full_attn)
         qk_sum, mine, theirs = attention_backward(
             places, qk_scale, raws[at], grad_attended, weights["attn"], at, count, back
         )
         qk_sums.append(qk_sum)
-        in_terms.append(chain.exchange(mine, theirs, starts[count + at]))
+        in_terms.append(chain.exchange(mine, theirs, starts["end"][at]))
     last = chain.after(back[-1])
-    collect(
-        "attn",
-        jnp.concatenate(
-            [tn_dot(full_in, last), tn_dot(full_attn[-1], attended)], axis=1
-        ).astype(LOW),
-    )
+    collect("attn", [(full_in, last), (full_attn[-1], attended)])
     small = jnp.concatenate(
         [sum(qk_sums), sum(member[0] for member in sums), sum(member[1] for member in sums)],
         axis=1,
@@ -1076,13 +1119,18 @@
     bg.add(move_task(place, start[0], transposed, start_rows))
     bg.add(move_task(place, small_in, only(to_half, lambda s, h, c: c == h), small_rows))
     bg.add(spread_task(place, "attn", shards["attn"], 1, ready))
+    bg.step((), 3)
     for member in start[1:]:
-        bg.add(move_task(place, member, transposed, start_rows, 2))
+        bg.add(move_task(place, member, transposed, start_rows))
     for name in ("up", "gate", "down"):
-        bg.add(spread_task(place, name, shards[name], 2, ready))
-    bg.step((), 3)
+        bg.add(spread_task(place, name, shards[name], 1, ready))
     bg.step((), len(start))
     start = [gather_lanes(place, start_rows[0])]
+
+    def late_rows():
+        start.extend(gather_lanes(place, member) for member in start_rows[1:])
+        return start[1:]
+
     edges = [0, width, width + units, width + 2 * units]
     qk, up, gate = (small_rows[0][:, a:b] for a, b in zip(edges[:3], edges[1:]))
     scales = (qk, attn_rate, up, gate, mlp_rate)
@@ -1107,44 +1155,69 @@
             total = total + (unswapped(place, value, bit) if bit else value).astype(F32)
         return total.astype(LOW)
 
-    first_out, kept_first = layer_forward(
-        place, places, bg, chain, start, weights, scales, (start_rows, len(streams))
+    def hops(members, source):
+        arrived = [hop(member, source) for member in members]
+        arrived[0], members = lax.optimization_barrier((arrived[0], members))
+        chain.beside = arrived
+        return arrived
+
+    result, kept_first = layer_forward(
+        place, places, bg, chain, start[:1], weights, scales, late_rows
     )
-    second_in = [hop(member, 0) for member in first_out]
-    second_out, kept_second = layer_forward(place, places, bg, chain, second_in, weights, scales)
+    first_out = [result(at) for at in streams]
+    second_in = hops(first_out, 0)
+    result, kept_second = layer_forward(place, places, bg, chain, second_in, weights, scales)
     hidden_out, grad_in, sums = [], [], []
     late = {}
+    none = [None] * len(streams)
     grad_mid, second_small, second_rates = layer_backward(
         place,
         places,
+        bg,
         chain,
         [[(member, 0)] for member in start],
         kept_second,
         weights,
         scales,
         late.__setitem__,
-        [None] * (2 * len(streams)),
+        {"mlp": none, "attention": none, "end": none},
     )
+
+    def product(factors):
+        parts = [tn_dot(left, right) for left, right in factors]
+        return (parts[0] if len(parts) == 1 else jnp.concatenate(parts, axis=1)).astype(LOW)
+
     grad_second = [summed(terms) for terms in grad_mid]
-    grad_back = [hop(member, 1) for member in grad_second]
+    late, grad_second[0] = lax.optimization_barrier((late, grad_second[0]))
+    late = {name: product(factors) for name, factors in late.items()}
+    second_out = [result(at, grad_second[0]) for at in streams]
+    out_rows = jnp.where(first, own_rows(first_out), own_rows(second_out))
+    grad_back = hops(grad_second, 1)
+    grad_back[0], late, out_rows = lax.optimization_barrier((grad_back[0], late, out_rows))
     stores = {name: [] for name in shards}
 
-    def collect(name, grad):
-        mine = jnp.where(first, grad, late[name])
-        bg.add(collect_task(place, mine, stores[name]))
+    def collect(name, factors):
+        mine = jnp.where(first, product(factors), late[name])
+        bg.add(collect_task(place, mine, stores[name], (1, 1)))
+        if name == "down":
+            bg.add(move_task(place, out_rows, transposed, hidden_out))
 
     grad_start, first_small, first_rates = layer_backward(
         place,
         places,
+        bg,
         chain,
         [[(member, 0)] for member in grad_back],
         kept_first,
         weights,
         scales,
         collect,
-        [None] * len(streams) + [2] + [1] * (len(streams) - 1),
+        {
+            "mlp": none,
+            "attention": [2] + [1] * (len(streams) - 1),
+            "end": [1] + [0] * (len(streams) - 1),
+        },
     )
-    grad_first = [summed(terms) for terms in grad_start]
     bg.add(
         small_task(
             place,
@@ -1153,11 +1226,17 @@
             sums,
         )
     )
-    in_rows = jnp.where(first, own_rows(grad_first), own_rows(grad_second))
-    bg.add(move_task(place, in_rows, transposed, grad_in))
-    out_rows = jnp.where(first, own_rows(first_out), own_rows(second_out))
-    bg.add(move_task(place, out_rows, transposed, hidden_out))
-    bg.step((), 3)
+
+    def in_rows(at):
+        value = jnp.where(first, summed(grad_start[at])[:part], grad_second[at][:part])
+        return move_task(place, value, transposed, grad_in)
+
+    for at in streams[:-1]:
+        bg.add(in_rows(at))
+    bg.step((), 1 + len(streams))
+    flying = bg.step([value for value, _ in grad_start[-1]], 0)
+    grad_start[-1] = [(value, bit) for value, (_, bit) in zip(flying, grad_start[-1])]
+    bg.add(in_rows(streams[-1]))
     bg.drain()
 
     def done(name, columns):
@@ -1171,7 +1250,7 @@
     model = total.shape[1] // 2
     return (
         hidden_out[0][None, :, None],
-        grad_in[0].astype(F32)[None, :, None],
+        jnp.stack(grad_in).astype(F32)[None, :, None],
         query[None],
         key[None],
         value[None],

time: 1000 us -> 888 us (0.89)
  Pallas kernels: 360 us -> 252 us
  waiting for transfers between devices: 343 us -> 273 us
  local copies, waits for them, and re-layouts: 47.1 us -> 110 us
  other arithmetic: 27.8 us -> 42.9 us
  starting transfers between devices: 165 us -> 150 us
    ppermute x106 -> x107, waiting for transfers between devices: 343 us -> 273 us  [move(): return lax.ppermute(value, AXES, links)]
    unnamed x230 -> x369, local copies, waits for them, and re-layouts: 28.4 us -> 93.7 us
    pallas_call x16, Pallas kernels: 163 us -> 109 us  [fused_dot(): pl.pallas_call(kernel, grid=(steps,), out_shape=out_shape, in_specs=in_sp...]
    pallas_call x16, Pallas kernels: 70.8 us -> 43.1 us  [the longest x8 27.4 us: blend_backward(): pl.pallas_call(kernel, grid=(steps,), out_shape=[jax.ShapeDtypeStruct((ro...]
    ppermute x106 -> x107, starting transfers between devices: 165 us -> 150 us  [move(): return lax.ppermute(value, AXES, links)]
    pallas_call x4, Pallas kernels: 14.1 us -> 3.02 us  [assemble(): pl.pallas_call(kernel, out_shape=jax.ShapeDtypeStruct(shard.shape, shard....]
  transfers between devices with their start and end apart: 106 -> 107, of which waited for: 54 -> 59; matrix products, arithmetic and copies ran while one was open for 8% -> 9% of each run, Pallas kernels for 34% -> 28%
where the time goes in v2:
time: 888 us; the launch traced here: 878 us
  waiting for transfers between devices  273 us (31%)
  Pallas kernels  252 us (28%)
  starting transfers between devices  150 us (17%)
  local copies, waits for them, and re-layouts  110 us (12%)
  matrix products  46 us (5%)
  other arithmetic  42.9 us (5%)
    ppermute x107, waiting for transfers between devices, move(): return lax.ppermute(value, AXES, links)  273 us
    ppermute x107, starting transfers between devices, move(): return lax.ppermute(value, AXES, links)  150 us
    pallas_call x16, Pallas kernels, fused_dot(): pl.pallas_call(kernel, grid=(steps,), out_shape=out_shape, in_specs=in_sp...  109 us
    unnamed x369, local copies, waits for them, and re-layouts  93.7 us
    pallas_call x4, Pallas kernels, attention_backward(): pl.pallas_call(kernel, grid=(1,), out_shape=[jax.ShapeDtypeStruct((length...  60.8 us
    dot_general x10, matrix products, tn_dot(): lax.dot_general(left, right, (((0,), (0,)), ((), ())), preferred_element_...  46 us
    pallas_call x8, Pallas kernels, blend_backward(): pl.pallas_call(kernel, grid=(steps,), out_shape=[jax.ShapeDtypeStruct((ro...  27.4 us
    pallas_call x4, Pallas kernels, attention_forward(): pl.pallas_call(kernel, grid=(1,), out_shape=[jax.ShapeDtypeStruct((length...  23.7 us
  transfers between devices with their start and end apart: 107, of which 59 were waited for; matrix products, arithmetic and copies ran while one was open for 9% of the time, Pallas kernels for 28%

profile of v2, /device:TPU:0, one launch (start us, length us, event | category | flops | bytes accessed | tf_op | source)
XLA Modules:
  0.0 878.1 jit_solution(11365013101070215054)
XLA Ops:
  18.6 15.0 %collective-permute-done.1 = f32[1,2304]{1,0:T(1,128)S(1)} collective-permute-done((f32[1,2304]{1,0:T(1,128)S(1)}, f32[1,2304]{1,0:T(1,128)S(1)}, u32[]{:S(2)}, u32[]{:S(2)}) %collective-permute-start.1) | collective-permute-done | bytes 9248 | tf_op jit(solution)/shard_map/ppermute | solution.py:59
  35.5 18.4 %collective-permute-start.3 = (bf16[256,1024]{1,0:T(8,128)(2,1)}, bf16[256,1024]{1,0:T(8,128)(2,1)}, u32[]{:S(2)}, u32[]{:S(2)}) collective-permute-start(bf16[256,1024]{1,0:T(8,128)(2,1)} %broadcast_select_fusion.1), channel_id=1, source_target_pairs={{0,4},{1,5},{2,6},{3,7},{4,0},{5,1},{6,2},{7,3},{8,12},{9,13},{10,... | collective-permute-start | bytes 1572872 | tf_op jit(solution)/shard_map/ppermute | solution.py:59
  83.6 16.7 %collective-permute-start.13 = (bf16[512,1024]{1,0:T(8,128)(2,1)}, bf16[512,1024]{1,0:T(8,128)(2,1)}, u32[]{:S(2)}, u32[]{:S(2)}) collective-permute-start(bf16[512,1024]{1,0:T(8,128)(2,1)} %get-tuple-element.396), channel_id=1, source_target_pairs={{0,8},{2,10},{4,12},{6,14},{9,1},{11,3},{13,5},{15,7},{16,24},{18,... | collective-permute-start | bytes 3145736 | tf_op jit(solution)/shard_map/ppermute | solution.py:59
  156.7 13.4 %collective-permute-done.17.refs_3_ = bf16[512,1024]{1,0:T(8,128)(2,1)S(1)} collective-permute-done((bf16[512,1024]{1,0:T(8,128)(2,1)S(1)}, bf16[512,1024]{1,0:T(8,128)(2,1)S(1)}, u32[]{:S(2)}, u32[]{:S(2)}) %collective-permute-start.17) | collective-permute-done | bytes 1048608 | tf_op jit(solution)/shard_map/ppermute | solution.py:59
  180.4 10.8 %mlp_forward.4 = (bf16[2048,1024]{1,0:T(8,128)(2,1)S(1)}, bf16[2048,1024]{1,0:T(8,128)(2,1)S(1)}, bf16[2048,1024]{1,0:T(8,128)(2,1)S(1)}, bf16[2048,1024]{1,0:T(...) custom-call(bf16[512,1024]{1,0:T(8,128)(2,1)S(1)} %get-tuple-element.426.refs_0_, ...), custom_call_target="tpu_custom_call" | custom-call | tf_op jit(solution)/shard_map/mlp_forward/pallas_call | solution.py:422
  206.1 10.8 %mlp_forward.5 = (bf16[2048,1024]{1,0:T(8,128)(2,1)S(1)}, bf16[2048,1024]{1,0:T(8,128)(2,1)S(1)}, bf16[2048,1024]{1,0:T(8,128)(2,1)S(1)}, bf16[2048,1024]{1,0:T(...) custom-call(bf16[512,1024]{1,0:T(8,128)(2,1)S(1)} %get-tuple-element, ...), custom_call_target="tpu_custom_call", output_to_operand_aliasing={{0}: (8, {}), {1}: (9, {}), {2}: (10, {}), {3}: (11, {})} | custom-call | tf_op jit(solution)/shard_map/mlp_forward/pallas_call | solution.py:422
  235.1 20.1 %collective-permute-done.29.refs_3_ = bf16[512,1024]{1,0:T(8,128)(2,1)S(1)} collective-permute-done((bf16[512,1024]{1,0:T(8,128)(2,1)S(1)}, bf16[512,1024]{1,0:T(8,128)(2,1)S(1)}, u32[]{:S(2)}, u32[]{:S(2)}) %collective-permute-start.29) | collective-permute-done | bytes 1048608 | tf_op jit(solution)/shard_map/ppermute | solution.py:59
  271.6 10.1 %collective-permute-done.32.refs_0_ = bf16[512,1024]{1,0:T(8,128)(2,1)S(1)} collective-permute-done((bf16[512,1024]{1,0:T(8,128)(2,1)S(1)}, bf16[512,1024]{1,0:T(8,128)(2,1)S(1)}, u32[]{:S(2)}, u32[]{:S(2)}) %collective-permute-start.32) | collective-permute-done | bytes 1048608 | tf_op jit(solution)/shard_map/ppermute | solution.py:59
  297.3 13.8 %collective-permute-done.36.refs_3_ = bf16[512,1024]{1,0:T(8,128)(2,1)S(1)} collective-permute-done((bf16[512,1024]{1,0:T(8,128)(2,1)S(1)}, bf16[512,1024]{1,0:T(8,128)(2,1)S(1)}, u32[]{:S(2)}, u32[]{:S(2)}) %collective-permute-start.36) | collective-permute-done | bytes 1048608 | tf_op jit(solution)/shard_map/ppermute | solution.py:59
  319.6 10.8 %mlp_forward.6 = (bf16[2048,1024]{1,0:T(8,128)(2,1)S(1)}, bf16[2048,1024]{1,0:T(8,128)(2,1)S(1)}, bf16[2048,1024]{1,0:T(8,128)(2,1)S(1)}, bf16[2048,1024]{1,0:T(...) custom-call(bf16[512,1024]{1,0:T(8,128)(2,1)S(1)} %get-tuple-element.477.refs_0_, ...), custom_call_target="tpu_custom_call" | custom-call | tf_op jit(solution)/shard_map/mlp_forward/pallas_call | solution.py:422
  357.4 11.0 %mlp_forward.7 = (bf16[2048,1024]{1,0:T(8,128)(2,1)S(1)}, bf16[2048,1024]{1,0:T(8,128)(2,1)S(1)}, bf16[2048,1024]{1,0:T(8,128)(2,1)S(1)}, bf16[2048,1024]{1,0:T(...) custom-call(bf16[512,1024]{1,0:T(8,128)(2,1)S(1)} %get-tuple-element, ...), custom_call_target="tpu_custom_call", output_to_operand_aliasing={{0}: (8, {}), {1}: (9, {}), {2}: (10, {}), {3}: (11, {})} | custom-call | tf_op jit(solution)/shard_map/mlp_forward/pallas_call | solution.py:422
  389.2 12.4 %mlp_backward.4 = (bf16[2048,1024]{1,0:T(8,128)(2,1)S(1)}, bf16[2048,1024]{1,0:T(8,128)(2,1)S(1)}, f32[1,1024]{1,0:T(1,128)S(1)}, f32[1,1024]{1,0:T(1,128)S(1)},...) custom-call(bf16[512,1024]{1,0:T(8,128)(2,1)S(1)} %get-tuple-element.500.refs_0_, ...), custom_call_target="tpu_custom_call" | custom-call | tf_op jit(solution)/shard_map/mlp_backward/pallas_call | solution.py:422
  424.4 12.4 %mlp_backward.5 = (bf16[2048,1024]{1,0:T(8,128)(2,1)S(1)}, bf16[2048,1024]{1,0:T(8,128)(2,1)S(1)}, f32[1,1024]{1,0:T(1,128)S(1)}, f32[1,1024]{1,0:T(1,128)S(1)},...) custom-call(bf16[512,1024]{1,0:T(8,128)(2,1)S(1)} %get-tuple-element, ...), custom_call_target="tpu_custom_call", output_to_operand_aliasing={{0}: (10, {}), {1}: (11, {}), {4}: (12, {})} | custom-call | tf_op jit(solution)/shard_map/mlp_backward/pallas_call | solution.py:422
  457.4 14.8 %attention_backward.4 = (bf16[2048,768]{1,0:T(8,128)(2,1)S(1)}, f32[1,256]{1,0:T(1,128)S(1)}, bf16[512,1024]{1,0:T(8,128)(2,1)S(1)}, bf16[512,1024]{1,0:T(8,128)(2,1)S(1)}) custom-call(s32[4]{0:T(128)S(1)} %pad_add_fusion.refs_0_, f32[1,256]{1,0:T(1,128)S(1)} %slice.239.refs_1_, bf16[1024,1024]{1,0:T(8,128)(2,1)S(1)} %assemble.4.refs_3_.refs_2_, ...), custom_call_target="tpu_custom_call" | custom-call | tf_op jit(solution)/shard_map/attention_backward/pallas_call | solution.py:720
  484.8 15.0 %attention_backward.5 = (bf16[2048,768]{1,0:T(8,128)(2,1)S(1)}, f32[1,256]{1,0:T(1,128)S(1)}, bf16[512,1024]{1,0:T(8,128)(2,1)S(1)}, bf16[512,1024]{1,0:T(8,128)(2,1)S(1)}) custom-call(s32[4]{0:T(128)S(1)} %pad_add_fusion.refs_0_, f32[1,256]{1,0:T(1,128)S(1)} %slice.239.refs_1_, ...), custom_call_target="tpu_custom_call", output_to_operand_aliasing={{0}: (5, {})} | custom-call | tf_op jit(solution)/shard_map/attention_backward/pallas_call | solution.py:720
  555.0 12.4 %mlp_backward.6 = (bf16[2048,1024]{1,0:T(8,128)(2,1)S(1)}, bf16[2048,1024]{1,0:T(8,128)(2,1)S(1)}, f32[1,1024]{1,0:T(1,128)S(1)}, f32[1,1024]{1,0:T(1,128)S(1)},...) custom-call(bf16[512,1024]{1,0:T(8,128)(2,1)S(1)} %get-tuple-element.577.refs_0_, ...), custom_call_target="tpu_custom_call" | custom-call | tf_op jit(solution)/shard_map/mlp_backward/pallas_call | solution.py:422
  585.0 13.5 %mlp_backward.7 = (bf16[2048,1024]{1,0:T(8,128)(2,1)S(1)}, bf16[2048,1024]{1,0:T(8,128)(2,1)S(1)}, f32[1,1024]{1,0:T(1,128)S(1)}, f32[1,1024]{1,0:T(1,128)S(1)},...) custom-call(bf16[512,1024]{1,0:T(8,128)(2,1)S(1)} %get-tuple-element, ...), custom_call_target="tpu_custom_call", output_to_operand_aliasing={{0}: (10, {}), {1}: (11, {}), {4}: (12, {})} | custom-call | tf_op jit(solution)/shard_map/mlp_backward/pallas_call | solution.py:422
  630.2 15.8 %attention_backward.6 = (bf16[2048,768]{1,0:T(8,128)(2,1)S(1)}, f32[1,256]{1,0:T(1,128)S(1)}, bf16[512,1024]{1,0:T(8,128)(2,1)S(1)}, bf16[512,1024]{1,0:T(8,128)(2,1)}) custom-call(s32[4]{0:T(128)S(1)} %pad_add_fusion.refs_0_, f32[1,256]{1,0:T(1,128)S(1)} %slice.239.refs_1_, bf16[1024,1024]{1,0:T(8,128)(2,1)S(1)} %assemble.4.refs_3_.refs_2_, ...), custom_call_target="tpu_custom_call" | custom-call | tf_op jit(solution)/shard_map/attention_backward/pallas_call | solution.py:720
  682.8 9.8 %collective-permute-done.80 = bf16[512,1024]{1,0:T(8,128)(2,1)S(1)} collective-permute-done((bf16[512,1024]{1,0:T(8,128)(2,1)}, bf16[512,1024]{1,0:T(8,128)(2,1)S(1)}, u32[]{:S(2)}, u32[]{:S(2)}) %collective-permute-start.80) | collective-permute-done | bytes 1048608 | tf_op jit(solution)/shard_map/ppermute | solution.py:59
  702.0 15.3 %attention_backward.7 = (bf16[2048,768]{1,0:T(8,128)(2,1)S(1)}, f32[1,256]{1,0:T(1,128)S(1)}, bf16[512,1024]{1,0:T(8,128)(2,1)S(1)}, bf16[512,1024]{1,0:T(8,128)(2,1)S(1)}) custom-call(s32[4]{0:T(128)S(1)} %pad_add_fusion.refs_0_, f32[1,256]{1,0:T(1,128)S(1)} %slice.239.refs_1_, ...), custom_call_target="tpu_custom_call", output_to_operand_aliasing={{0}: (5, {})} | custom-call | tf_op jit(solution)/shard_map/attention_backward/pallas_call | solution.py:720
  755.0 13.5 %collective-permute-done.91 = bf16[512,1024]{1,0:T(8,128)(2,1)S(1)} collective-permute-done((bf16[512,1024]{1,0:T(8,128)(2,1)S(1)}, bf16[512,1024]{1,0:T(8,128)(2,1)S(1)}, u32[]{:S(2)}, u32[]{:S(2)}) %collective-permute-start.91) | collective-permute-done | bytes 1048608 | tf_op jit(solution)/shard_map/ppermute | solution.py:59
  778.2 23.0 %collective-permute-done.87 = bf16[512,1024]{1,0:T(8,128)(2,1)S(1)} collective-permute-done((bf16[512,1024]{1,0:T(8,128)(2,1)S(1)}, bf16[512,1024]{1,0:T(8,128)(2,1)S(1)}, u32[]{:S(2)}, u32[]{:S(2)}) %collective-permute-start.87) | collective-permute-done | bytes 1048608 | tf_op jit(solution)/shard_map/ppermute | solution.py:59
  801.2 11.9 %collective-permute-done.95 = bf16[512,1024]{1,0:T(8,128)(2,1)S(1)} collective-permute-done((bf16[512,1024]{1,0:T(8,128)(2,1)S(1)}, bf16[512,1024]{1,0:T(8,128)(2,1)S(1)}, u32[]{:S(2)}, u32[]{:S(2)}) %collective-permute-start.95) | collective-permute-done | bytes 1048608 | tf_op jit(solution)/shard_map/ppermute | solution.py:59
  822.6 23.1 %collective-permute-done.101 = f32[1,6656]{1,0:T(1,128)S(1)} collective-permute-done((f32[1,6656]{1,0:T(1,128)S(1)}, f32[1,6656]{1,0:T(1,128)S(1)}, u32[]{:S(2)}, u32[]{:S(2)}) %collective-permute-start.101) | collective-permute-done | bytes 26656 | tf_op jit(solution)/shard_map/ppermute | solution.py:59
  (715 shorter events, 530.7 us)
Async XLA Ops:
  35.5 32.8 %collective-permute-start.3 = (bf16[256,1024]{1,0:T(8,128)(2,1)}, bf16[256,1024]{1,0:T(8,128)(2,1)}, u32[]{:S(2)}, u32[]{:S(2)}) collective-permute-start(bf16[256,1024]{1,0:T(8,128)(2,1)} %broadcast_select_fusion.1), channel_id=1, source_target_pairs={{0,4},{1,5},{2,6},{3,7},{4,0},{5,1},{6,2},{7,3},{8,12},{9,13},{10,... | collective-permute-start | bytes 1572872 | tf_op jit(solution)/shard_map/ppermute | solution.py:59
  82.0 45.2 %collective-permute-start.12 = (bf16[512,1024]{1,0:T(8,128)(2,1)}, bf16[512,1024]{1,0:T(8,128)(2,1)}, u32[]{:S(2)}, u32[]{:S(2)}) collective-permute-start(bf16[512,1024]{1,0:T(8,128)(2,1)} %collective-permute-done.8.refs_0_), channel_id=1, source_target_pairs={{1,3},{3,1},{5,7},{7,5},{8,10},{10,8},{12,14},{14,12},{17,19},{19,... | collective-permute-start | bytes 3145736 | tf_op jit(solution)/shard_map/ppermute | solution.py:59
  83.6 43.6 %collective-permute-start.13 = (bf16[512,1024]{1,0:T(8,128)(2,1)}, bf16[512,1024]{1,0:T(8,128)(2,1)}, u32[]{:S(2)}, u32[]{:S(2)}) collective-permute-start(bf16[512,1024]{1,0:T(8,128)(2,1)} %get-tuple-element.396), channel_id=1, source_target_pairs={{0,8},{2,10},{4,12},{6,14},{9,1},{11,3},{13,5},{15,7},{16,24},{18,... | collective-permute-start | bytes 3145736 | tf_op jit(solution)/shard_map/ppermute | solution.py:59
  134.2 35.9 %collective-permute-start.17 = (bf16[512,1024]{1,0:T(8,128)(2,1)S(1)}, bf16[512,1024]{1,0:T(8,128)(2,1)S(1)}, u32[]{:S(2)}, u32[]{:S(2)}) collective-permute-start(bf16[512,1024]{1,0:T(8,128)(2,1)S(1)} %add_convert_fusion.25.refs_2_), channel_id=1, source_target_pairs={{0,4},{1,5},{2,6},{3,7},{4,0},{5,1},{6,2},{7,3},{8,12},{9,13},{10,... | collective-permute-start | bytes 3145736 | tf_op jit(solution)/shard_map/ppermute | solution.py:59
  231.6 28.6 %collective-permute-start.28 = (bf16[512,1024]{1,0:T(8,128)(2,1)S(1)}, bf16[512,1024]{1,0:T(8,128)(2,1)S(1)}, u32[]{:S(2)}, u32[]{:S(2)}) collective-permute-start(bf16[512,1024]{1,0:T(8,128)(2,1)S(1)} %blend_forward.10), channel_id=1, source_target_pairs={{0,16},{1,17},{2,18},{3,19},{4,20},{5,21},{6,22},{7,23},{8,24},{9,... | collective-permute-start | bytes 3145736 | tf_op jit(solution)/shard_map/ppermute | solution.py:59
  344.6 29.8 %collective-permute-start.44 = (bf16[512,1024]{1,0:T(8,128)(2,1)}, bf16[512,1024]{1,0:T(8,128)(2,1)}, u32[]{:S(2)}, u32[]{:S(2)}) collective-permute-start(bf16[512,1024]{1,0:T(8,128)(2,1)} %add_convert_fusion.19.refs_2_), channel_id=1, source_target_pairs={{0,4},{1,5},{2,6},{3,7},{4,0},{5,1},{6,2},{7,3},{8,12},{9,13},{10,... | collective-permute-start | bytes 3145736 | tf_op jit(solution)/shard_map/ppermute | solution.py:59
  378.6 28.9 %collective-permute-start.48 = (bf16[512,1024]{1,0:T(8,128)(2,1)}, bf16[512,1024]{1,0:T(8,128)(2,1)S(1)}, u32[]{:S(2)}, u32[]{:S(2)}) collective-permute-start(bf16[512,1024]{1,0:T(8,128)(2,1)} %add_convert_fusion.18.refs_2_), channel_id=1, source_target_pairs={{0,4},{1,5},{2,6},{3,7},{4,0},{5,1},{6,2},{7,3},{8,12},{9,13},{10,... | collective-permute-start | bytes 3145736 | tf_op jit(solution)/shard_map/ppermute | solution.py:59
  410.6 31.2 %collective-permute-start.52 = (bf16[512,1024]{1,0:T(8,128)(2,1)S(1)}, bf16[512,1024]{1,0:T(8,128)(2,1)}, u32[]{:S(2)}, u32[]{:S(2)}) collective-permute-start(bf16[512,1024]{1,0:T(8,128)(2,1)S(1)} %add_convert_fusion.17.refs_5_), channel_id=1, source_target_pairs={{0,4},{1,5},{2,6},{3,7},{4,0},{5,1},{6,2},{7,3},{8,12},{9,13},{10,... | collective-permute-start | bytes 3145736 | tf_op jit(solution)/shard_map/ppermute | solution.py:59
  505.3 41.9 %collective-permute-start.62 = (bf16[512,1024]{1,0:T(8,128)(2,1)}, bf16[512,1024]{1,0:T(8,128)(2,1)}, u32[]{:S(2)}, u32[]{:S(2)}) collective-permute-start(bf16[512,1024]{1,0:T(8,128)(2,1)} %add_convert_fusion.13), channel_id=1, source_target_pairs={{16,0},{17,1},{18,2},{19,3},{20,4},{21,5},{22,6},{23,7},{24,8},{25... | collective-permute-start | bytes 3145736 | tf_op jit(solution)/shard_map/ppermute | solution.py:59
  542.7 28.7 %collective-permute-start.64 = (bf16[512,1024]{1,0:T(8,128)(2,1)S(1)}, bf16[512,1024]{1,0:T(8,128)(2,1)S(1)}, u32[]{:S(2)}, u32[]{:S(2)}) collective-permute-start(bf16[512,1024]{1,0:T(8,128)(2,1)S(1)} %add_convert_fusion.12), channel_id=1, source_target_pairs={{16,0},{17,1},{18,2},{19,3},{20,4},{21,5},{22,6},{23,7},{24,8},{25... | collective-permute-start | bytes 3145736 | tf_op jit(solution)/shard_map/ppermute | solution.py:59
  574.5 29.0 %collective-permute-start.70 = (bf16[512,1024]{1,0:T(8,128)(2,1)S(1)}, bf16[512,1024]{1,0:T(8,128)(2,1)S(1)}, u32[]{:S(2)}, u32[]{:S(2)}) collective-permute-start(bf16[512,1024]{1,0:T(8,128)(2,1)S(1)} %add_convert_fusion.11.refs_5_), channel_id=1, source_target_pairs={{0,4},{1,5},{2,6},{3,7},{4,0},{5,1},{6,2},{7,3},{8,12},{9,13},{10,... | collective-permute-start | bytes 3145736 | tf_op jit(solution)/shard_map/ppermute | solution.py:59
  622.4 29.6 %collective-permute-start.74 = (bf16[512,1024]{1,0:T(8,128)(2,1)S(1)}, bf16[512,1024]{1,0:T(8,128)(2,1)S(1)}, u32[]{:S(2)}, u32[]{:S(2)}) collective-permute-start(bf16[512,1024]{1,0:T(8,128)(2,1)S(1)} %constant_dynamic-slice_fusion.3), channel_id=1, source_target_pairs={{0,2},{1,3},{2,0},{3,1},{4,6},{5,7},{6,4},{7,5},{8,10},{9,11},{10,... | collective-permute-start | bytes 3145736 | tf_op jit(solution)/shard_map/ppermute | solution.py:59
  624.9 35.7 %collective-permute-start.76 = (bf16[512,1024]{1,0:T(8,128)(2,1)S(1)}, bf16[512,1024]{1,0:T(8,128)(2,1)S(1)}, u32[]{:S(2)}, u32[]{:S(2)}) collective-permute-start(bf16[512,1024]{1,0:T(8,128)(2,1)S(1)} %add_convert_fusion.10.refs_5_), channel_id=1, source_target_pairs={{0,4},{1,5},{2,6},{3,7},{4,0},{5,1},{6,2},{7,3},{8,12},{9,13},{10,... | collective-permute-start | bytes 3145736 | tf_op jit(solution)/shard_map/ppermute | solution.py:59
  663.2 29.4 %collective-permute-start.80 = (bf16[512,1024]{1,0:T(8,128)(2,1)}, bf16[512,1024]{1,0:T(8,128)(2,1)S(1)}, u32[]{:S(2)}, u32[]{:S(2)}) collective-permute-start(bf16[512,1024]{1,0:T(8,128)(2,1)} %add_convert_fusion.9), channel_id=1, source_target_pairs={{1,9},{3,11},{5,13},{7,15},{8,0},{10,2},{12,4},{14,6},{17,25},{19,... | collective-permute-start | bytes 3145736 | tf_op jit(solution)/shard_map/ppermute | solution.py:59
  681.9 50.9 %collective-permute-start.85 = (bf16[512,1024]{1,0:T(8,128)(2,1)S(1)}, bf16[512,1024]{1,0:T(8,128)(2,1)S(1)}, u32[]{:S(2)}, u32[]{:S(2)}) collective-permute-start(bf16[512,1024]{1,0:T(8,128)(2,1)S(1)} %add_convert_fusion.8), channel_id=1, source_target_pairs={{0,4},{1,5},{2,6},{3,7},{4,0},{5,1},{6,2},{7,3},{8,12},{9,13},{10,... | collective-permute-start | bytes 3145736 | tf_op jit(solution)/shard_map/ppermute | solution.py:59
  696.4 29.0 %collective-permute-start.83 = (bf16[512,1024]{1,0:T(8,128)(2,1)S(1)}, bf16[512,1024]{1,0:T(8,128)(2,1)S(1)}, u32[]{:S(2)}, u32[]{:S(2)}) collective-permute-start(bf16[512,1024]{1,0:T(8,128)(2,1)S(1)} %add_convert_fusion.6), channel_id=1, source_target_pairs={{1,9},{3,11},{5,13},{7,15},{8,0},{10,2},{12,4},{14,6},{17,25},{19,... | collective-permute-start | bytes 3145736 | tf_op jit(solution)/shard_map/ppermute | solution.py:59
  697.9 34.2 %collective-permute-start.84 = (bf16[512,1024]{1,0:T(8,128)(2,1)S(1)}, bf16[512,1024]{1,0:T(8,128)(2,1)S(1)}, u32[]{:S(2)}, u32[]{:S(2)}) collective-permute-start(bf16[512,1024]{1,0:T(8,128)(2,1)S(1)} %constant_dynamic-slice_fusion.1), channel_id=1, source_target_pairs={{0,2},{1,3},{2,0},{3,1},{4,6},{5,7},{6,4},{7,5},{8,10},{9,11},{10,... | collective-permute-start | bytes 3145736 | tf_op jit(solution)/shard_map/ppermute | solution.py:59
  770.5 30.7 %collective-permute-start.87 = (bf16[512,1024]{1,0:T(8,128)(2,1)S(1)}, bf16[512,1024]{1,0:T(8,128)(2,1)S(1)}, u32[]{:S(2)}, u32[]{:S(2)}) collective-permute-start(bf16[512,1024]{1,0:T(8,128)(2,1)S(1)} %add_convert_fusion.3), channel_id=1, source_target_pairs={{0,4},{1,5},{2,6},{3,7},{4,0},{5,1},{6,2},{7,3},{8,12},{9,13},{10,... | collective-permute-start | bytes 3145736 | tf_op jit(solution)/shard_map/ppermute | solution.py:59
  770.5 30.7 %collective-permute-start.92 = (bf16[512,1024]{1,0:T(8,128)(2,1)S(1)}, bf16[512,1024]{1,0:T(8,128)(2,1)S(1)}, u32[]{:S(2)}, u32[]{:S(2)}) collective-permute-start(bf16[512,1024]{1,0:T(8,128)(2,1)S(1)} %add_convert_fusion.5.refs_0_), channel_id=1, source_target_pairs={{0,1},{2,3},{4,5},{6,7},{9,8},{11,10},{13,12},{15,14},{16,17},{18,... | collective-permute-start | bytes 3145736 | tf_op jit(solution)/shard_map/ppermute | solution.py:59
  772.6 28.6 %collective-permute-start.93 = (bf16[512,1024]{1,0:T(8,128)(2,1)S(1)}, bf16[512,1024]{1,0:T(8,128)(2,1)S(1)}, u32[]{:S(2)}, u32[]{:S(2)}) collective-permute-start(bf16[512,1024]{1,0:T(8,128)(2,1)S(1)} %collective-permute-done.90.refs_1_), channel_id=1, source_target_pairs={{0,1},{2,3},{4,5},{6,7},{9,8},{11,10},{13,12},{15,14},{16,17},{18,... | collective-permute-start | bytes 3145736 | tf_op jit(solution)/shard_map/ppermute | solution.py:59
  777.6 35.6 %collective-permute-start.95 = (bf16[512,1024]{1,0:T(8,128)(2,1)S(1)}, bf16[512,1024]{1,0:T(8,128)(2,1)S(1)}, u32[]{:S(2)}, u32[]{:S(2)}) collective-permute-start(bf16[512,1024]{1,0:T(8,128)(2,1)S(1)} %constant_dynamic-slice_fusion), channel_id=1, source_target_pairs={{0,2},{1,3},{2,0},{3,1},{4,6},{5,7},{6,4},{7,5},{8,10},{9,11},{10,... | collective-permute-start | bytes 3145736 | tf_op jit(solution)/shard_map/ppermute | solution.py:59
  813.7 32.1 %collective-permute-start.98 = (bf16[512,1024]{1,0:T(8,128)(2,1)S(1)}, bf16[512,1024]{1,0:T(8,128)(2,1)S(1)}, u32[]{:S(2)}, u32[]{:S(2)}) collective-permute-start(bf16[512,1024]{1,0:T(8,128)(2,1)S(1)} %add_convert_fusion.2.refs_0_), channel_id=1, source_target_pairs={{0,1},{2,3},{4,5},{6,7},{9,8},{11,10},{13,12},{15,14},{16,17},{18,... | collective-permute-start | bytes 3145736 | tf_op jit(solution)/shard_map/ppermute | solution.py:59
  815.0 31.8 %collective-permute-start.99 = (bf16[512,1024]{1,0:T(8,128)(2,1)S(1)}, bf16[512,1024]{1,0:T(8,128)(2,1)S(1)}, u32[]{:S(2)}, u32[]{:S(2)}) collective-permute-start(bf16[512,1024]{1,0:T(8,128)(2,1)S(1)} %collective-permute-done.94.refs_1_), channel_id=1, source_target_pairs={{0,1},{2,3},{4,5},{6,7},{9,8},{11,10},{13,12},{15,14},{16,17},{18,... | collective-permute-start | bytes 3145736 | tf_op jit(solution)/shard_map/ppermute | solution.py:59
  816.4 31.4 %collective-permute-start.100 = (bf16[512,1024]{1,0:T(8,128)(2,1)S(1)}, bf16[512,1024]{1,0:T(8,128)(2,1)S(1)}, u32[]{:S(2)}, u32[]{:S(2)}) collective-permute-start(bf16[512,1024]{1,0:T(8,128)(2,1)S(1)} %add_convert_fusion.1), channel_id=1, source_target_pairs={{1,9},{3,11},{5,13},{7,15},{8,0},{10,2},{12,4},{14,6},{17,25},{19,... | collective-permute-start | bytes 3145736 | tf_op jit(solution)/shard_map/ppermute | solution.py:59
  (265 other events, 2620.1 us)

commit v3 on v2

--- a/solution.py
+++ b/solution.py
@@ -12,7 +12,7 @@
 AXES = ("section", "tensor", "dp")
 F32 = jnp.float32
 LOW = jnp.bfloat16
-VMEM_LIMIT = 24 * 1024 * 1024
+VMEM_LIMIT = 32 * 1024 * 1024
 BAND = 256
 
 
@@ -136,8 +136,19 @@
         return anchor
 
     def drain(self):
-        while self.busy():
-            self.step((), 8)
+        tasks = [(task, flying) for task, flying, _ in self.active]
+        tasks += [(task, None) for task in self.waiting]
+        while tasks:
+            going = []
+            for task, flying in tasks:
+                try:
+                    wanted = task.send(flying)
+                except StopIteration:
+                    continue
+                wanted = wanted[0] if isinstance(wanted, tuple) else wanted
+                going.append((task, [self.place.move(array, target) for array, target in wanted]))
+            tasks = going
+        self.active, self.waiting = [], []
 
 
 def spec(count):
@@ -1215,7 +1226,7 @@
         {
             "mlp": none,
             "attention": [2] + [1] * (len(streams) - 1),
-            "end": [1] + [0] * (len(streams) - 1),
+            "end": none[1:] + [1],
         },
     )
     bg.add(
@@ -1231,12 +1242,8 @@
         value = jnp.where(first, summed(grad_start[at])[:part], grad_second[at][:part])
         return move_task(place, value, transposed, grad_in)
 
-    for at in streams[:-1]:
+    for at in streams:
         bg.add(in_rows(at))
-    bg.step((), 1 + len(streams))
-    flying = bg.step([value for value, _ in grad_start[-1]], 0)
-    grad_start[-1] = [(value, bit) for value, (_, bit) in zip(flying, grad_start[-1])]
-    bg.add(in_rows(streams[-1]))
     bg.drain()
 
     def done(name, columns):

time: 888 us -> 844 us (0.950)
  local copies, waits for them, and re-layouts: 110 us -> 76.5 us
  starting transfers between devices: 150 us -> 160 us
  waiting for transfers between devices: 273 us -> 264 us
    unnamed x369 -> x313, local copies, waits for them, and re-layouts: 93.7 us -> 59.4 us
    ppermute x107, starting transfers between devices: 150 us -> 160 us  [move(): return lax.ppermute(value, AXES, links)]
    ppermute x107, waiting for transfers between devices: 273 us -> 264 us  [move(): return lax.ppermute(value, AXES, links)]
    pallas_call x16, Pallas kernels: 109 us -> 119 us  [fused_dot(): pl.pallas_call(kernel, grid=(steps,), out_shape=out_shape, in_specs=in_sp...]
  transfers between devices with their start and end apart: 107 -> 107, of which waited for: 59 -> 65; matrix products, arithmetic and copies ran while one was open for 9% -> 11% of each run, Pallas kernels for 28% -> 29%
where the time goes in v3:
time: 844 us; the launch traced here: 835 us
  waiting for transfers between devices  264 us (31%)
  Pallas kernels  248 us (29%)
  starting transfers between devices  160 us (19%)
  local copies, waits for them, and re-layouts  76.5 us (9%)
  matrix products  48.3 us (6%)
  other arithmetic  34.7 us (4%)
    ppermute x107, waiting for transfers between devices, move(): return lax.ppermute(value, AXES, links)  264 us
    ppermute x107, starting transfers between devices, move(): return lax.ppermute(value, AXES, links)  160 us
    pallas_call x16, Pallas kernels, fused_dot(): pl.pallas_call(kernel, grid=(steps,), out_shape=out_shape, in_specs=in_sp...  119 us
    pallas_call x4, Pallas kernels, attention_backward(): pl.pallas_call(kernel, grid=(1,), out_shape=[jax.ShapeDtypeStruct((length...  59.5 us
    unnamed x313, local copies, waits for them, and re-layouts  59.4 us
    dot_general x10, matrix products, tn_dot(): lax.dot_general(left, right, (((0,), (0,)), ((), ())), preferred_element_...  48.3 us
    pallas_call x4, Pallas kernels, attention_forward(): pl.pallas_call(kernel, grid=(1,), out_shape=[jax.ShapeDtypeStruct((length...  23.7 us
    pallas_call x8, Pallas kernels, blend_backward(): pl.pallas_call(kernel, grid=(steps,), out_shape=[jax.ShapeDtypeStruct((ro...  20.6 us
  transfers between devices with their start and end apart: 107, of which 65 were waited for; matrix products, arithmetic and copies ran while one was open for 11% of the time, Pallas kernels for 29%

profile of v3, /device:TPU:0, one launch (start us, length us, event | category | flops | bytes accessed | tf_op | source)
XLA Modules:
  0.0 835.3 jit_solution(568609021887408075)
XLA Ops:
  18.6 15.0 %collective-permute-done.1 = f32[1,2304]{1,0:T(1,128)S(1)} collective-permute-done((f32[1,2304]{1,0:T(1,128)S(1)}, f32[1,2304]{1,0:T(1,128)S(1)}, u32[]{:S(2)}, u32[]{:S(2)}) %collective-permute-start.1) | collective-permute-done | bytes 9248 | tf_op jit(solution)/shard_map/ppermute | solution.py:59
  35.5 18.4 %collective-permute-start.3 = (bf16[256,1024]{1,0:T(8,128)(2,1)}, bf16[256,1024]{1,0:T(8,128)(2,1)}, u32[]{:S(2)}, u32[]{:S(2)}) collective-permute-start(bf16[256,1024]{1,0:T(8,128)(2,1)} %broadcast_select_fusion.1), channel_id=1, source_target_pairs={{0,4},{1,5},{2,6},{3,7},{4,0},{5,1},{6,2},{7,3},{8,12},{9,13},{10,... | collective-permute-start | bytes 1572872 | tf_op jit(solution)/shard_map/ppermute | solution.py:59
  83.6 16.6 %collective-permute-start.13 = (bf16[512,1024]{1,0:T(8,128)(2,1)}, bf16[512,1024]{1,0:T(8,128)(2,1)}, u32[]{:S(2)}, u32[]{:S(2)}) collective-permute-start(bf16[512,1024]{1,0:T(8,128)(2,1)} %get-tuple-element.347), channel_id=1, source_target_pairs={{0,8},{2,10},{4,12},{6,14},{9,1},{11,3},{13,5},{15,7},{16,24},{18,... | collective-permute-start | bytes 3145736 | tf_op jit(solution)/shard_map/ppermute | solution.py:59
  156.4 13.4 %collective-permute-done.17.refs_3_ = bf16[512,1024]{1,0:T(8,128)(2,1)S(1)} collective-permute-done((bf16[512,1024]{1,0:T(8,128)(2,1)S(1)}, bf16[512,1024]{1,0:T(8,128)(2,1)S(1)}, u32[]{:S(2)}, u32[]{:S(2)}) %collective-permute-start.17) | collective-permute-done | bytes 1048608 | tf_op jit(solution)/shard_map/ppermute | solution.py:59
  180.1 12.1 %mlp_forward.4 = (bf16[2048,1024]{1,0:T(8,128)(2,1)S(1)}, bf16[2048,1024]{1,0:T(8,128)(2,1)S(1)}, bf16[2048,1024]{1,0:T(8,128)(2,1)}, bf16[2048,1024]{1,0:T(8,12...) custom-call(bf16[512,1024]{1,0:T(8,128)(2,1)S(1)} %get-tuple-element.377.refs_0_, ...), custom_call_target="tpu_custom_call" | custom-call | tf_op jit(solution)/shard_map/mlp_forward/pallas_call | solution.py:433
  206.5 12.1 %mlp_forward.5 = (bf16[2048,1024]{1,0:T(8,128)(2,1)S(1)}, bf16[2048,1024]{1,0:T(8,128)(2,1)S(1)}, bf16[2048,1024]{1,0:T(8,128)(2,1)}, bf16[2048,1024]{1,0:T(8,12...) custom-call(bf16[512,1024]{1,0:T(8,128)(2,1)S(1)} %get-tuple-element, ...), custom_call_target="tpu_custom_call", output_to_operand_aliasing={{0}: (8, {}), {1}: (9, {}), {2}: (10, {}), {3}: (11, {})} | custom-call | tf_op jit(solution)/shard_map/mlp_forward/pallas_call | solution.py:433
  236.7 19.1 %collective-permute-done.29.refs_3_ = bf16[512,1024]{1,0:T(8,128)(2,1)S(1)} collective-permute-done((bf16[512,1024]{1,0:T(8,128)(2,1)S(1)}, bf16[512,1024]{1,0:T(8,128)(2,1)S(1)}, u32[]{:S(2)}, u32[]{:S(2)}) %collective-permute-start.29) | collective-permute-done | bytes 1048608 | tf_op jit(solution)/shard_map/ppermute | solution.py:59
  273.6 9.9 %collective-permute-done.32.refs_0_ = bf16[512,1024]{1,0:T(8,128)(2,1)S(1)} collective-permute-done((bf16[512,1024]{1,0:T(8,128)(2,1)S(1)}, bf16[512,1024]{1,0:T(8,128)(2,1)S(1)}, u32[]{:S(2)}, u32[]{:S(2)}) %collective-permute-start.32) | collective-permute-done | bytes 1048608 | tf_op jit(solution)/shard_map/ppermute | solution.py:59
  299.7 13.1 %collective-permute-done.36.refs_3_ = bf16[512,1024]{1,0:T(8,128)(2,1)S(1)} collective-permute-done((bf16[512,1024]{1,0:T(8,128)(2,1)S(1)}, bf16[512,1024]{1,0:T(8,128)(2,1)S(1)}, u32[]{:S(2)}, u32[]{:S(2)}) %collective-permute-start.36) | collective-permute-done | bytes 1048608 | tf_op jit(solution)/shard_map/ppermute | solution.py:59
  320.4 12.0 %mlp_forward.6 = (bf16[2048,1024]{1,0:T(8,128)(2,1)S(1)}, bf16[2048,1024]{1,0:T(8,128)(2,1)S(1)}, bf16[2048,1024]{1,0:T(8,128)(2,1)}, bf16[2048,1024]{1,0:T(8,12...) custom-call(bf16[512,1024]{1,0:T(8,128)(2,1)S(1)} %get-tuple-element.428.refs_0_, ...), custom_call_target="tpu_custom_call" | custom-call | tf_op jit(solution)/shard_map/mlp_forward/pallas_call | solution.py:433
  348.8 12.3 %mlp_forward.7 = (bf16[2048,1024]{1,0:T(8,128)(2,1)S(1)}, bf16[2048,1024]{1,0:T(8,128)(2,1)S(1)}, bf16[2048,1024]{1,0:T(8,128)(2,1)}, bf16[2048,1024]{1,0:T(8,12...) custom-call(bf16[512,1024]{1,0:T(8,128)(2,1)S(1)} %get-tuple-element, ...), custom_call_target="tpu_custom_call", output_to_operand_aliasing={{0}: (8, {}), {1}: (9, {}), {2}: (10, {}), {3}: (11, {})} | custom-call | tf_op jit(solution)/shard_map/mlp_forward/pallas_call | solution.py:433
  379.5 13.7 %mlp_backward.4 = (bf16[2048,1024]{1,0:T(8,128)(2,1)S(1)}, bf16[2048,1024]{1,0:T(8,128)(2,1)S(1)}, f32[1,1024]{1,0:T(1,128)S(1)}, f32[1,1024]{1,0:T(1,128)S(1)},...) custom-call(bf16[512,1024]{1,0:T(8,128)(2,1)S(1)} %get-tuple-element.451.refs_0_, ...), custom_call_target="tpu_custom_call" | custom-call | tf_op jit(solution)/shard_map/mlp_backward/pallas_call | solution.py:433
  413.0 13.8 %mlp_backward.5 = (bf16[2048,1024]{1,0:T(8,128)(2,1)S(1)}, bf16[2048,1024]{1,0:T(8,128)(2,1)S(1)}, f32[1,1024]{1,0:T(1,128)S(1)}, f32[1,1024]{1,0:T(1,128)S(1)},...) custom-call(bf16[512,1024]{1,0:T(8,128)(2,1)S(1)} %get-tuple-element, ...), custom_call_target="tpu_custom_call", output_to_operand_aliasing={{0}: (10, {}), {1}: (11, {}), {4}: (12, {})} | custom-call | tf_op jit(solution)/shard_map/mlp_backward/pallas_call | solution.py:433
  442.8 14.8 %attention_backward.4 = (bf16[2048,768]{1,0:T(8,128)(2,1)S(1)}, f32[1,256]{1,0:T(1,128)S(1)}, bf16[512,1024]{1,0:T(8,128)(2,1)S(1)}, bf16[512,1024]{1,0:T(8,128)(2,1)S(1)}) custom-call(s32[4]{0:T(128)S(1)} %pad_add_fusion.refs_0_, f32[1,256]{1,0:T(1,128)S(1)} %slice.239.refs_1_, bf16[1024,1024]{1,0:T(8,128)(2,1)S(1)} %assemble.4.refs_3_.refs_2_, ...), custom_call_target="tpu_custom_call" | custom-call | tf_op jit(solution)/shard_map/attention_backward/pallas_call | solution.py:731
  471.5 15.0 %attention_backward.5 = (bf16[2048,768]{1,0:T(8,128)(2,1)S(1)}, f32[1,256]{1,0:T(1,128)S(1)}, bf16[512,1024]{1,0:T(8,128)(2,1)S(1)}, bf16[512,1024]{1,0:T(8,128)(2,1)S(1)}) custom-call(s32[4]{0:T(128)S(1)} %pad_add_fusion.refs_0_, f32[1,256]{1,0:T(1,128)S(1)} %slice.239.refs_1_, ...), custom_call_target="tpu_custom_call", output_to_operand_aliasing={{0}: (5, {})} | custom-call | tf_op jit(solution)/shard_map/attention_backward/pallas_call | solution.py:731
  535.2 13.8 %mlp_backward.6 = (bf16[2048,1024]{1,0:T(8,128)(2,1)S(1)}, bf16[2048,1024]{1,0:T(8,128)(2,1)S(1)}, f32[1,1024]{1,0:T(1,128)S(1)}, f32[1,1024]{1,0:T(1,128)S(1)},...) custom-call(bf16[512,1024]{1,0:T(8,128)(2,1)S(1)} %get-tuple-element.527.refs_0_, ...), custom_call_target="tpu_custom_call" | custom-call | tf_op jit(solution)/shard_map/mlp_backward/pallas_call | solution.py:433
  563.4 14.2 %mlp_backward.7 = (bf16[2048,1024]{1,0:T(8,128)(2,1)S(1)}, bf16[2048,1024]{1,0:T(8,128)(2,1)S(1)}, f32[1,1024]{1,0:T(1,128)S(1)}, f32[1,1024]{1,0:T(1,128)S(1)},...) custom-call(bf16[512,1024]{1,0:T(8,128)(2,1)S(1)} %get-tuple-element, ...), custom_call_target="tpu_custom_call", output_to_operand_aliasing={{0}: (10, {}), {1}: (11, {}), {4}: (12, {})} | custom-call | tf_op jit(solution)/shard_map/mlp_backward/pallas_call | solution.py:433
  605.2 15.0 %attention_backward.6 = (bf16[2048,768]{1,0:T(8,128)(2,1)S(1)}, f32[1,256]{1,0:T(1,128)S(1)}, bf16[512,1024]{1,0:T(8,128)(2,1)S(1)}, bf16[512,1024]{1,0:T(8,128)(2,1)S(1)}) custom-call(s32[4]{0:T(128)S(1)} %pad_add_fusion.refs_0_, f32[1,256]{1,0:T(1,128)S(1)} %slice.239.refs_1_, bf16[1024,1024]{1,0:T(8,128)(2,1)S(1)} %assemble.4.refs_3_.refs_2_, ...), custom_call_target="tpu_custom_call" | custom-call | tf_op jit(solution)/shard_map/attention_backward/pallas_call | solution.py:731
  652.9 14.8 %attention_backward.7 = (bf16[2048,768]{1,0:T(8,128)(2,1)S(1)}, f32[1,256]{1,0:T(1,128)S(1)}, bf16[512,1024]{1,0:T(8,128)(2,1)S(1)}, bf16[512,1024]{1,0:T(8,128)(2,1)S(1)}) custom-call(s32[4]{0:T(128)S(1)} %pad_add_fusion.refs_0_, f32[1,256]{1,0:T(1,128)S(1)} %slice.239.refs_1_, ...), custom_call_target="tpu_custom_call", output_to_operand_aliasing={{0}: (5, {})} | custom-call | tf_op jit(solution)/shard_map/attention_backward/pallas_call | solution.py:731
  703.6 9.0 %collective-permute-done.99 = bf16[512,1024]{1,0:T(8,128)(2,1)} collective-permute-done((bf16[512,1024]{1,0:T(8,128)(2,1)}, bf16[512,1024]{1,0:T(8,128)(2,1)}, u32[]{:S(2)}, u32[]{:S(2)}) %collective-permute-start.99) | collective-permute-done | bytes 1048608 | tf_op jit(solution)/shard_map/ppermute | solution.py:59
  716.1 18.4 %collective-permute-done.87 = bf16[512,1024]{1,0:T(8,128)(2,1)} collective-permute-done((bf16[512,1024]{1,0:T(8,128)(2,1)}, bf16[512,1024]{1,0:T(8,128)(2,1)}, u32[]{:S(2)}, u32[]{:S(2)}) %collective-permute-start.87) | collective-permute-done | bytes 1048608 | tf_op jit(solution)/shard_map/ppermute | solution.py:59
  749.3 15.9 %collective-permute-done.100 = bf16[512,1024]{1,0:T(8,128)(2,1)S(1)} collective-permute-done((bf16[512,1024]{1,0:T(8,128)(2,1)S(1)}, bf16[512,1024]{1,0:T(8,128)(2,1)S(1)}, u32[]{:S(2)}, u32[]{:S(2)}) %collective-permute-start.100) | collective-permute-done | bytes 1048608 | tf_op jit(solution)/shard_map/ppermute | solution.py:59
  765.9 10.5 %collective-permute-done.88 = bf16[512,1024]{1,0:T(8,128)(2,1)S(1)} collective-permute-done((bf16[512,1024]{1,0:T(8,128)(2,1)S(1)}, bf16[512,1024]{1,0:T(8,128)(2,1)S(1)}, u32[]{:S(2)}, u32[]{:S(2)}) %collective-permute-start.88) | collective-permute-done | bytes 1048608 | tf_op jit(solution)/shard_map/ppermute | solution.py:59
  804.6 9.0 %collective-permute-start.90 = (bf16[512,1024]{1,0:T(8,128)(2,1)S(1)}, bf16[512,1024]{1,0:T(8,128)(2,1)S(1)}, u32[]{:S(2)}, u32[]{:S(2)}) collective-permute-start(bf16[512,1024]{1,0:T(8,128)(2,1)S(1)} %add_convert_fusion.3.refs_0_), channel_id=1, source_target_pairs={{0,1},{2,3},{4,5},{6,7},{9,8},{11,10},{13,12},{15,14},{16,17},{18,... | collective-permute-start | bytes 3145736 | tf_op jit(solution)/shard_map/ppermute | solution.py:59
  (659 shorter events, 499.6 us)
Async XLA Ops:
  35.5 32.8 %collective-permute-start.3 = (bf16[256,1024]{1,0:T(8,128)(2,1)}, bf16[256,1024]{1,0:T(8,128)(2,1)}, u32[]{:S(2)}, u32[]{:S(2)}) collective-permute-start(bf16[256,1024]{1,0:T(8,128)(2,1)} %broadcast_select_fusion.1), channel_id=1, source_target_pairs={{0,4},{1,5},{2,6},{3,7},{4,0},{5,1},{6,2},{7,3},{8,12},{9,13},{10,... | collective-permute-start | bytes 1572872 | tf_op jit(solution)/shard_map/ppermute | solution.py:59
  82.0 45.2 %collective-permute-start.12 = (bf16[512,1024]{1,0:T(8,128)(2,1)}, bf16[512,1024]{1,0:T(8,128)(2,1)}, u32[]{:S(2)}, u32[]{:S(2)}) collective-permute-start(bf16[512,1024]{1,0:T(8,128)(2,1)} %collective-permute-done.8.refs_0_), channel_id=1, source_target_pairs={{1,3},{3,1},{5,7},{7,5},{8,10},{10,8},{12,14},{14,12},{17,19},{19,... | collective-permute-start | bytes 3145736 | tf_op jit(solution)/shard_map/ppermute | solution.py:59
  83.6 43.6 %collective-permute-start.13 = (bf16[512,1024]{1,0:T(8,128)(2,1)}, bf16[512,1024]{1,0:T(8,128)(2,1)}, u32[]{:S(2)}, u32[]{:S(2)}) collective-permute-start(bf16[512,1024]{1,0:T(8,128)(2,1)} %get-tuple-element.347), channel_id=1, source_target_pairs={{0,8},{2,10},{4,12},{6,14},{9,1},{11,3},{13,5},{15,7},{16,24},{18,... | collective-permute-start | bytes 3145736 | tf_op jit(solution)/shard_map/ppermute | solution.py:59
  128.6 27.8 %collective-permute-start.16 = (bf16[512,1024]{1,0:T(8,128)(2,1)S(1)}, bf16[512,1024]{1,0:T(8,128)(2,1)S(1)}, u32[]{:S(2)}, u32[]{:S(2)}) collective-permute-start(bf16[512,1024]{1,0:T(8,128)(2,1)S(1)} %copy-done.147), channel_id=1, source_target_pairs={{0,8},{2,10},{4,12},{6,14},{9,1},{11,3},{13,5},{15,7},{16,24},{18,... | collective-permute-start | bytes 3145736 | tf_op jit(solution)/shard_map/ppermute | solution.py:59
  133.9 35.9 %collective-permute-start.17 = (bf16[512,1024]{1,0:T(8,128)(2,1)S(1)}, bf16[512,1024]{1,0:T(8,128)(2,1)S(1)}, u32[]{:S(2)}, u32[]{:S(2)}) collective-permute-start(bf16[512,1024]{1,0:T(8,128)(2,1)S(1)} %add_convert_fusion.25.refs_2_), channel_id=1, source_target_pairs={{0,4},{1,5},{2,6},{3,7},{4,0},{5,1},{6,2},{7,3},{8,12},{9,13},{10,... | collective-permute-start | bytes 3145736 | tf_op jit(solution)/shard_map/ppermute | solution.py:59
  233.3 28.8 %collective-permute-start.28 = (bf16[512,1024]{1,0:T(8,128)(2,1)S(1)}, bf16[512,1024]{1,0:T(8,128)(2,1)S(1)}, u32[]{:S(2)}, u32[]{:S(2)}) collective-permute-start(bf16[512,1024]{1,0:T(8,128)(2,1)S(1)} %blend_forward.10), channel_id=1, source_target_pairs={{0,16},{1,17},{2,18},{3,19},{4,20},{5,21},{6,22},{7,23},{8,24},{9,... | collective-permute-start | bytes 3145736 | tf_op jit(solution)/shard_map/ppermute | solution.py:59
  400.9 30.0 %collective-permute-start.52 = (bf16[512,1024]{1,0:T(8,128)(2,1)S(1)}, bf16[512,1024]{1,0:T(8,128)(2,1)S(1)}, u32[]{:S(2)}, u32[]{:S(2)}) collective-permute-start(bf16[512,1024]{1,0:T(8,128)(2,1)S(1)} %add_convert_fusion.17.refs_5_), channel_id=1, source_target_pairs={{0,4},{1,5},{2,6},{3,7},{4,0},{5,1},{6,2},{7,3},{8,12},{9,13},{10,... | collective-permute-start | bytes 3145736 | tf_op jit(solution)/shard_map/ppermute | solution.py:59
  490.6 38.0 %collective-permute-start.62 = (bf16[512,1024]{1,0:T(8,128)(2,1)S(1)}, bf16[512,1024]{1,0:T(8,128)(2,1)S(1)}, u32[]{:S(2)}, u32[]{:S(2)}) collective-permute-start(bf16[512,1024]{1,0:T(8,128)(2,1)S(1)} %add_convert_fusion.13), channel_id=1, source_target_pairs={{16,0},{17,1},{18,2},{19,3},{20,4},{21,5},{22,6},{23,7},{24,8},{25... | collective-permute-start | bytes 3145736 | tf_op jit(solution)/shard_map/ppermute | solution.py:59
  495.0 26.9 %collective-permute-start.63 = (bf16[512,1024]{1,0:T(8,128)(2,1)S(1)}, bf16[512,1024]{1,0:T(8,128)(2,1)}, u32[]{:S(2)}, u32[]{:S(2)}) collective-permute-start(bf16[512,1024]{1,0:T(8,128)(2,1)S(1)} %add_convert_fusion.14), channel_id=1, source_target_pairs={{0,4},{1,5},{2,6},{3,7},{4,0},{5,1},{6,2},{7,3},{8,12},{9,13},{10,... | collective-permute-start | bytes 3145736 | tf_op jit(solution)/shard_map/ppermute | solution.py:59
  524.4 27.5 %collective-permute-start.64 = (bf16[512,1024]{1,0:T(8,128)(2,1)S(1)}, bf16[512,1024]{1,0:T(8,128)(2,1)S(1)}, u32[]{:S(2)}, u32[]{:S(2)}) collective-permute-start(bf16[512,1024]{1,0:T(8,128)(2,1)S(1)} %add_convert_fusion.12), channel_id=1, source_target_pairs={{16,0},{17,1},{18,2},{19,3},{20,4},{21,5},{22,6},{23,7},{24,8},{25... | collective-permute-start | bytes 3145736 | tf_op jit(solution)/shard_map/ppermute | solution.py:59
  590.6 35.7 %collective-permute-start.74 = (bf16[512,1024]{1,0:T(8,128)(2,1)S(1)}, bf16[512,1024]{1,0:T(8,128)(2,1)S(1)}, u32[]{:S(2)}, u32[]{:S(2)}) collective-permute-start(bf16[512,1024]{1,0:T(8,128)(2,1)S(1)} %add_convert_fusion.10.refs_5_), channel_id=1, source_target_pairs={{0,4},{1,5},{2,6},{3,7},{4,0},{5,1},{6,2},{7,3},{8,12},{9,13},{10,... | collective-permute-start | bytes 3145736 | tf_op jit(solution)/shard_map/ppermute | solution.py:59
  600.9 46.7 %collective-permute-start.78 = (bf16[512,1024]{1,0:T(8,128)(2,1)}, bf16[512,1024]{1,0:T(8,128)(2,1)}, u32[]{:S(2)}, u32[]{:S(2)}) collective-permute-start(bf16[512,1024]{1,0:T(8,128)(2,1)} %constant_dynamic-slice_fusion.3), channel_id=1, source_target_pairs={{0,2},{1,3},{2,0},{3,1},{4,6},{5,7},{6,4},{7,5},{8,10},{9,11},{10,... | collective-permute-start | bytes 3145736 | tf_op jit(solution)/shard_map/ppermute | solution.py:59
  601.4 46.2 %collective-permute-start.79 = (bf16[2,256,1024]{2,1,0:T(8,128)(2,1)S(1)}, bf16[2,256,1024]{2,1,0:T(8,128)(2,1)}, u32[]{:S(2)}, u32[]{:S(2)}) collective-permute-start(bf16[2,256,1024]{2,1,0:T(8,128)(2,1)S(1)} %copy-done.126), channel_id=1, source_target_pairs={{1,8},{3,10},{5,12},{7,14},{8,1},{10,3},{12,5},{14,7},{17,24},{19,... | collective-permute-start | bytes 3145736 | tf_op jit(solution)/shard_map/ppermute | solution.py:59
  647.5 36.8 %collective-permute-start.82 = (bf16[512,1024]{1,0:T(8,128)(2,1)S(1)}, bf16[512,1024]{1,0:T(8,128)(2,1)S(1)}, u32[]{:S(2)}, u32[]{:S(2)}) collective-permute-start(bf16[512,1024]{1,0:T(8,128)(2,1)S(1)} %add_convert_fusion.9), channel_id=1, source_target_pairs={{0,4},{1,5},{2,6},{3,7},{4,0},{5,1},{6,2},{7,3},{8,12},{9,13},{10,... | collective-permute-start | bytes 3145736 | tf_op jit(solution)/shard_map/ppermute | solution.py:59
  686.3 26.4 %collective-permute-start.99 = (bf16[512,1024]{1,0:T(8,128)(2,1)}, bf16[512,1024]{1,0:T(8,128)(2,1)}, u32[]{:S(2)}, u32[]{:S(2)}) collective-permute-start(bf16[512,1024]{1,0:T(8,128)(2,1)} %constant_dynamic-slice_fusion.1), channel_id=1, source_target_pairs={{0,2},{1,3},{2,0},{3,1},{4,6},{5,7},{6,4},{7,5},{8,10},{9,11},{10,... | collective-permute-start | bytes 3145736 | tf_op jit(solution)/shard_map/ppermute | solution.py:59
  695.1 39.4 %collective-permute-start.87 = (bf16[512,1024]{1,0:T(8,128)(2,1)}, bf16[512,1024]{1,0:T(8,128)(2,1)}, u32[]{:S(2)}, u32[]{:S(2)}) collective-permute-start(bf16[512,1024]{1,0:T(8,128)(2,1)} %constant_dynamic-slice_fusion), channel_id=1, source_target_pairs={{0,2},{1,3},{2,0},{3,1},{4,6},{5,7},{6,4},{7,5},{8,10},{9,11},{10,... | collective-permute-start | bytes 3145736 | tf_op jit(solution)/shard_map/ppermute | solution.py:59
  701.3 37.6 %collective-permute-start.94 = (f32[1,6656]{1,0:T(1,128)S(1)}, f32[1,6656]{1,0:T(1,128)S(1)}, u32[]{:S(2)}, u32[]{:S(2)}) collective-permute-start(f32[1,6656]{1,0:T(1,128)S(1)} %add.231), channel_id=1, source_target_pairs={{0,2},{1,3},{2,0},{3,1},{4,6},{5,7},{6,4},{7,5},{8,10},{9,11},{10,... | collective-permute-start | bytes 79880 | tf_op jit(solution)/shard_map/ppermute | solution.py:59
  702.3 45.3 %collective-permute-start.95 = (bf16[512,1024]{1,0:T(8,128)(2,1)}, bf16[512,1024]{1,0:T(8,128)(2,1)S(1)}, u32[]{:S(2)}, u32[]{:S(2)}) collective-permute-start(bf16[512,1024]{1,0:T(8,128)(2,1)} %add_convert_fusion.6), channel_id=1, source_target_pairs={{1,9},{3,11},{5,13},{7,15},{8,0},{10,2},{12,4},{14,6},{17,25},{19,... | collective-permute-start | bytes 3145736 | tf_op jit(solution)/shard_map/ppermute | solution.py:59
  714.6 50.5 %collective-permute-start.100 = (bf16[512,1024]{1,0:T(8,128)(2,1)S(1)}, bf16[512,1024]{1,0:T(8,128)(2,1)S(1)}, u32[]{:S(2)}, u32[]{:S(2)}) collective-permute-start(bf16[512,1024]{1,0:T(8,128)(2,1)S(1)} %add_convert_fusion.1), channel_id=1, source_target_pairs={{1,9},{3,11},{5,13},{7,15},{8,0},{10,2},{12,4},{14,6},{17,25},{19,... | collective-permute-start | bytes 3145736 | tf_op jit(solution)/shard_map/ppermute | solution.py:59
  736.3 40.1 %collective-permute-start.88 = (bf16[512,1024]{1,0:T(8,128)(2,1)S(1)}, bf16[512,1024]{1,0:T(8,128)(2,1)S(1)}, u32[]{:S(2)}, u32[]{:S(2)}) collective-permute-start(bf16[512,1024]{1,0:T(8,128)(2,1)S(1)} %add_convert_fusion.4), channel_id=1, source_target_pairs={{1,9},{3,11},{5,13},{7,15},{8,0},{10,2},{12,4},{14,6},{17,25},{19,... | collective-permute-start | bytes 3145736 | tf_op jit(solution)/shard_map/ppermute | solution.py:59
  739.0 51.2 %collective-permute-start.105 = (bf16[512,1024]{1,0:T(8,128)(2,1)S(1)}, bf16[512,1024]{1,0:T(8,128)(2,1)S(1)}, u32[]{:S(2)}, u32[]{:S(2)}) collective-permute-start(bf16[512,1024]{1,0:T(8,128)(2,1)S(1)} %add_convert_fusion.7.refs_0_), channel_id=1, source_target_pairs={{0,1},{2,3},{4,5},{6,7},{9,8},{11,10},{13,12},{15,14},{16,17},{18,... | collective-permute-start | bytes 3145736 | tf_op jit(solution)/shard_map/ppermute | solution.py:59
  745.1 36.6 %collective-permute-start.104 = (bf16[512,1024]{1,0:T(8,128)(2,1)S(1)}, bf16[512,1024]{1,0:T(8,128)(2,1)S(1)}, u32[]{:S(2)}, u32[]{:S(2)}) collective-permute-start(bf16[512,1024]{1,0:T(8,128)(2,1)S(1)} %add_convert_fusion.7.refs_0_), channel_id=1, source_target_pairs={{0,2},{2,0},{4,6},{6,4},{9,11},{11,9},{13,15},{15,13},{16,18},{18,... | collective-permute-start | bytes 3145736 | tf_op jit(solution)/shard_map/ppermute | solution.py:59
  747.7 49.5 %collective-permute-start.85 = (bf16[512,1024]{1,0:T(8,128)(2,1)S(1)}, bf16[512,1024]{1,0:T(8,128)(2,1)S(1)}, u32[]{:S(2)}, u32[]{:S(2)}) collective-permute-start(bf16[512,1024]{1,0:T(8,128)(2,1)S(1)} %copy-done.138), channel_id=1, source_target_pairs={{0,4},{1,5},{2,6},{3,7},{4,0},{5,1},{6,2},{7,3},{8,12},{9,13},{10,... | collective-permute-start | bytes 3145736 | tf_op jit(solution)/shard_map/ppermute | solution.py:59
  804.6 26.4 %collective-permute-start.90 = (bf16[512,1024]{1,0:T(8,128)(2,1)S(1)}, bf16[512,1024]{1,0:T(8,128)(2,1)S(1)}, u32[]{:S(2)}, u32[]{:S(2)}) collective-permute-start(bf16[512,1024]{1,0:T(8,128)(2,1)S(1)} %add_convert_fusion.3.refs_0_), channel_id=1, source_target_pairs={{0,1},{2,3},{4,5},{6,7},{9,8},{11,10},{13,12},{15,14},{16,17},{18,... | collective-permute-start | bytes 3145736 | tf_op jit(solution)/shard_map/ppermute | solution.py:59
  (237 other events, 2489.6 us)
